TPU v7x, 32 devices: a whole 2x2x4 slice. The times are simulated.
32 devices in a mesh: gx: 8 (over z, y), sa: 4 (over x, core).
Axes of the slice: x: 2, y: 2, z: 4, core: 2. Of those that a mesh axis runs over, the one named last changes fastest.
Arguments:
- gas: float32 [4, 16, 32, 1024], P(None, 'gx', None, 'sa'), may hold values from -6 to 6
- melt: float32 [2, 16, 128, 1024], P(None, 'gx', 'sa'), may hold values from -6 to 6
- surface_mask: int32 [16, 1024], P('gx'), may hold values 0 or 1
- melt_level: int32 [16, 1024], P('gx'), may hold values from 32 to 128
Outputs:
- gas_rate: float32 [4, 16, 32, 1024], P(None, 'gx', None, 'sa')
- melt_rate: float32 [2, 16, 128, 1024], P(None, 'gx', 'sa')
Inputs may be any that keep to these rules, and one draw needn't show every extreme that they name: `melt_level`: a level equal to 128 means the column is liquid to the bottom.
All inputs are finite; a program needn't handle non-finite values. No bound on the sum of `surface_mask` on one device may be relied on, other than what follows from the above.
Results may differ from a plain program's by a relative error of at most 0.0003.
Values sent between devices are 32-bit elements; how exact they have to be, the bound alone decides.
No kernel may reach another device: no remote copies, remote signals or barrier semaphores. Data moves between devices by JAX's collectives and lax.ppermute only.
A program may use at most 64 MiB of HBM per device.

v0:
```python
import jax
import jax.numpy as jnp
from jax import lax
from jax.sharding import PartitionSpec as P

gas_viscosity = 0.05
gas_diffusivity = 0.07
turbulent_prandtl = 0.85
melt_viscosity = 0.2
melt_diffusivity = 0.5
epsilon = 1e-06


def with_halo(cells, sides, width):
    for axis, dim in sides:
        count = lax.axis_size(axis)
        head = lax.slice_in_dim(cells, 0, width, axis=dim)
        tail = lax.slice_in_dim(cells, cells.shape[dim] - width, cells.shape[dim], axis=dim)
        cells = jnp.concatenate(
            [
                lax.ppermute(tail, axis, [(i, (i + 1) % count) for i in range(count)]),
                cells,
                lax.ppermute(head, axis, [((i + 1) % count, i) for i in range(count)]),
            ],
            axis=dim,
        )
    return cells


def wall_pad(source):
    return jnp.concatenate([-source[..., 0:1, :], source, source[..., -1:, :]], axis=-2)


def strip_margin(source, width):
    return source[..., width : source.shape[-3] - width, :, width : source.shape[-1] - width]


def gradients(source):
    padded = wall_pad(source)
    along_x = 0.5 * (source[..., 2:, :, 1:-1] - source[..., :-2, :, 1:-1])
    along_y = 0.5 * (source[..., 1:-1, :, 2:] - source[..., 1:-1, :, :-2])
    along_z = 0.5 * (padded[..., 1:-1, 2:, 1:-1] - padded[..., 1:-1, :-2, 1:-1])
    return jnp.stack([along_x, along_y, along_z], axis=-4)


def test_filter(source):
    along = (
        0.25 * source[..., :-2, :, :] + 0.5 * source[..., 1:-1, :, :] + 0.25 * source[..., 2:, :, :]
    )
    return 0.25 * along[..., :-2] + 0.5 * along[..., 1:-1] + 0.25 * along[..., 2:]


def laplacian(source):
    padded = wall_pad(source)
    middle = source[..., 1:-1, :, 1:-1]
    beside_all = (
        source[..., 2:, :, 1:-1]
        + source[..., :-2, :, 1:-1]
        + source[..., 1:-1, :, 2:]
        + source[..., 1:-1, :, :-2]
    )
    return beside_all + padded[..., 1:-1, 2:, 1:-1] + padded[..., 1:-1, :-2, 1:-1] - 6.0 * middle


def strain_of(gradient):
    strain = 0.5 * (gradient + jnp.swapaxes(gradient, 0, 1))
    magnitude = jnp.sqrt(2.0 * jnp.sum(strain * strain, axis=(0, 1)))
    return (strain, magnitude)


def germano_parts(velocity):
    gradient = gradients(velocity)
    strain, magnitude = strain_of(gradient)
    inner = strip_margin(velocity, 1)
    resolved_filtered = test_filter(magnitude * strain)
    pair_filtered = test_filter(inner[:, None] * inner[None, :])
    coarse_velocity = test_filter(velocity)
    coarse_strain, coarse_magnitude = strain_of(gradients(coarse_velocity))
    coarse_inner = strip_margin(coarse_velocity, 1)
    leonard = pair_filtered - coarse_inner[:, None] * coarse_inner[None, :]
    model_term = resolved_filtered - 4.0 * coarse_magnitude * coarse_strain
    numerator = jnp.sum(leonard * model_term, axis=(0, 1, 4))
    denominator = jnp.sum(model_term * model_term, axis=(0, 1, 4))
    return (numerator, denominator, gradient, magnitude)


def lilly_coefficient(numerator, denominator, span_cells):
    mean_numerator = numerator / span_cells
    mean_denominator = denominator / span_cells
    return -mean_numerator / (2.0 * (mean_denominator + epsilon))


def gas_rates(velocity, heat_field, gradient, magnitude, coefficient):
    inner_magnitude = strip_margin(magnitude, 1)
    eddy = coefficient[:, :, None] * inner_magnitude
    inner_velocity = strip_margin(velocity, 2)
    inner_gradient = strip_margin(gradient, 1)
    advection = jnp.sum(inner_velocity[None, :] * inner_gradient, axis=1)
    momentum = -advection + (gas_viscosity + eddy) * laplacian(strip_margin(velocity, 1))
    heat_gradient = gradients(heat_field)
    transport = jnp.sum(inner_velocity * heat_gradient, axis=0)
    energy = -transport + (gas_diffusivity + eddy / turbulent_prandtl) * laplacian(heat_field)
    section_rate = jnp.concatenate([momentum, energy[None]], axis=0)
    planes = (
        inner_velocity[0, :, 0, :],
        strip_margin(heat_field, 1)[:, 0, :],
        inner_magnitude[:, 0, :],
    )
    return (section_rate, planes)


def wall_fluxes(streamwise_plane, heat_plane, magnitude_plane, wall_coefficient):
    eddy = wall_coefficient[:, None] * magnitude_plane
    wall_shear = (gas_viscosity + eddy) * 2.0 * streamwise_plane
    wall_heat = (gas_diffusivity + eddy / turbulent_prandtl) * 2.0 * heat_plane
    return (wall_shear, wall_heat)


def upper_ghost(top_rows, surface_mask):
    streamwise = jnp.where(surface_mask == 1, top_rows[0], -top_rows[0])
    return jnp.stack([streamwise, top_rows[1]])


def melt_rates(
    x_upper, x_lower, depth_padded, surface_mask, melt_level, depth_index, wall_shear, wall_heat
):
    centre = depth_padded[:, :, 1:-1, :]
    beside_all = x_upper + x_lower + depth_padded[:, :, 2:, :] + depth_padded[:, :, :-2, :]
    beside_all = beside_all + jnp.roll(centre, 1, axis=-1) + jnp.roll(centre, -1, axis=-1)
    laplace = beside_all - 6.0 * centre
    surface = (depth_index == 0).astype(jnp.float32)[None, :, None]
    liquid_share = surface_mask.astype(jnp.float32)
    momentum = melt_viscosity * laplace[0] + surface * (liquid_share * wall_shear)[:, None, :]
    solid = depth_index[None, :, None] >= melt_level[:, None, :]
    momentum = jnp.where(solid, jnp.zeros_like(momentum), momentum)
    energy = melt_diffusivity * laplace[1] + surface * wall_heat[:, None, :]
    return jnp.stack([momentum, energy])


def on_device(gas, melt, surface_mask, melt_level):
    padded_gas = with_halo(gas, (("gx", 1), ("sa", 3)), 2)
    velocity = padded_gas[:3]
    heat_field = strip_margin(padded_gas[3], 1)
    padded_melt = with_halo(melt, (("gx", 1), ("sa", 2)), 1)
    numerator, denominator, gradient, magnitude = germano_parts(velocity)
    span_cells = float(gas.shape[-1] * lax.axis_size("sa"))
    total_numerator, total_denominator = lax.psum((numerator, denominator), "sa")
    coefficient = lilly_coefficient(total_numerator, total_denominator, span_cells)
    section_rate, planes = gas_rates(velocity, heat_field, gradient, magnitude, coefficient)
    local_shear, local_heat = wall_fluxes(planes[0], planes[1], planes[2], coefficient[:, 0])
    interface = lax.all_gather(jnp.stack([local_shear, local_heat]), "sa", axis=2, tiled=True)
    wall_shear = interface[0]
    wall_heat = interface[1]
    centre_rows = padded_melt[:, 1:-1]
    position = lax.axis_index("sa")
    devices = lax.axis_size("sa")
    surface_row = upper_ghost(centre_rows[:, :, 1, :], surface_mask)
    upper_row = jnp.where(position == 0, surface_row, centre_rows[:, :, 0, :])
    lower_row = jnp.where(
        position == devices - 1, centre_rows[:, :, -2, :], centre_rows[:, :, -1, :]
    )
    depth_padded = jnp.concatenate(
        [upper_row[:, :, None], centre_rows[:, :, 1:-1], lower_row[:, :, None]], axis=2
    )
    levels_here = melt.shape[2]
    depth_index = position * levels_here + jnp.arange(levels_here, dtype=jnp.int32)
    melt_section = melt_rates(
        padded_melt[:, 2:, 1:-1],
        padded_melt[:, :-2, 1:-1],
        depth_padded,
        surface_mask,
        melt_level,
        depth_index,
        wall_shear,
        wall_heat,
    )
    return (section_rate, melt_section)


def solution(mesh):
    in_specs = (P(None, "gx", None, "sa"), P(None, "gx", "sa", None), P("gx", None), P("gx", None))
    out_specs = (P(None, "gx", None, "sa"), P(None, "gx", "sa", None))
    return jax.shard_map(
        on_device, mesh=mesh, in_specs=in_specs, out_specs=out_specs, check_vma=False
    )
```

profile of v0, /device:TPU:0, one launch (start us, length us, event | category | flops | bytes accessed | tf_op | source)
XLA Modules:
  0.0 66.7 jit_solution(7205657698506381801)
XLA Ops:
  0.6 3.0 %collective-permute-start = (f32[4,2,32,256]{3,2,1,0:T(8,128)}, f32[4,2,32,256]{3,2,1,0:T(8,128)S(1)}, u32[]{:S(2)}, u32[]{:S(2)}) collective-permute-start(f32[4,2,32,256]{3,2,1,0:T(8,128)} %param.4), channel_id=1, source_target_pairs={{0,4},{4,8},{8,12},{12,16},{16,20},{20,24},{24,28},{28,0},{1,5},{5... | collective-permute-start | bytes 786440 | tf_op jit(solution)/shard_map/ppermute | solution.py:21
  3.7 3.1 %collective-permute-start.1 = (f32[4,2,32,256]{3,2,1,0:T(8,128)}, f32[4,2,32,256]{3,2,1,0:T(8,128)S(1)}, u32[]{:S(2)}, u32[]{:S(2)}) collective-permute-start(f32[4,2,32,256]{3,2,1,0:T(8,128)} %param.4), channel_id=1, source_target_pairs={{4,0},{8,4},{12,8},{16,12},{20,16},{24,20},{28,24},{0,28},{5,1},{9... | collective-permute-start | bytes 786440 | tf_op jit(solution)/shard_map/ppermute | solution.py:23
  6.8 1.1 %fusion.71 = (f32[2,1,32,1024]{3,2,1,0:T(8,128)S(1)}, f32[2,1,32,1024]{3,2,1,0:T(8,128)S(1)}) fusion(f32[2,2,32,1024]{3,2,1,0:T(8,128)} %param.5), kind=kLoop, calls=%fused_computation.168 | loop fusion | bytes 1048576 | tf_op jit(solution)/shard_map/slice | solution.py:18
  7.8 1.0 %copy.48 = f32[2,1,32,1024]{3,1,2,0:T(1,128)} copy(f32[2,1,32,1024]{3,2,1,0:T(8,128)S(1)} %get-tuple-element.30) | data formatting | bytes 524288 | tf_op jit(solution)/shard_map/slice | solution.py:17
  8.8 2.0 %collective-permute-start.4 = (f32[2,1,32,1024]{3,1,2,0:T(1,128)}, f32[2,1,32,1024]{3,1,2,0:T(1,128)}, u32[]{:S(2)}, u32[]{:S(2)}) collective-permute-start(f32[2,1,32,1024]{3,1,2,0:T(1,128)} %copy.48), channel_id=1, source_target_pairs={{4,0},{8,4},{12,8},{16,12},{20,16},{24,20},{28,24},{0,28},{5,1},{9... | collective-permute-start | bytes 786440 | tf_op jit(solution)/shard_map/ppermute | solution.py:23
  10.8 1.0 %copy.50 = f32[2,1,32,1024]{3,1,2,0:T(1,128)} copy(f32[2,1,32,1024]{3,2,1,0:T(8,128)S(1)} %get-tuple-element.29) | data formatting | bytes 524288 | tf_op jit(solution)/shard_map/slice | solution.py:18
  11.8 1.1 %fusion.69 = (f32[2,2,32,1023]{3,2,1,0:T(8,128)}, f32[2,2,32,1023]{3,2,1,0:T(8,128)}) fusion(f32[2,2,32,1024]{3,2,1,0:T(8,128)S(1)} %copy-done.1), kind=kLoop, calls=%fused_computation.166 | loop fusion | bytes 2095104 | tf_op jit(solution)/shard_map/jit(_roll_static)/slice | solution.py:129
  13.0 0.7 %fusion.70 = (f32[2,2,32,1]{3,2,1,0:T(8,128)}, f32[2,2,32,1]{3,2,1,0:T(8,128)}) fusion(f32[2,2,32,1024]{3,2,1,0:T(8,128)S(1)} %copy-done.1), kind=kLoop, calls=%fused_computation.167 | loop fusion | bytes 2048 | tf_op jit(solution)/shard_map/jit(_roll_static)/slice | solution.py:129
  15.2 6.7 %collective-permute-done = f32[4,2,32,256]{3,2,1,0:T(8,128)S(1)} collective-permute-done((f32[4,2,32,256]{3,2,1,0:T(8,128)}, f32[4,2,32,256]{3,2,1,0:T(8,128)S(1)}, u32[]{:S(2)}, u32[]{:S(2)}) %collective-permute-start) | collective-permute-done | bytes 262176 | tf_op jit(solution)/shard_map/ppermute | solution.py:21
  22.0 2.4 %collective-permute-done.1 = f32[4,2,32,256]{3,2,1,0:T(8,128)S(1)} collective-permute-done((f32[4,2,32,256]{3,2,1,0:T(8,128)}, f32[4,2,32,256]{3,2,1,0:T(8,128)S(1)}, u32[]{:S(2)}, u32[]{:S(2)}) %collective-permute-start.1) | collective-permute-done | bytes 262176 | tf_op jit(solution)/shard_map/ppermute | solution.py:23
  24.6 1.7 %collective-permute-start.3 = (f32[4,6,32,2]{3,2,1,0:T(8,128)S(1)}, f32[4,6,32,2]{3,2,1,0:T(8,128)S(1)}, u32[]{:S(2)}, u32[]{:S(2)}) collective-permute-start(f32[4,6,32,2]{3,2,1,0:T(8,128)S(1)} %get-tuple-element.16), channel_id=1, source_target_pairs={{1,0},{2,1},{3,2},{0,3},{5,4},{6,5},{7,6},{4,7},{9,8},{10,9},{11,1... | collective-permute-start | bytes 18440 | tf_op jit(solution)/shard_map/ppermute | solution.py:23
  26.3 2.3 %collective-permute-done.4 = f32[2,1,32,1024]{3,1,2,0:T(1,128)} collective-permute-done((f32[2,1,32,1024]{3,1,2,0:T(1,128)}, f32[2,1,32,1024]{3,1,2,0:T(1,128)}, u32[]{:S(2)}, u32[]{:S(2)}) %collective-permute-start.4) | collective-permute-done | bytes 262176 | tf_op jit(solution)/shard_map/ppermute | solution.py:23
  28.6 1.4 %pad_maximum_fusion.23 = (f32[2,4,1,1024]{3,1,2,0:T(4,128)S(1)}, f32[2,4,1,1024]{3,1,2,0:T(4,128)}) fusion(f32[2,1,32,1024]{3,1,2,0:T(1,128)} %collective-permute-done.4, f32[2,2,32,1024]{3,1,2,0:T(2,128)S(1)} %copy.52, f32[2,1,32,1024]{3,1,2,0:T(1,128)} %collective-permute-done.5), kind=kLoop, calls=%fused_computation.137 | loop fusion | flops 32768 | bytes 1114112 | tf_op jit(solution)/shard_map/slice | solution.py:17
  30.0 1.7 %collective-permute-start.6 = (f32[2,4,1,1024]{3,1,2,0:T(4,128)S(1)}, f32[2,4,1,1024]{3,1,2,0:T(4,128)}, u32[]{:S(2)}, u32[]{:S(2)}) collective-permute-start(f32[2,4,1,1024]{3,1,2,0:T(4,128)S(1)} %get-tuple-element.13), channel_id=1, source_target_pairs={{1,0},{2,1},{3,2},{0,3},{5,4},{6,5},{7,6},{4,7},{9,8},{10,9},{11,1... | collective-permute-start | bytes 98312 | tf_op jit(solution)/shard_map/ppermute | solution.py:23
  31.7 1.7 %copy.51 = f32[2,1,32,1024]{3,2,1,0:T(8,128)} copy(f32[2,1,32,1024]{3,1,2,0:T(1,128)} %collective-permute-done.5) | data formatting | bytes 524288 | tf_op jit(solution)/shard_map/ppermute | solution.py:21
  33.5 1.7 %copy.49 = f32[2,1,32,1024]{3,2,1,0:T(8,128)} copy(f32[2,1,32,1024]{3,1,2,0:T(1,128)} %collective-permute-done.4) | data formatting | bytes 524288 | tf_op jit(solution)/shard_map/ppermute | solution.py:23
  38.1 0.7 fusion.8
  39.4 0.7 %broadcast_multiply_fusion.1 = (f32[4,32,258]{2,1,0:T(8,128)S(1)}, f32[4,32,258]{2,1,0:T(8,128)}) fusion(f32[4,32,258]{2,1,0:T(8,128)S(1)} %multiply_reduce_fusion), kind=kLoop, calls=%fused_computation.121 | loop fusion | flops 66048 | bytes 396288 | tf_op jit(solution)/shard_map/mul | solution.py:75
  41.7 0.8 %multiply_bitcast_fusion = (f32[1,2,32,256]{3,2,1,0:T(8,128)S(1)}, f32[2,32,256]{2,1,0:T(8,128)}, f32[2,32,256]{2,1,0:T(8,128)}) fusion(f32[4,1,258]{2,1,0:T(1,128)S(1)} %get-tuple-element.34, f32[4,32,258]{2,1,0:T(8,128)S(1)} %slice.476, f32[4,1,258]{2,1,0:T(1,128)S(1)} %get-tuple-element.33), kind=kLoop, calls=%fused_computation.130 | loop fusion | flops 65536 | bytes 336960 | tf_op jit(solution)/shard_map/stack | solution.py:43
  42.5 0.7 fusion.72
  43.1 0.9 %fusion.22 = f32[3,2,32,256]{3,2,1,0:T(8,128)} fusion(f32[3,3,4,32,258]{4,3,2,0,1:T(8,128)S(1)} %get-tuple-element.47, f32[3,2,32,256]{3,2,1,0:T(8,128)S(1)} %get-tuple-element.35), kind=kLoop, calls=%fused_computation.50 | loop fusion | flops 245760 | bytes 983040 | tf_op jit(solution)/shard_map/reduce_sum | solution.py:98
  44.0 1.4 %fusion.20 = (f32[2,32]{1,0:T(2,128)}, f32[2,32]{1,0:T(2,128)}) fusion(f32[3,3,2,32,258]{4,3,2,0,1:T(8,128)S(1)} %fusion.3, f32[3,2,32,256]{3,2,1,0:T(8,128)S(1)} %get-tuple-element.17, f32[2,32,256]{2,1,0:T(8,128)S(1)} %sqrt_multiply_fusion, f32[3,3,2,32,256]{4,3,2,1,0:T(8,128)S(1)} %pad_maximum_fusion.4, f32[3,3,2,32,258]{4,3,2,0,1:T(8,128)S(1)} %fusion.1), kind=kLoop, calls=%fused_computation.45 | loop fusion | flops 2801536 | bytes 4588032 | tf_op jit(solution)/shard_map/reduce_sum | solution.py:82
  45.4 8.2 %all-reduce = (f32[2,32]{1,0:T(2,128)}, f32[2,32]{1,0:T(2,128)}) all-reduce(f32[2,32]{1,0:T(2,128)} %get-tuple-element.3, f32[2,32]{1,0:T(2,128)} %get-tuple-element.2), channel_id=1, replica_groups=mesh['gx'=8,'sa'=4] {'sa'}, use_global_device_ids=true, to_apply=%region_6.0 | all-reduce | flops 128 | bytes 1024 | tf_op jit(solution)/shard_map/psum | solution.py:147
  53.6 0.7 %multiply_divide_fusion = f32[2,32]{1,0:T(2,128)S(1)} fusion(f32[2,32]{1,0:T(2,128)} %get-tuple-element.4, f32[2,32]{1,0:T(2,128)} %get-tuple-element.5), kind=kLoop, calls=%fused_computation.160 | loop fusion | flops 384 | bytes 768 | tf_op jit(solution)/shard_map/div | solution.py:90
  54.5 0.8 %bitcast_multiply_fusion.1 = (f32[1,2,256]{2,0,1:T(1,128)S(1)}, f32[1,2,256]{2,0,1:T(1,128)S(1)}) fusion(f32[4,2,32,256]{3,2,1,0:T(8,128)S(1)} %copy-done.2, f32[4,32,258]{2,1,0:T(8,128)} %get-tuple-element.42, f32[2]{0:T(128)S(1)} %slice_reduce_fusion, f32[6,32,260]{2,1,0:T(8,128)S(1)} %slice_bitcast_fusion), kind=kLoop, calls=%fused_computation.157 | loop fusion | flops 4096 | bytes 10248 | tf_op jit(solution)/shard_map/mul | solution.py:114
  55.3 5.2 %all_gather.3 = f32[2,2,1024]{2,0,1:T(2,128)S(1)} all-gather(f32[2,2,256]{2,0,1:T(2,128)S(1)} %pad_maximum_fusion.24), channel_id=1, replica_groups=mesh['gx'=8,'sa'=4] {'sa'}, dimensions={2}, use_global_device_ids=true | all-gather | bytes 20480 | tf_op jit(solution)/shard_map/all_gather | solution.py:151
  60.5 0.7 %bitcast_multiply_fusion = (f32[2,1024]{1,0:T(2,128)S(1)}, f32[1,2,1,1024]{3,1,2,0:T(2,128)S(1)}) fusion(f32[1,2,1024]{2,0,1:T(1,128)S(1)} %get-tuple-element.43, s32[2,1024]{1,0:T(2,128)S(1)} %copy-done.14, f32[2,2,32,1024]{3,1,2,0:T(2,128)} %copy-done.3), kind=kLoop, calls=%fused_computation.150 | loop fusion | flops 10240 | bytes 40960 | tf_op jit(solution)/shard_map/mul | solution.py:133
  61.2 1.1 %fusion.61 = (f32[2,32,256]{2,1,0:T(8,128)S(1)}, f32[1,2,32,256]{3,2,1,0:T(8,128)S(1)}) fusion(f32[4,32,258]{2,1,0:T(8,128)} %get-tuple-element.42, f32[2,32]{1,0:T(2,128)S(1)} %multiply_divide_fusion, f32[6,32,260]{2,1,0:T(8,128)S(1)} %slice_bitcast_fusion, f32[2,32,256]{2,1,0:T(8,128)} %get-tuple-element.8, f32[2,32,256]{2,1,0:T(8,128)} %get-tuple-element.7, ...), kind=kLoop, calls=%fused_computation.134 | loop fusion | flops 229376 | bytes 721152 | tf_op jit(solution)/shard_map/add | solution.py:99
  63.0 0.7 %pad_maximum_fusion.10 = f32[4,2,32,256]{3,2,1,0:T(8,128)} fusion(f32[1,2,32,256]{3,2,1,0:T(8,128)S(1)} %get-tuple-element.38, f32[3,2,32,256]{3,2,1,0:T(8,128)S(1)} %fusion.42), kind=kLoop, calls=%fused_computation.86 | loop fusion | flops 65536 | bytes 524288 | tf_op jit(solution)/shard_map/concatenate | solution.py:103
  63.7 0.8 %slice_select_fusion = f32[2,2,1,1024]{3,1,2,0:T(2,128)S(1)} fusion(f32[2,4,1,1024]{3,1,2,0:T(4,128)} %collective-permute-done.7, f32[1,2,1,1024]{3,1,2,0:T(2,128)S(1)} %slice.483, f32[1,2,1,1024]{3,1,2,0:T(2,128)S(1)} %get-tuple-element.46, pred[]{:T(512)S(6)} %eq.23), kind=kLoop, calls=%fused_computation.141 | loop fusion | flops 8192 | bytes 49153 | tf_op jit(solution)/shard_map/jit(_where)/select_n | solution.py:158
  64.5 0.8 %slice_select_fusion.1 = f32[2,2,1,1024]{3,1,2,0:T(2,128)S(1)} fusion(f32[2,4,1,1024]{3,1,2,0:T(4,128)} %collective-permute-done.6, f32[2,2,32,1024]{3,1,2,0:T(2,128)} %copy-done.3, pred[]{:T(512)S(6)} %eq.22), kind=kLoop, calls=%fused_computation.142 | loop fusion | flops 4096 | bytes 49153 | tf_op jit(solution)/shard_map/jit(_where)/select_n | solution.py:159
  65.9 0.8 %pad_maximum_fusion.9 = f32[2,2,32,1024]{3,2,1,0:T(8,128)} fusion(f32[1,2,32,1024]{3,2,1,0:T(8,128)S(1)} %get-tuple-element.24, f32[1,2,32,1024]{3,2,1,0:T(8,128)S(1)} %get-tuple-element.23), kind=kLoop, calls=%fused_computation.79 | loop fusion | flops 131072 | bytes 1048576 | tf_op jit(solution)/shard_map/stack | solution.py:137
  (81 shorter events, 8.1 us)
Async XLA Ops:
  0.6 11.2 %copy-start.1 = (f32[2,2,32,1024]{3,2,1,0:T(8,128)S(1)}, f32[2,2,32,1024]{3,2,1,0:T(8,128)}, u32[]{:S(2)}) copy-start(f32[2,2,32,1024]{3,2,1,0:T(8,128)} %param.5) | copy-start | bytes 1572868
  0.6 21.3 %collective-permute-start = (f32[4,2,32,256]{3,2,1,0:T(8,128)}, f32[4,2,32,256]{3,2,1,0:T(8,128)S(1)}, u32[]{:S(2)}, u32[]{:S(2)}) collective-permute-start(f32[4,2,32,256]{3,2,1,0:T(8,128)} %param.4), channel_id=1, source_target_pairs={{0,4},{4,8},{8,12},{12,16},{16,20},{20,24},{24,28},{28,0},{1,5},{5... | collective-permute-start | bytes 786440 | tf_op jit(solution)/shard_map/ppermute | solution.py:21
  3.7 20.7 %collective-permute-start.1 = (f32[4,2,32,256]{3,2,1,0:T(8,128)}, f32[4,2,32,256]{3,2,1,0:T(8,128)S(1)}, u32[]{:S(2)}, u32[]{:S(2)}) collective-permute-start(f32[4,2,32,256]{3,2,1,0:T(8,128)} %param.4), channel_id=1, source_target_pairs={{4,0},{8,4},{12,8},{16,12},{20,16},{24,20},{28,24},{0,28},{5,1},{9... | collective-permute-start | bytes 786440 | tf_op jit(solution)/shard_map/ppermute | solution.py:23
  8.8 19.8 %collective-permute-start.4 = (f32[2,1,32,1024]{3,1,2,0:T(1,128)}, f32[2,1,32,1024]{3,1,2,0:T(1,128)}, u32[]{:S(2)}, u32[]{:S(2)}) collective-permute-start(f32[2,1,32,1024]{3,1,2,0:T(1,128)} %copy.48), channel_id=1, source_target_pairs={{4,0},{8,4},{12,8},{16,12},{20,16},{24,20},{28,24},{0,28},{5,1},{9... | collective-permute-start | bytes 786440 | tf_op jit(solution)/shard_map/ppermute | solution.py:23
  11.7 10.2 %copy-start.2 = (f32[4,2,32,256]{3,2,1,0:T(8,128)S(1)}, f32[4,2,32,256]{3,2,1,0:T(8,128)}, u32[]{:S(2)}) copy-start(f32[4,2,32,256]{3,2,1,0:T(8,128)} %param.4) | copy-start | bytes 786436
  11.7 16.9 %collective-permute-start.5 = (f32[2,1,32,1024]{3,1,2,0:T(1,128)}, f32[2,1,32,1024]{3,1,2,0:T(1,128)}, u32[]{:S(2)}, u32[]{:S(2)}) collective-permute-start(f32[2,1,32,1024]{3,1,2,0:T(1,128)} %copy.50), channel_id=1, source_target_pairs={{0,4},{4,8},{8,12},{12,16},{16,20},{20,24},{24,28},{28,0},{1,5},{5... | collective-permute-start | bytes 786440 | tf_op jit(solution)/shard_map/ppermute | solution.py:21
  15.2 14.8 %copy-start.3 = (f32[2,2,32,1024]{3,1,2,0:T(2,128)}, f32[2,2,32,1024]{3,1,2,0:T(2,128)S(1)}, u32[]{:S(2)}) copy-start(f32[2,2,32,1024]{3,1,2,0:T(2,128)S(1)} %copy.52) | copy-start | bytes 1572868
  24.3 9.1 %copy-start.6 = (f32[4,2,32,256]{3,2,1,0:T(8,128)}, f32[4,2,32,256]{3,2,1,0:T(8,128)S(1)}, u32[]{:S(2)}) copy-start(f32[4,2,32,256]{3,2,1,0:T(8,128)S(1)} %collective-permute-done.1) | copy-start | bytes 786436
  24.5 10.6 %collective-permute-start.2 = (f32[4,6,32,2]{3,2,1,0:T(8,128)S(1)}, f32[4,6,32,2]{3,2,1,0:T(8,128)S(1)}, u32[]{:S(2)}, u32[]{:S(2)}) collective-permute-start(f32[4,6,32,2]{3,2,1,0:T(8,128)S(1)} %get-tuple-element.15), channel_id=1, source_target_pairs={{0,1},{1,2},{2,3},{3,0},{4,5},{5,6},{6,7},{7,4},{8,9},{9,10},{10,1... | collective-permute-start | bytes 18440 | tf_op jit(solution)/shard_map/ppermute | solution.py:21
  24.6 10.8 %collective-permute-start.3 = (f32[4,6,32,2]{3,2,1,0:T(8,128)S(1)}, f32[4,6,32,2]{3,2,1,0:T(8,128)S(1)}, u32[]{:S(2)}, u32[]{:S(2)}) collective-permute-start(f32[4,6,32,2]{3,2,1,0:T(8,128)S(1)} %get-tuple-element.16), channel_id=1, source_target_pairs={{1,0},{2,1},{3,2},{0,3},{5,4},{6,5},{7,6},{4,7},{9,8},{10,9},{11,1... | collective-permute-start | bytes 18440 | tf_op jit(solution)/shard_map/ppermute | solution.py:23
  30.0 33.7 %collective-permute-start.7 = (f32[2,4,1,1024]{3,1,2,0:T(4,128)}, f32[2,4,1,1024]{3,1,2,0:T(4,128)}, u32[]{:S(2)}, u32[]{:S(2)}) collective-permute-start(f32[2,4,1,1024]{3,1,2,0:T(4,128)} %get-tuple-element.14), channel_id=1, source_target_pairs={{0,1},{1,2},{2,3},{3,0},{4,5},{5,6},{6,7},{7,4},{8,9},{9,10},{10,1... | collective-permute-start | bytes 98312 | tf_op jit(solution)/shard_map/ppermute | solution.py:21
  30.0 34.5 %collective-permute-start.6 = (f32[2,4,1,1024]{3,1,2,0:T(4,128)S(1)}, f32[2,4,1,1024]{3,1,2,0:T(4,128)}, u32[]{:S(2)}, u32[]{:S(2)}) collective-permute-start(f32[2,4,1,1024]{3,1,2,0:T(4,128)S(1)} %get-tuple-element.13), channel_id=1, source_target_pairs={{1,0},{2,1},{3,2},{0,3},{5,4},{6,5},{7,6},{4,7},{9,8},{10,9},{11,1... | collective-permute-start | bytes 98312 | tf_op jit(solution)/shard_map/ppermute | solution.py:23
  35.8 1.0 %copy-start = (f32[4,6,32,260]{3,2,1,0:T(8,128)}, f32[4,6,32,260]{3,2,1,0:T(8,128)S(1)}, u32[]{:S(2)}) copy-start(f32[4,6,32,260]{3,2,1,0:T(8,128)S(1)} %pad_maximum_fusion.1) | copy-start | bytes 2396164
  36.9 1.2 %slice-start = ((f32[4,6,32,260]{3,2,1,0:T(8,128)}), f32[3,6,32,260]{3,2,1,0:T(8,128)S(1)}, s32[]{:S(2)}) async-start(f32[4,6,32,260]{3,2,1,0:T(8,128)} %copy-done), calls=%async_computation | async-start | bytes 1769472 | tf_op jit(solution)/shard_map/slice | solution.py:142
  44.0 16.5 %copy-start.14 = (s32[2,1024]{1,0:T(2,128)S(1)}, s32[2,1024]{1,0:T(2,128)}, u32[]{:S(2)}) copy-start(s32[2,1024]{1,0:T(2,128)} %param.6) | copy-start | bytes 24580
  53.6 8.9 %copy-start.7 = (f32[4,2,32,256]{3,2,1,0:T(8,128)S(1)}, f32[4,2,32,256]{3,2,1,0:T(8,128)}, u32[]{:S(2)}) copy-start(f32[4,2,32,256]{3,2,1,0:T(8,128)} %copy-done.6) | copy-start | bytes 786436
  53.6 8.9 %copy-start.10 = (f32[3,2,32,256]{3,2,1,0:T(8,128)S(1)}, f32[3,2,32,256]{3,2,1,0:T(8,128)}, u32[]{:S(2)}) copy-start(f32[3,2,32,256]{3,2,1,0:T(8,128)} %fusion.22) | copy-start | bytes 589828
  62.5 2.8 %copy-start.4 = (f32[2,2,32,1023]{3,2,1,0:T(8,128)S(1)}, f32[2,2,32,1023]{3,2,1,0:T(8,128)}, u32[]{:S(2)}) copy-start(f32[2,2,32,1023]{3,2,1,0:T(8,128)} %get-tuple-element.25) | copy-start | bytes 1571332
  62.6 2.8 %copy-start.5 = (f32[2,2,32,1023]{3,2,1,0:T(8,128)S(1)}, f32[2,2,32,1023]{3,2,1,0:T(8,128)}, u32[]{:S(2)}) copy-start(f32[2,2,32,1023]{3,2,1,0:T(8,128)} %get-tuple-element.26) | copy-start | bytes 1571332
  62.6 2.8 %copy-start.8 = (f32[2,1,32,1024]{3,2,1,0:T(8,128)S(1)}, f32[2,1,32,1024]{3,2,1,0:T(8,128)}, u32[]{:S(2)}) copy-start(f32[2,1,32,1024]{3,2,1,0:T(8,128)} %copy.51) | copy-start | bytes 786436
  62.6 2.8 %copy-start.9 = (f32[2,1,32,1024]{3,2,1,0:T(8,128)S(1)}, f32[2,1,32,1024]{3,2,1,0:T(8,128)}, u32[]{:S(2)}) copy-start(f32[2,1,32,1024]{3,2,1,0:T(8,128)} %copy.49) | copy-start | bytes 786436
  62.6 2.8 %copy-start.11 = (f32[2,2,32,1]{3,2,1,0:T(8,128)S(1)}, f32[2,2,32,1]{3,2,1,0:T(8,128)}, u32[]{:S(2)}) copy-start(f32[2,2,32,1]{3,2,1,0:T(8,128)} %get-tuple-element.27) | copy-start | bytes 1540
  62.6 2.8 %copy-start.12 = (f32[2,2,32,1]{3,2,1,0:T(8,128)S(1)}, f32[2,2,32,1]{3,2,1,0:T(8,128)}, u32[]{:S(2)}) copy-start(f32[2,2,32,1]{3,2,1,0:T(8,128)} %get-tuple-element.28) | copy-start | bytes 1540
  63.0 2.8 %copy-start.13 = (s32[2,1024]{1,0:T(2,128)S(1)}, s32[2,1024]{1,0:T(2,128)}, u32[]{:S(2)}) copy-start(s32[2,1024]{1,0:T(2,128)} %param.7) | copy-start | bytes 24580
  63.0 2.8 %copy-start.15 = (f32[32]{0:T(128)S(1)}, f32[32]{0:T(128)}, u32[]{:S(2)}) copy-start(f32[32]{0:T(128)} %compare_convert_fusion) | copy-start | bytes 388
  63.0 2.8 %copy-start.16 = (s32[32]{0:T(128)S(1)}, s32[32]{0:T(128)}, u32[]{:S(2)}) copy-start(s32[32]{0:T(128)} %iota_add_fusion) | copy-start | bytes 388
where the time goes:
time: 67.3 us; the launch traced here: 66.7 us
  other arithmetic  18.6 us (28%)
  blocking collectives  13.4 us (20%)
  starting transfers between devices  11.7 us (17%)
  waiting for transfers between devices  11.5 us (17%)
  local copies, waits for them, and re-layouts  10.4 us (15%)
  between operations  1.1 us (2%)
    ppermute x4, starting transfers between devices, with_halo(): lax.ppermute(head, axis, [((i + 1) % count, i) for i in range(count)])  8.54 us
    psum x1, blocking collectives, on_device(): lax.psum((numerator, denominator), 'sa')  8.25 us
    ppermute x4, waiting for transfers between devices, with_halo(): lax.ppermute(tail, axis, [(i, (i + 1) % count) for i in range(count)])  6.73 us
    all_gather x1, blocking collectives, on_device(): lax.all_gather(jnp.stack([local_shear, local_heat]), 'sa', axis=2, tiled=...  5.17 us
    ppermute x4, waiting for transfers between devices, with_halo(): lax.ppermute(head, axis, [((i + 1) % count, i) for i in range(count)])  4.8 us
    ppermute x4, starting transfers between devices, with_halo(): lax.ppermute(tail, axis, [(i, (i + 1) % count) for i in range(count)])  3.15 us
    slice x3, local copies, waits for them, and re-layouts, with_halo(): lax.slice_in_dim(cells, cells.shape[dim] - width, cells.shape[dim], axis=...  2.22 us
    another operation x5, other arithmetic, gradients(): return jnp.stack([along_x, along_y, along_z], axis=-4)  2.05 us
  transfers between devices with their start and end apart: 8, of which 4 were waited for; matrix products, arithmetic and copies ran while one was open for 39% of the time, Pallas kernels for 0%

commit v1 on v0

v1 whole, which is shorter than its diff:
```python
import functools

import jax
import jax.numpy as jnp
from jax import lax
from jax.experimental import pallas as pl
from jax.experimental.pallas import tpu as pltpu
from jax.sharding import PartitionSpec as P

gas_viscosity = 0.05
gas_diffusivity = 0.07
turbulent_prandtl = 0.85
melt_viscosity = 0.2
melt_diffusivity = 0.5
epsilon = 1e-06

LANES = 128
SUB = 8
EDGE = 4
PAIRS = ((0, 0), (1, 1), (2, 2), (0, 1), (0, 2), (1, 2))
VMEM = pl.BlockSpec(memory_space=pltpu.VMEM)


def shift_lanes(source, amount):
    extent = source.shape[-1]
    return pltpu.roll(source, amount % extent, source.ndim - 1)


def slot(row_block, cell, component, cells):
    return ((row_block * cells + cell) * 4 + component) * EDGE


def pack_gas(gas_ref, edge_ref):
    _, cells, rows, span = gas_ref.shape
    lane = lax.broadcasted_iota(jnp.int32, (SUB, LANES), 1)
    tile = jnp.zeros((SUB, LANES), jnp.float32)
    for block in range(rows // SUB):
        for cell in range(cells):
            for component in range(4):
                at = slot(block, cell, component, cells)
                here = pl.ds(SUB * block, SUB)
                first = gas_ref[component, cell, here, 0:LANES]
                last = gas_ref[component, cell, here, span - LANES : span]
                tile = jnp.where((lane >= at) & (lane < at + 2), shift_lanes(first, at), tile)
                tile = jnp.where(
                    (lane >= at + 2) & (lane < at + 4), shift_lanes(last, at + 4), tile
                )
    edge_ref[...] = tile


def pack_melt(melt_ref, first_ref, last_ref, rows_ref):
    components, cells, depth, _ = melt_ref.shape
    first_ref[...] = melt_ref[:, 0]
    last_ref[...] = melt_ref[:, cells - 1]
    for component in range(components):
        for cell in range(cells):
            at = component * cells + cell
            rows_ref[0, at : at + 1, :] = melt_ref[component, cell, 0:1, :]
            rows_ref[1, at : at + 1, :] = melt_ref[component, cell, depth - 1 : depth, :]


def binomial(source):
    pair = source + shift_lanes(source, 1)
    return pair + shift_lanes(pair, -1)


def germano(own_ref, left_ref, right_ref, below_ref, above_ref, base_ref, eddy_ref, sums_ref, field, coarse, strength):
    _, cells, rows, span = own_ref.shape
    wide = span + LANES
    lane = lax.broadcasted_iota(jnp.int32, (SUB, LANES), 1)
    for index in range(cells + 4):
        if index < 2:
            source, group, cell = left_ref, 0, index + cells - 2
        elif index < cells + 2:
            source, group, cell = own_ref, 1, index - 2
        else:
            source, group, cell = right_ref, 2, index - cells - 2
        for component in range(4 if 1 <= index <= cells + 2 else 3):
            for block in range(rows // SUB):
                at = slot(block, cell, component, cells)
                place = pl.ds(SUB * (block + 1), SUB)
                field[index, component, place, 0:span] = source[
                    component, cell, SUB * block : SUB * (block + 1), :
                ]
                field[index, component, place, span:wide] = jnp.where(
                    lane < LANES // 2,
                    shift_lanes(above_ref[group], -at),
                    shift_lanes(below_ref[group], LANES - 4 - at),
                )
            field[index, component, SUB - 1 : SUB, :] = -field[index, component, SUB : SUB + 1, :]
            field[index, component, SUB + rows : SUB + rows + 1, :] = field[
                index, component, SUB + rows - 1 : SUB + rows, :
            ]

    def filter_block(block, carry):
        place = pl.ds(pl.multiple_of(SUB * (block + 1), SUB), SUB)
        for component in range(3):
            pair = [
                field[i, component, place, :] + field[i + 1, component, place, :]
                for i in range(cells + 3)
            ]
            for i in range(cells + 2):
                coarse[i, component, place, :] = binomial(pair[i] + pair[i + 1])
        return carry

    lax.fori_loop(0, rows // SUB, filter_block, 0)
    for i in range(cells + 2):
        for component in range(3):
            coarse[i, component, SUB - 1 : SUB, :] = -coarse[i, component, SUB : SUB + 1, :]
            coarse[i, component, SUB + rows : SUB + rows + 1, :] = coarse[
                i, component, SUB + rows - 1 : SUB + rows, :
            ]

    row = lax.broadcasted_iota(jnp.int32, (SUB, wide), 0)

    def around(ref, index, component, block):
        previous, place, following = (
            pl.ds(pl.multiple_of(SUB * (block + step), SUB), SUB) for step in range(3)
        )
        middle = ref[index, component, place, :]
        below = jnp.where(row == SUB - 1, ref[index, component, previous, :], middle)
        above = jnp.where(row == 0, ref[index, component, following, :], middle)
        return (
            middle,
            (ref[index - 1, component, place, :], ref[index + 1, component, place, :]),
            (shift_lanes(middle, 1), shift_lanes(middle, -1)),
            (pltpu.roll(below, 1, 0), pltpu.roll(above, SUB - 1, 0)),
        )

    def strain(gradient):
        parts = [
            gradient[i][i] if i == j else gradient[i][j] + gradient[j][i] for i, j in PAIRS
        ]
        diagonal = parts[0] * parts[0] + parts[1] * parts[1] + parts[2] * parts[2]
        off = parts[3] * parts[3] + parts[4] * parts[4] + parts[5] * parts[5]
        return parts, jnp.sqrt(0.5 * diagonal + 0.25 * off)

    column = lax.broadcasted_iota(jnp.int32, (SUB, LANES), 1)

    def rate_block(block, carry):
        out_rows = pl.ds(pl.multiple_of(SUB * block, SUB), SUB)
        place = pl.ds(pl.multiple_of(SUB * (block + 1), SUB), SUB)
        stressed = []
        for index in range(1, cells + 3):
            points = [around(field, index, c, block) for c in range(3)]
            gradient = [[p[1 + j][1] - p[1 + j][0] for j in range(3)] for p in points]
            parts, magnitude = strain(gradient)
            stressed.append([magnitude * part for part in parts])
            if 2 <= index < cells + 2:
                cell = index - 2
                points = points + [around(field, index, 3, block)]
                gradient = gradient + [[points[3][1 + j][1] - points[3][1 + j][0] for j in range(3)]]
                speed = [0.5 * points[j][0][:, :span] for j in range(3)]
                own_magnitude = magnitude[:, :span]
                strength[cell, out_rows, :] = own_magnitude
                for c in range(4):
                    middle, along, across, upward = points[c]
                    laplace = (
                        (along[0] + along[1]) + (across[0] + across[1]) + (upward[0] + upward[1])
                    )[:, :span] - 6.0 * middle[:, :span]
                    advection = (
                        speed[0] * gradient[c][0][:, :span]
                        + speed[1] * gradient[c][1][:, :span]
                        + speed[2] * gradient[c][2][:, :span]
                    )
                    molecular = gas_viscosity if c < 3 else gas_diffusivity
                    base_ref[c, cell, out_rows, :] = molecular * laplace - advection
                    eddy = own_magnitude * laplace
                    eddy_ref[c, cell, out_rows, :] = eddy if c < 3 else eddy * (1.0 / turbulent_prandtl)
        filtered = []
        for k, (i, j) in enumerate(PAIRS):
            pair = [stressed[x][k] + stressed[x + 1][k] for x in range(cells + 1)]
            filtered.append([binomial(pair[x] + pair[x + 1])[:, :span] for x in range(cells)])
        products = []
        for i, j in PAIRS:
            values = [
                field[x, i, place, :] * field[x, j, place, :] for x in range(1, cells + 3)
            ]
            pair = [values[x] + values[x + 1] for x in range(cells + 1)]
            products.append([binomial(pair[x] + pair[x + 1])[:, :span] for x in range(cells)])
        tile = jnp.zeros((SUB, LANES), jnp.float32)
        for cell in range(cells):
            points = [around(coarse, cell + 1, c, block) for c in range(3)]
            gradient = [[(p[1 + j][1] - p[1 + j][0])[:, :span] for j in range(3)] for p in points]
            parts, magnitude = strain(gradient)
            quarter = 0.25 * magnitude
            speed = [0.25 * p[0][:, :span] for p in points]
            numerator = diagonal = off = 0.0
            for k, (i, j) in enumerate(PAIRS):
                model = filtered[k][cell] - quarter * parts[k]
                leonard = products[k][cell] - speed[i] * speed[j]
                numerator = numerator + leonard * model
                if i == j:
                    diagonal = diagonal + model * model
                else:
                    off = off + model * model
            denominator = diagonal + 0.5 * off
            total = jnp.sum(numerator, axis=1, keepdims=True) * (1.0 / 512.0)
            tile = jnp.where(column == cell, total, tile)
            total = jnp.sum(denominator, axis=1, keepdims=True) * (1.0 / 1024.0)
            tile = jnp.where(column == cells + cell, total, tile)
        sums_ref[out_rows, :] = tile
        return carry

    lax.fori_loop(0, rows // SUB, rate_block, 0)
    tiles = span // LANES
    for cell in range(cells):
        planes = (
            strength[cell, 0:1, :],
            own_ref[0, cell, 0:1, :],
            own_ref[3, cell, 0:1, :],
        )
        for p, plane in enumerate(planes):
            for t in range(tiles):
                at = rows + (p * cells + cell) * tiles + t
                sums_ref[at : at + 1, :] = plane[:, t * LANES : (t + 1) * LANES]
    used = rows + 3 * cells * tiles
    if used < sums_ref.shape[0]:
        sums_ref[used:, :] = jnp.zeros((sums_ref.shape[0] - used, LANES), jnp.float32)


def lilly(total, cells, span_cells):
    mean_numerator = total / span_cells
    mean_denominator = shift_lanes(total, -cells) / span_cells
    return -mean_numerator / (2.0 * (mean_denominator + epsilon))


def finish_gas(span_cells, devices, base_ref, eddy_ref, *refs):
    messages, out_ref = refs[:devices], refs[devices]
    _, cells, rows, _ = base_ref.shape
    total = messages[0][0:rows, :]
    for message in messages[1:]:
        total = total + message[0:rows, :]
    coefficient = lilly(total, cells, span_cells)
    for cell in range(cells):
        factor = coefficient[:, cell : cell + 1]
        for component in range(4):
            out_ref[component, cell] = base_ref[component, cell] + factor * eddy_ref[component, cell]


def finish_melt(
    span_cells, devices, rows, span, place_ref, melt_ref, left_ref, right_ref, below_ref, above_ref, mask_ref, level_ref, *refs
):
    messages, out_ref = refs[:devices], refs[devices]
    _, cells, depth, width = melt_ref.shape
    position = place_ref[0]
    total = messages[0][0:SUB, :]
    for message in messages[1:]:
        total = total + message[0:SUB, :]
    coefficient = lilly(total, cells, span_cells)
    tiles = span // LANES
    level_id = lax.broadcasted_iota(jnp.int32, (SUB, width), 0)
    for cell in range(cells):
        factor = coefficient[0:1, cell : cell + 1]
        planes = [
            jnp.concatenate(
                [
                    message[at : at + 1, :]
                    for message in messages
                    for at in range(rows + (p * cells + cell) * tiles, rows + (p * cells + cell + 1) * tiles)
                ],
                axis=1,
            )
            for p in range(3)
        ]
        eddy = factor * planes[0]
        mask = mask_ref[cell : cell + 1, :]
        shear = mask.astype(jnp.float32) * ((gas_viscosity + eddy) * 2.0 * planes[1])
        heat = (gas_diffusivity + eddy / turbulent_prandtl) * 2.0 * planes[2]
        top = position == 0
        shear = jnp.where(top, shear, 0.0)
        heat = jnp.where(top, heat, 0.0)
        levels = level_ref[cell : cell + 1, :]
        for component in range(2):
            at = component * cells + cell
            first = melt_ref[component, cell, 0:1, :]
            ghost = jnp.where(mask == 1, first, -first) if component == 0 else first
            upper = jnp.where(top, ghost, below_ref[at : at + 1, :])
            final = melt_ref[component, cell, depth - 1 : depth, :]
            lower = jnp.where(position == place_ref[1] - 1, final, above_ref[at : at + 1, :])
            for block in range(depth // SUB):
                here = slice(SUB * block, SUB * (block + 1))
                middle = melt_ref[component, cell, here, :]
                over = (
                    jnp.where(level_id == 0, upper, pltpu.roll(middle, 1, 0))
                    if block == 0
                    else melt_ref[component, cell, SUB * block - 1 : SUB * (block + 1) - 1, :]
                )
                under = (
                    jnp.where(level_id == SUB - 1, lower, pltpu.roll(middle, SUB - 1, 0))
                    if block == depth // SUB - 1
                    else melt_ref[component, cell, SUB * block + 1 : SUB * (block + 1) + 1, :]
                )
                before = left_ref[component, here, :] if cell == 0 else melt_ref[component, cell - 1, here, :]
                after = (
                    right_ref[component, here, :]
                    if cell == cells - 1
                    else melt_ref[component, cell + 1, here, :]
                )
                laplace = (before + after) + (over + under)
                laplace = laplace + (shift_lanes(middle, 1) + shift_lanes(middle, -1)) - 6.0 * middle
                rate = (melt_viscosity if component == 0 else melt_diffusivity) * laplace
                if block == 0:
                    rate = rate + jnp.where(level_id == 0, shear if component == 0 else heat, 0.0)
                if component == 0:
                    index = position * depth + SUB * block + level_id
                    rate = jnp.where(index >= levels, 0.0, rate)
                out_ref[component, cell, here, :] = rate


def ring(source, axis, step):
    count = lax.axis_size(axis)
    return lax.ppermute(source, axis, [(i, (i + step) % count) for i in range(count)])


def exchange(source, axis):
    count = lax.axis_size(axis)
    if count & (count - 1):
        return [source] + [ring(source, axis, -k) for k in range(1, count)]
    return [source] + [
        lax.ppermute(source, axis, [(i, i ^ k) for i in range(count)]) for k in range(1, count)
    ]


def call(kernel, outs, scratch=(), specs=None):
    return pl.pallas_call(
        kernel,
        out_shape=outs,
        in_specs=specs,
        out_specs=jax.tree.map(lambda _: VMEM, outs),
        scratch_shapes=scratch,
        compiler_params=pltpu.CompilerParams(vmem_limit_bytes=24 * 1024 * 1024),
    )


def array(*shape):
    return jax.ShapeDtypeStruct(shape, jnp.float32)


def on_device(gas, melt, surface_mask, melt_level):
    _, cells, rows, span = gas.shape
    _, _, depth, width = melt.shape
    devices = lax.axis_size("sa")
    span_cells = float(span * devices)
    gas_left = ring(gas, "gx", 1)
    gas_right = ring(gas, "gx", -1)
    edges = call(pack_gas, array(SUB, LANES), specs=[VMEM])(gas)
    edges = jnp.stack([ring(edges, "gx", 1), edges, ring(edges, "gx", -1)])
    below = ring(edges, "sa", 1)
    above = ring(edges, "sa", -1)
    first, last, depth_rows = call(
        pack_melt,
        (array(2, depth, width), array(2, depth, width), array(2, 2 * cells, width)),
        specs=[VMEM],
    )(melt)
    upper = ring(depth_rows[1], "sa", 1)
    lower = ring(depth_rows[0], "sa", -1)
    gas_left, gas_right, first, last = lax.optimization_barrier((gas_left, gas_right, first, last))
    melt_left = ring(last, "gx", 1)
    melt_right = ring(first, "gx", -1)
    wide = span + LANES
    used = rows + 3 * cells * (span // LANES)
    message_rows = -(-used // SUB) * SUB
    base, eddy, message = call(
        germano,
        (array(4, cells, rows, span), array(4, cells, rows, span), array(message_rows, LANES)),
        scratch=(
            pltpu.VMEM((cells + 4, 4, rows + 2 * SUB, wide), jnp.float32),
            pltpu.VMEM((cells + 2, 3, rows + 2 * SUB, wide), jnp.float32),
            pltpu.VMEM((cells, rows, span), jnp.float32),
        ),
        specs=[VMEM] * 5,
    )(gas, gas_left, gas_right, below, above)
    messages = exchange(message, "sa")
    gas_rate = call(
        functools.partial(finish_gas, span_cells, devices),
        array(4, cells, rows, span),
        specs=[VMEM] * (2 + devices),
    )(base, eddy, *messages)
    place = jnp.stack([lax.axis_index("sa"), devices]).astype(jnp.int32)
    melt_rate = call(
        functools.partial(finish_melt, span_cells, devices, rows, span),
        array(2, cells, depth, width),
        specs=[pl.BlockSpec(memory_space=pltpu.SMEM)] + [VMEM] * (7 + devices),
    )(place, melt, melt_left, melt_right, upper, lower, surface_mask, melt_level, *messages)
    return (gas_rate, melt_rate)


def solution(mesh):
    in_specs = (P(None, "gx", None, "sa"), P(None, "gx", "sa", None), P("gx", None), P("gx", None))
    out_specs = (P(None, "gx", None, "sa"), P(None, "gx", "sa", None))
    return jax.shard_map(
        on_device, mesh=mesh, in_specs=in_specs, out_specs=out_specs, check_vma=False
    )
```

time: 67.3 us -> 43.6 us (0.65)
  other arithmetic: 18.6 us -> 0.08 us
  blocking collectives: 13.4 us -> 0 us
  local copies, waits for them, and re-layouts: 10.4 us -> 2.63 us
  Pallas kernels: 0 us -> 6.96 us
  starting transfers between devices: 11.7 us -> 18.1 us
  waiting for transfers between devices: 11.5 us -> 14.9 us
    psum x1 -> x0, blocking collectives: 8.25 us -> none  [on_device(): lax.psum((numerator, denominator), 'sa')]
    pallas_call x0 -> x5, Pallas kernels: none -> 6.96 us  [the longest x1 4.17 us: on_device(): call(germano, (array(4, cells, rows, span), array(4, cells, rows, span),...]
    ppermute x8 -> x13, starting transfers between devices: 11.7 us -> 18.1 us  [the longest x10 16.4 us: ring(): lax.ppermute(source, axis, [(i, (i + step) % count) for i in range(count)])]
    slice x12 -> x0, local copies, waits for them, and re-layouts: 5.92 us -> none  [the longest x3 2.22 us: with_halo(): lax.slice_in_dim(cells, cells.shape[dim] - width, cells.shape[dim], axis=...]
    all_gather x1 -> x0, blocking collectives: 5.17 us -> none  [on_device(): lax.all_gather(jnp.stack([local_shear, local_heat]), 'sa', axis=2, tiled=...]
    ppermute x2 -> x0, local copies, waits for them, and re-layouts: 3.43 us -> none  [the longest x1 1.72 us: with_halo(): lax.ppermute(head, axis, [((i + 1) % count, i) for i in range(count)])]
    ppermute x8 -> x13, waiting for transfers between devices: 11.5 us -> 14.9 us  [the longest x10 11.6 us: ring(): lax.ppermute(source, axis, [(i, (i + step) % count) for i in range(count)])]
    slice x5 -> x0, other arithmetic: 3.01 us -> none  [the longest x3 1.58 us: strip_margin(): source[..., width:source.shape[-3] - width, :, width:source.shape[-1] - w...]
  transfers between devices with their start and end apart: 8 -> 13, of which waited for: 4 -> 5; matrix products, arithmetic and copies ran while one was open for 39% -> 0% of each run, Pallas kernels for 0% -> 2%
where the time goes in v1:
time: 43.6 us; the launch traced here: 43.4 us
  starting transfers between devices  18.1 us (42%)
  waiting for transfers between devices  14.9 us (34%)
  Pallas kernels  6.96 us (16%)
  local copies, waits for them, and re-layouts  2.63 us (6%)
  between operations  0.7 us (2%)
    ppermute x10, starting transfers between devices, ring(): lax.ppermute(source, axis, [(i, (i + step) % count) for i in range(count)])  16.4 us
    ppermute x10, waiting for transfers between devices, ring(): lax.ppermute(source, axis, [(i, (i + step) % count) for i in range(count)])  11.6 us
    pallas_call x1, Pallas kernels, on_device(): call(germano, (array(4, cells, rows, span), array(4, cells, rows, span),...  4.17 us
    ppermute x3, waiting for transfers between devices, exchange(): lax.ppermute(source, axis, [(i, i ^ k) for i in range(count)])  3.37 us
    unnamed x12, local copies, waits for them, and re-layouts  2.63 us
    pallas_call x1, Pallas kernels, on_device(): call(functools.partial(finish_melt, span_cells, devices, rows, span), arr...  1.74 us
    ppermute x3, starting transfers between devices, exchange(): lax.ppermute(source, axis, [(i, i ^ k) for i in range(count)])  1.7 us
    pallas_call x1, Pallas kernels, on_device(): call(functools.partial(finish_gas, span_cells, devices), array(4, cells,...  0.88 us
  transfers between devices with their start and end apart: 13, of which 5 were waited for; matrix products, arithmetic and copies ran while one was open for 0% of the time, Pallas kernels for 2%

profile of v1, /device:TPU:0, one launch (start us, length us, event | category | flops | bytes accessed | tf_op | source)
XLA Modules:
  0.0 43.4 jit_solution(16989669214038673120)
XLA Ops:
  0.6 3.0 %collective-permute-start = (f32[4,2,32,256]{3,2,1,0:T(8,128)}, f32[4,2,32,256]{3,2,1,0:T(8,128)S(1)}, u32[]{:S(2)}, u32[]{:S(2)}) collective-permute-start(f32[4,2,32,256]{3,2,1,0:T(8,128)} %own_ref.1), channel_id=1, source_target_pairs={{0,4},{4,8},{8,12},{12,16},{16,20},{20,24},{24,28},{28,0},{1,5},{5... | collective-permute-start | bytes 786440 | tf_op jit(solution)/shard_map/ppermute | solution.py:313
  3.6 3.1 %collective-permute-start.1 = (f32[4,2,32,256]{3,2,1,0:T(8,128)}, f32[4,2,32,256]{3,2,1,0:T(8,128)S(1)}, u32[]{:S(2)}, u32[]{:S(2)}) collective-permute-start(f32[4,2,32,256]{3,2,1,0:T(8,128)} %own_ref.1), channel_id=1, source_target_pairs={{0,28},{4,0},{8,4},{12,8},{16,12},{20,16},{24,20},{28,24},{1,29},{... | collective-permute-start | bytes 786440 | tf_op jit(solution)/shard_map/ppermute | solution.py:313
  6.8 1.0 %copy-done.2 = f32[4,2,32,256]{3,2,1,0:T(8,128)S(1)} copy-done((f32[4,2,32,256]{3,2,1,0:T(8,128)S(1)}, f32[4,2,32,256]{3,2,1,0:T(8,128)}, u32[]{:S(2)}) %copy-start.2) | copy-done | bytes 262168
  7.7 0.1 shard_map.60
  7.9 2.0 %collective-permute-start.3 = (f32[8,128]{1,0:T(8,128)S(1)}, f32[8,128]{1,0:T(8,128)S(1)}, u32[]{:S(2)}, u32[]{:S(2)}) collective-permute-start(f32[8,128]{1,0:T(8,128)S(1)} %shard_map.60), channel_id=1, source_target_pairs={{0,28},{4,0},{8,4},{12,8},{16,12},{20,16},{24,20},{28,24},{1,29},{... | collective-permute-start | bytes 12296 | tf_op jit(solution)/shard_map/ppermute | solution.py:313
  9.9 0.1 collective-permute-start.2
  10.0 7.5 %collective-permute-done.3 = f32[8,128]{1,0:T(8,128)S(1)} collective-permute-done((f32[8,128]{1,0:T(8,128)S(1)}, f32[8,128]{1,0:T(8,128)S(1)}, u32[]{:S(2)}, u32[]{:S(2)}) %collective-permute-start.3) | collective-permute-done | bytes 4128 | tf_op jit(solution)/shard_map/ppermute | solution.py:313
  17.4 0.0 collective-permute-done.2
  17.4 0.0 collective-permute-start.4
  17.4 1.7 %collective-permute-start.5 = (f32[3,8,128]{2,1,0:T(8,128)S(1)}, f32[3,8,128]{2,1,0:T(8,128)S(1)}, u32[]{:S(2)}, u32[]{:S(2)}) collective-permute-start(f32[3,8,128]{2,1,0:T(8,128)S(1)} %pad_maximum_fusion), channel_id=1, source_target_pairs={{0,3},{1,0},{2,1},{3,2},{4,7},{5,4},{6,5},{7,6},{8,11},{9,8},{10,9... | collective-permute-start | bytes 36872 | tf_op jit(solution)/shard_map/ppermute | solution.py:313
  19.2 1.0 %copy-done = f32[2,2,32,1024]{3,2,1,0:T(8,128)S(1)} copy-done((f32[2,2,32,1024]{3,2,1,0:T(8,128)S(1)}, f32[2,2,32,1024]{3,2,1,0:T(8,128)}, u32[]{:S(2)}) %copy-start) | copy-done | bytes 524312
  20.3 0.0 collective-permute-done.left_ref
  20.3 0.0 collective-permute-done.1.right_ref
  20.3 0.3 collective-permute-done.4.below_ref
  20.5 0.0 collective-permute-done.5.above_ref
  20.6 0.6 %copy-done.3 = f32[4,2,32,256]{3,2,1,0:T(8,128)S(1)} copy-done((f32[4,2,32,256]{3,2,1,0:T(8,128)S(1)}, f32[4,2,32,256]{3,2,1,0:T(8,128)}, u32[]{:S(2)}) %copy-start.3) | copy-done | bytes 262168
  21.2 4.2 %shard_map.61 = (f32[4,2,32,256]{3,2,1,0:T(8,128)S(1)}, f32[4,2,32,256]{3,2,1,0:T(8,128)S(1)}, f32[48,128]{1,0:T(8,128)S(1)}) custom-call(f32[4,2,32,256]{3,2,1,0:T(8,128)S(1)} %copy-done.3, f32[4,2,32,256]{3,2,1,0:T(8,128)S(1)} %collective-permute-done.left_ref, f32[4,2,32,256]{3,2,1,0:T(8,128)S(1)} %collective-permute-done.1.right_ref, ...), custom_call_target="tpu_custom_call" | custom-call | tf_op jit(solution)/shard_map/pallas_call | solution.py:364
  25.3 0.0 copy-start.1
  25.4 1.1 %collective-permute-start.6 = (f32[48,128]{1,0:T(8,128)S(1)}, f32[48,128]{1,0:T(8,128)S(1)}, u32[]{:S(2)}, u32[]{:S(2)}) collective-permute-start(f32[48,128]{1,0:T(8,128)S(1)} %get-tuple-element.18.refs_0_), channel_id=1, source_target_pairs={{0,1},{1,0},{2,3},{3,2},{4,5},{5,4},{6,7},{7,6},{8,9},{9,8},{10,11... | collective-permute-start | bytes 73736 | tf_op jit(solution)/shard_map/ppermute | solution.py:321
  26.4 0.6 %collective-permute-start.7 = (f32[48,128]{1,0:T(8,128)S(1)}, f32[48,128]{1,0:T(8,128)S(1)}, u32[]{:S(2)}, u32[]{:S(2)}) collective-permute-start(f32[48,128]{1,0:T(8,128)S(1)} %get-tuple-element.18.refs_0_), channel_id=1, source_target_pairs={{0,2},{1,3},{2,0},{3,1},{4,6},{5,7},{6,4},{7,5},{8,10},{9,11},{10,... | collective-permute-start | bytes 73736 | tf_op jit(solution)/shard_map/ppermute | solution.py:321
  27.0 0.3 collective-permute-start.9
  27.3 4.4 %collective-permute-start.10 = (f32[2,32,1024]{2,1,0:T(8,128)S(1)}, f32[2,32,1024]{2,1,0:T(8,128)S(1)}, u32[]{:S(2)}, u32[]{:S(2)}) collective-permute-start(f32[2,32,1024]{2,1,0:T(8,128)S(1)} %get-tuple-element.20), channel_id=1, source_target_pairs={{0,28},{4,0},{8,4},{12,8},{16,12},{20,16},{24,20},{28,24},{1,29},{... | collective-permute-start | bytes 786440 | tf_op jit(solution)/shard_map/ppermute | solution.py:313
  31.7 0.0 collective-permute-start.11
  31.7 1.7 %collective-permute-start.12 = (f32[4,1024]{1,0:T(4,128)S(1)}, f32[4,1024]{1,0:T(4,128)S(1)}, u32[]{:S(2)}, u32[]{:S(2)}) collective-permute-start(f32[4,1024]{1,0:T(4,128)S(1)} %get-tuple-element.22), channel_id=1, source_target_pairs={{0,3},{1,0},{2,1},{3,2},{4,7},{5,4},{6,5},{7,6},{8,11},{9,8},{10,9... | collective-permute-start | bytes 49160 | tf_op jit(solution)/shard_map/ppermute | solution.py:313
  33.5 0.0 collective-permute-done.7.refs_2_
  33.5 0.1 collective-permute-start.8
  33.5 0.1 pad_add_fusion.place_ref
  33.6 3.4 %collective-permute-done.8.refs_3_ = f32[48,128]{1,0:T(8,128)S(1)} collective-permute-done((f32[48,128]{1,0:T(8,128)S(1)}, f32[48,128]{1,0:T(8,128)S(1)}, u32[]{:S(2)}, u32[]{:S(2)}) %collective-permute-start.8) | collective-permute-done | bytes 24608 | tf_op jit(solution)/shard_map/ppermute | solution.py:321
  37.0 0.9 %shard_map.62 = f32[4,2,32,256]{3,2,1,0:T(8,128)} custom-call(f32[4,2,32,256]{3,2,1,0:T(8,128)S(1)} %get-tuple-element.16.base_ref, f32[4,2,32,256]{3,2,1,0:T(8,128)S(1)} %get-tuple-element.17.eddy_ref, f32[48,128]{1,0:T(8,128)S(1)} %get-tuple-element.18.refs_0_, f32[48,128]{1,0:T(8,128)S(1)} %collective-permute-done.6.refs_1_, ...), custom_call_target="tpu_custom_call" | custom-call | tf_op jit(solution)/shard_map/pallas_call | solution.py:375
  37.9 0.9 %collective-permute-done.9.left_ref = f32[2,32,1024]{2,1,0:T(8,128)S(1)} collective-permute-done((f32[2,32,1024]{2,1,0:T(8,128)S(1)}, f32[2,32,1024]{2,1,0:T(8,128)S(1)}, u32[]{:S(2)}, u32[]{:S(2)}) %collective-permute-start.9) | collective-permute-done | bytes 262176 | tf_op jit(solution)/shard_map/ppermute | solution.py:313
  38.8 2.9 %collective-permute-done.10.right_ref = f32[2,32,1024]{2,1,0:T(8,128)S(1)} collective-permute-done((f32[2,32,1024]{2,1,0:T(8,128)S(1)}, f32[2,32,1024]{2,1,0:T(8,128)S(1)}, u32[]{:S(2)}, u32[]{:S(2)}) %collective-permute-start.10) | collective-permute-done | bytes 262176 | tf_op jit(solution)/shard_map/ppermute | solution.py:313
  41.7 1.7 %shard_map.63 = f32[2,2,32,1024]{3,2,1,0:T(8,128)} custom-call(s32[2]{0:T(128)S(1)} %pad_add_fusion.place_ref, f32[2,2,32,1024]{3,2,1,0:T(8,128)S(1)} %copy-done.1, f32[2,32,1024]{2,1,0:T(8,128)S(1)} %collective-permute-done.9.left_ref, f32[2,32,1024]{2,1,0:T(8,128)S(1)} %collective-permute-done.10.right_ref, ...), custom_call_target="tpu_custom_call" | custom-call | tf_op jit(solution)/shard_map/pallas_call | solution.py:381
  (14 shorter events, 0.1 us)
Async XLA Ops:
  0.6 19.6 %collective-permute-start = (f32[4,2,32,256]{3,2,1,0:T(8,128)}, f32[4,2,32,256]{3,2,1,0:T(8,128)S(1)}, u32[]{:S(2)}, u32[]{:S(2)}) collective-permute-start(f32[4,2,32,256]{3,2,1,0:T(8,128)} %own_ref.1), channel_id=1, source_target_pairs={{0,4},{4,8},{8,12},{12,16},{16,20},{20,24},{24,28},{28,0},{1,5},{5... | collective-permute-start | bytes 786440 | tf_op jit(solution)/shard_map/ppermute | solution.py:313
  3.6 16.6 %collective-permute-start.1 = (f32[4,2,32,256]{3,2,1,0:T(8,128)}, f32[4,2,32,256]{3,2,1,0:T(8,128)S(1)}, u32[]{:S(2)}, u32[]{:S(2)}) collective-permute-start(f32[4,2,32,256]{3,2,1,0:T(8,128)} %own_ref.1), channel_id=1, source_target_pairs={{0,28},{4,0},{8,4},{12,8},{16,12},{20,16},{24,20},{28,24},{1,29},{... | collective-permute-start | bytes 786440 | tf_op jit(solution)/shard_map/ppermute | solution.py:313
  6.8 1.0 %copy-start.2 = (f32[4,2,32,256]{3,2,1,0:T(8,128)S(1)}, f32[4,2,32,256]{3,2,1,0:T(8,128)}, u32[]{:S(2)}) copy-start(f32[4,2,32,256]{3,2,1,0:T(8,128)} %own_ref.1) | copy-start | bytes 786436
  7.9 9.5 %collective-permute-start.3 = (f32[8,128]{1,0:T(8,128)S(1)}, f32[8,128]{1,0:T(8,128)S(1)}, u32[]{:S(2)}, u32[]{:S(2)}) collective-permute-start(f32[8,128]{1,0:T(8,128)S(1)} %shard_map.60), channel_id=1, source_target_pairs={{0,28},{4,0},{8,4},{12,8},{16,12},{20,16},{24,20},{28,24},{1,29},{... | collective-permute-start | bytes 12296 | tf_op jit(solution)/shard_map/ppermute | solution.py:313
  9.9 7.5 %collective-permute-start.2 = (f32[8,128]{1,0:T(8,128)S(1)}, f32[8,128]{1,0:T(8,128)S(1)}, u32[]{:S(2)}, u32[]{:S(2)}) collective-permute-start(f32[8,128]{1,0:T(8,128)S(1)} %shard_map.60), channel_id=1, source_target_pairs={{0,4},{4,8},{8,12},{12,16},{16,20},{20,24},{24,28},{28,0},{1,5},{5... | collective-permute-start | bytes 12296 | tf_op jit(solution)/shard_map/ppermute | solution.py:313
  17.4 3.1 %collective-permute-start.4 = (f32[3,8,128]{2,1,0:T(8,128)S(1)}, f32[3,8,128]{2,1,0:T(8,128)S(1)}, u32[]{:S(2)}, u32[]{:S(2)}) collective-permute-start(f32[3,8,128]{2,1,0:T(8,128)S(1)} %pad_maximum_fusion), channel_id=1, source_target_pairs={{0,1},{1,2},{2,3},{3,0},{4,5},{5,6},{6,7},{7,4},{8,9},{9,10},{10,1... | collective-permute-start | bytes 36872 | tf_op jit(solution)/shard_map/ppermute | solution.py:313
  17.4 3.1 %collective-permute-start.5 = (f32[3,8,128]{2,1,0:T(8,128)S(1)}, f32[3,8,128]{2,1,0:T(8,128)S(1)}, u32[]{:S(2)}, u32[]{:S(2)}) collective-permute-start(f32[3,8,128]{2,1,0:T(8,128)S(1)} %pad_maximum_fusion), channel_id=1, source_target_pairs={{0,3},{1,0},{2,1},{3,2},{4,7},{5,4},{6,5},{7,6},{8,11},{9,8},{10,9... | collective-permute-start | bytes 36872 | tf_op jit(solution)/shard_map/ppermute | solution.py:313
  19.2 1.0 %copy-start = (f32[2,2,32,1024]{3,2,1,0:T(8,128)S(1)}, f32[2,2,32,1024]{3,2,1,0:T(8,128)}, u32[]{:S(2)}) copy-start(f32[2,2,32,1024]{3,2,1,0:T(8,128)} %melt_ref.3) | copy-start | bytes 1572868
  20.2 0.9 %copy-start.3 = (f32[4,2,32,256]{3,2,1,0:T(8,128)S(1)}, f32[4,2,32,256]{3,2,1,0:T(8,128)}, u32[]{:S(2)}) copy-start(f32[4,2,32,256]{3,2,1,0:T(8,128)} %own_ref.1) | copy-start | bytes 786436
  25.3 16.3 %copy-start.1 = (f32[2,2,32,1024]{3,2,1,0:T(8,128)S(1)}, f32[2,2,32,1024]{3,2,1,0:T(8,128)}, u32[]{:S(2)}) copy-start(f32[2,2,32,1024]{3,2,1,0:T(8,128)} %melt_ref.3) | copy-start | bytes 1572868
  25.4 6.4 %collective-permute-start.6 = (f32[48,128]{1,0:T(8,128)S(1)}, f32[48,128]{1,0:T(8,128)S(1)}, u32[]{:S(2)}, u32[]{:S(2)}) collective-permute-start(f32[48,128]{1,0:T(8,128)S(1)} %get-tuple-element.18.refs_0_), channel_id=1, source_target_pairs={{0,1},{1,0},{2,3},{3,2},{4,5},{5,4},{6,7},{7,6},{8,9},{9,8},{10,11... | collective-permute-start | bytes 73736 | tf_op jit(solution)/shard_map/ppermute | solution.py:321
  26.4 7.1 %collective-permute-start.7 = (f32[48,128]{1,0:T(8,128)S(1)}, f32[48,128]{1,0:T(8,128)S(1)}, u32[]{:S(2)}, u32[]{:S(2)}) collective-permute-start(f32[48,128]{1,0:T(8,128)S(1)} %get-tuple-element.18.refs_0_), channel_id=1, source_target_pairs={{0,2},{1,3},{2,0},{3,1},{4,6},{5,7},{6,4},{7,5},{8,10},{9,11},{10,... | collective-permute-start | bytes 73736 | tf_op jit(solution)/shard_map/ppermute | solution.py:321
  27.0 11.8 %collective-permute-start.9 = (f32[2,32,1024]{2,1,0:T(8,128)S(1)}, f32[2,32,1024]{2,1,0:T(8,128)S(1)}, u32[]{:S(2)}, u32[]{:S(2)}) collective-permute-start(f32[2,32,1024]{2,1,0:T(8,128)S(1)} %get-tuple-element.19), channel_id=1, source_target_pairs={{0,4},{4,8},{8,12},{12,16},{16,20},{20,24},{24,28},{28,0},{1,5},{5... | collective-permute-start | bytes 786440 | tf_op jit(solution)/shard_map/ppermute | solution.py:313
  27.3 14.4 %collective-permute-start.10 = (f32[2,32,1024]{2,1,0:T(8,128)S(1)}, f32[2,32,1024]{2,1,0:T(8,128)S(1)}, u32[]{:S(2)}, u32[]{:S(2)}) collective-permute-start(f32[2,32,1024]{2,1,0:T(8,128)S(1)} %get-tuple-element.20), channel_id=1, source_target_pairs={{0,28},{4,0},{8,4},{12,8},{16,12},{20,16},{24,20},{28,24},{1,29},{... | collective-permute-start | bytes 786440 | tf_op jit(solution)/shard_map/ppermute | solution.py:313
  31.7 6.2 %collective-permute-start.11 = (f32[4,1024]{1,0:T(4,128)S(1)}, f32[4,1024]{1,0:T(4,128)S(1)}, u32[]{:S(2)}, u32[]{:S(2)}) collective-permute-start(f32[4,1024]{1,0:T(4,128)S(1)} %get-tuple-element.23), channel_id=1, source_target_pairs={{0,1},{1,2},{2,3},{3,0},{4,5},{5,6},{6,7},{7,4},{8,9},{9,10},{10,1... | collective-permute-start | bytes 49160 | tf_op jit(solution)/shard_map/ppermute | solution.py:313
  31.7 6.1 %collective-permute-start.12 = (f32[4,1024]{1,0:T(4,128)S(1)}, f32[4,1024]{1,0:T(4,128)S(1)}, u32[]{:S(2)}, u32[]{:S(2)}) collective-permute-start(f32[4,1024]{1,0:T(4,128)S(1)} %get-tuple-element.22), channel_id=1, source_target_pairs={{0,3},{1,0},{2,1},{3,2},{4,7},{5,4},{6,5},{7,6},{8,11},{9,8},{10,9... | collective-permute-start | bytes 49160 | tf_op jit(solution)/shard_map/ppermute | solution.py:313
  33.5 3.5 %collective-permute-start.8 = (f32[48,128]{1,0:T(8,128)S(1)}, f32[48,128]{1,0:T(8,128)S(1)}, u32[]{:S(2)}, u32[]{:S(2)}) collective-permute-start(f32[48,128]{1,0:T(8,128)S(1)} %get-tuple-element.18.refs_0_), channel_id=1, source_target_pairs={{0,3},{1,2},{2,1},{3,0},{4,7},{5,6},{6,5},{7,4},{8,11},{9,10},{10,... | collective-permute-start | bytes 73736 | tf_op jit(solution)/shard_map/ppermute | solution.py:321
  37.0 4.7 %copy-start.4 = (s32[2,1024]{1,0:T(2,128)S(1)}, s32[2,1024]{1,0:T(2,128)}, u32[]{:S(2)}) copy-start(s32[2,1024]{1,0:T(2,128)} %mask_ref.1) | copy-start | bytes 24580
  37.0 4.7 %copy-start.5 = (s32[2,1024]{1,0:T(2,128)S(1)}, s32[2,1024]{1,0:T(2,128)}, u32[]{:S(2)}) copy-start(s32[2,1024]{1,0:T(2,128)} %level_ref.1) | copy-start | bytes 24580

commit v2 on v1

--- a/solution.py
+++ b/solution.py
@@ -19,6 +19,8 @@
 EDGE = 4
 PAIRS = ((0, 0), (1, 1), (2, 2), (0, 1), (0, 2), (1, 2))
 VMEM = pl.BlockSpec(memory_space=pltpu.VMEM)
+SMEM = pl.BlockSpec(memory_space=pltpu.SMEM)
+ANY = pl.BlockSpec(memory_space=pl.ANY)
 
 
 def shift_lanes(source, amount):
@@ -30,8 +32,9 @@
     return ((row_block * cells + cell) * 4 + component) * EDGE
 
 
-def pack_gas(gas_ref, edge_ref):
+def pack_sides(place_ref, gas_ref, melt_ref, mate_ref, cross_ref):
     _, cells, rows, span = gas_ref.shape
+    components, _, depth, width = melt_ref.shape
     lane = lax.broadcasted_iota(jnp.int32, (SUB, LANES), 1)
     tile = jnp.zeros((SUB, LANES), jnp.float32)
     for block in range(rows // SUB):
@@ -45,18 +48,34 @@
                 tile = jnp.where(
                     (lane >= at + 2) & (lane < at + 4), shift_lanes(last, at + 4), tile
                 )
-    edge_ref[...] = tile
-
-
-def pack_melt(melt_ref, first_ref, last_ref, rows_ref):
-    components, cells, depth, _ = melt_ref.shape
-    first_ref[...] = melt_ref[:, 0]
-    last_ref[...] = melt_ref[:, cells - 1]
+    mate_ref[0:SUB, :] = tile
+    cross_ref[0:SUB, :] = tile
+    even = place_ref[0] % 2 == 0
     for component in range(components):
         for cell in range(cells):
-            at = component * cells + cell
-            rows_ref[0, at : at + 1, :] = melt_ref[component, cell, 0:1, :]
-            rows_ref[1, at : at + 1, :] = melt_ref[component, cell, depth - 1 : depth, :]
+            first = melt_ref[component, cell, 0:1, :]
+            last = melt_ref[component, cell, depth - 1 : depth, :]
+            mate = jnp.where(even, last, first)
+            cross = jnp.where(even, first, last)
+            for t in range(width // LANES):
+                at = SUB + t * components * cells + component * cells + cell
+                mate_ref[at : at + 1, :] = mate[:, t * LANES : (t + 1) * LANES]
+                cross_ref[at : at + 1, :] = cross[:, t * LANES : (t + 1) * LANES]
+
+
+def pack_melt(place_ref, melt_ref, after_ref, mate_ref, cross_ref):
+    last = melt_ref.shape[1] - 1
+    even = place_ref[1] % 2 == 0
+
+    @pl.when(even)
+    def _():
+        mate_ref[...] = melt_ref[:, last]
+        cross_ref[...] = melt_ref[:, 0]
+
+    @pl.when(jnp.logical_not(even))
+    def _():
+        mate_ref[...] = melt_ref[:, 0]
+        cross_ref[...] = melt_ref[:, last]
 
 
 def binomial(source):
@@ -64,28 +83,50 @@
     return pair + shift_lanes(pair, -1)
 
 
-def germano(own_ref, left_ref, right_ref, below_ref, above_ref, base_ref, eddy_ref, sums_ref, field, coarse, strength):
+def germano(
+    place_ref,
+    own_ref,
+    mate_ref,
+    cross_ref,
+    halo_ref,
+    halo_mate_ref,
+    halo_cross_ref,
+    base_ref,
+    eddy_ref,
+    sums_ref,
+    field,
+    coarse,
+    strength,
+):
     _, cells, rows, span = own_ref.shape
     wide = span + LANES
     lane = lax.broadcasted_iota(jnp.int32, (SUB, LANES), 1)
+    even = place_ref[1] % 2 == 0
+    halo = halo_ref[...]
+    halo_left = jnp.where(even, halo_cross_ref[...], halo_mate_ref[...])
+    halo_right = jnp.where(even, halo_mate_ref[...], halo_cross_ref[...])
     for index in range(cells + 4):
         if index < 2:
-            source, group, cell = left_ref, 0, index + cells - 2
+            columns, cell = halo_left, index + cells - 2
+            sources = cross_ref, mate_ref
         elif index < cells + 2:
-            source, group, cell = own_ref, 1, index - 2
+            columns, cell = halo, index - 2
+            sources = own_ref, own_ref
         else:
-            source, group, cell = right_ref, 2, index - cells - 2
+            columns, cell = halo_right, index - cells - 2
+            sources = mate_ref, cross_ref
         for component in range(4 if 1 <= index <= cells + 2 else 3):
             for block in range(rows // SUB):
                 at = slot(block, cell, component, cells)
                 place = pl.ds(SUB * (block + 1), SUB)
-                field[index, component, place, 0:span] = source[
-                    component, cell, SUB * block : SUB * (block + 1), :
-                ]
+                here = slice(SUB * block, SUB * (block + 1))
+                field[index, component, place, 0:span] = jnp.where(
+                    even, sources[0][component, cell, here, :], sources[1][component, cell, here, :]
+                )
                 field[index, component, place, span:wide] = jnp.where(
                     lane < LANES // 2,
-                    shift_lanes(above_ref[group], -at),
-                    shift_lanes(below_ref[group], LANES - 4 - at),
+                    shift_lanes(columns, -at),
+                    shift_lanes(columns, LANES - 4 - at),
                 )
             field[index, component, SUB - 1 : SUB, :] = -field[index, component, SUB : SUB + 1, :]
             field[index, component, SUB + rows : SUB + rows + 1, :] = field[
@@ -225,13 +266,9 @@
     return -mean_numerator / (2.0 * (mean_denominator + epsilon))
 
 
-def finish_gas(span_cells, devices, base_ref, eddy_ref, *refs):
-    messages, out_ref = refs[:devices], refs[devices]
+def finish_gas(span_cells, mine_ref, theirs_ref, base_ref, eddy_ref, out_ref):
     _, cells, rows, _ = base_ref.shape
-    total = messages[0][0:rows, :]
-    for message in messages[1:]:
-        total = total + message[0:rows, :]
-    coefficient = lilly(total, cells, span_cells)
+    coefficient = lilly(mine_ref[0:rows, :] + theirs_ref[0:rows, :], cells, span_cells)
     for cell in range(cells):
         factor = coefficient[:, cell : cell + 1]
         for component in range(4):
@@ -239,30 +276,47 @@
 
 
 def finish_melt(
-    span_cells, devices, rows, span, place_ref, melt_ref, left_ref, right_ref, below_ref, above_ref, mask_ref, level_ref, *refs
+    span_cells,
+    devices,
+    rows,
+    span,
+    place_ref,
+    mine_ref,
+    theirs_ref,
+    melt_ref,
+    beside_mate_ref,
+    beside_cross_ref,
+    mate_ref,
+    cross_ref,
+    mask_ref,
+    level_ref,
+    out_ref,
 ):
-    messages, out_ref = refs[:devices], refs[devices]
-    _, cells, depth, width = melt_ref.shape
+    components, cells, depth, width = melt_ref.shape
     position = place_ref[0]
-    total = messages[0][0:SUB, :]
-    for message in messages[1:]:
-        total = total + message[0:SUB, :]
-    coefficient = lilly(total, cells, span_cells)
+    even = position % 2 == 0
+    even_cell = place_ref[1] % 2 == 0
+    coefficient = lilly(mine_ref[0:SUB, :] + theirs_ref[0:SUB, :], cells, span_cells)
     tiles = span // LANES
+    held = (mine_ref.shape[0] - rows) // (devices // 2)
     level_id = lax.broadcasted_iota(jnp.int32, (SUB, width), 0)
+
+    def row_of(ref, at):
+        step = components * cells
+        return jnp.concatenate(
+            [ref[at + t * step : at + t * step + 1, :] for t in range(width // LANES)], axis=1
+        )
+
     for cell in range(cells):
         factor = coefficient[0:1, cell : cell + 1]
-        planes = [
-            jnp.concatenate(
-                [
-                    message[at : at + 1, :]
-                    for message in messages
-                    for at in range(rows + (p * cells + cell) * tiles, rows + (p * cells + cell + 1) * tiles)
-                ],
-                axis=1,
-            )
-            for p in range(3)
-        ]
+        planes = []
+        for p in range(3):
+            parts = []
+            for device in range(devices):
+                ref = mine_ref if device < devices // 2 else theirs_ref
+                at = rows + device % (devices // 2) * held + (p * cells + cell) * tiles
+                parts = parts + [ref[at + t : at + t + 1, :] for t in range(tiles)]
+            planes.append(jnp.concatenate(parts, axis=1))
         eddy = factor * planes[0]
         mask = mask_ref[cell : cell + 1, :]
         shear = mask.astype(jnp.float32) * ((gas_viscosity + eddy) * 2.0 * planes[1])
@@ -271,13 +325,14 @@
         shear = jnp.where(top, shear, 0.0)
         heat = jnp.where(top, heat, 0.0)
         levels = level_ref[cell : cell + 1, :]
-        for component in range(2):
-            at = component * cells + cell
+        for component in range(components):
+            at = SUB + component * cells + cell
+            from_mate, from_cross = row_of(mate_ref, at), row_of(cross_ref, at)
             first = melt_ref[component, cell, 0:1, :]
             ghost = jnp.where(mask == 1, first, -first) if component == 0 else first
-            upper = jnp.where(top, ghost, below_ref[at : at + 1, :])
+            upper = jnp.where(top, ghost, jnp.where(even, from_cross, from_mate))
             final = melt_ref[component, cell, depth - 1 : depth, :]
-            lower = jnp.where(position == place_ref[1] - 1, final, above_ref[at : at + 1, :])
+            lower = jnp.where(position == devices - 1, final, jnp.where(even, from_mate, from_cross))
             for block in range(depth // SUB):
                 here = slice(SUB * block, SUB * (block + 1))
                 middle = melt_ref[component, cell, here, :]
@@ -291,9 +346,21 @@
                     if block == depth // SUB - 1
                     else melt_ref[component, cell, SUB * block + 1 : SUB * (block + 1) + 1, :]
                 )
-                before = left_ref[component, here, :] if cell == 0 else melt_ref[component, cell - 1, here, :]
+                before = (
+                    jnp.where(
+                        even_cell,
+                        beside_cross_ref[component, here, :],
+                        beside_mate_ref[component, here, :],
+                    )
+                    if cell == 0
+                    else melt_ref[component, cell - 1, here, :]
+                )
                 after = (
-                    right_ref[component, here, :]
+                    jnp.where(
+                        even_cell,
+                        beside_mate_ref[component, here, :],
+                        beside_cross_ref[component, here, :],
+                    )
                     if cell == cells - 1
                     else melt_ref[component, cell + 1, here, :]
                 )
@@ -308,21 +375,36 @@
                 out_ref[component, cell, here, :] = rate
 
 
-def ring(source, axis, step):
+def swap(source, axis, mask):
+    return lax.ppermute(source, axis, [(i, i ^ mask) for i in range(lax.axis_size(axis))])
+
+
+def swap_across(source, axis):
     count = lax.axis_size(axis)
-    return lax.ppermute(source, axis, [(i, (i + step) % count) for i in range(count)])
-
-
-def exchange(source, axis):
+    pairs = [(i, (i + 1) % count) for i in range(1, count, 2)]
+    return lax.ppermute(source, axis, pairs + [(j, i) for i, j in pairs])
+
+
+def exchange(message, rows, axis):
     count = lax.axis_size(axis)
-    if count & (count - 1):
-        return [source] + [ring(source, axis, -k) for k in range(1, count)]
-    return [source] + [
-        lax.ppermute(source, axis, [(i, i ^ k) for i in range(count)]) for k in range(1, count)
-    ]
-
-
-def call(kernel, outs, scratch=(), specs=None):
+    mask = 1
+    while True:
+        other = swap(message, axis, mask)
+        mask = 2 * mask
+        if mask == count:
+            return message, other
+        message = jnp.concatenate([message[:rows] + other[:rows], message[rows:], other[rows:]])
+
+
+def fenced(place, part, *arrays):
+    def no_part(*arrays):
+        shapes = jax.eval_shape(part, *arrays)
+        return jax.tree.map(lambda leaf: jnp.zeros(leaf.shape, leaf.dtype), shapes)
+
+    return lax.cond(place[0] < lax.axis_size("sa"), part, no_part, *arrays)
+
+
+def call(kernel, outs, specs, scratch=(), flops=1):
     return pl.pallas_call(
         kernel,
         out_shape=outs,
@@ -330,6 +412,7 @@
         out_specs=jax.tree.map(lambda _: VMEM, outs),
         scratch_shapes=scratch,
         compiler_params=pltpu.CompilerParams(vmem_limit_bytes=24 * 1024 * 1024),
+        cost_estimate=pl.CostEstimate(flops=flops, bytes_accessed=1, transcendentals=0),
     )
 
 
@@ -339,50 +422,61 @@
 
 def on_device(gas, melt, surface_mask, melt_level):
     _, cells, rows, span = gas.shape
-    _, _, depth, width = melt.shape
+    components, _, depth, width = melt.shape
     devices = lax.axis_size("sa")
+    assert devices & (devices - 1) == 0 and devices > 1
     span_cells = float(span * devices)
-    gas_left = ring(gas, "gx", 1)
-    gas_right = ring(gas, "gx", -1)
-    edges = call(pack_gas, array(SUB, LANES), specs=[VMEM])(gas)
-    edges = jnp.stack([ring(edges, "gx", 1), edges, ring(edges, "gx", -1)])
-    below = ring(edges, "sa", 1)
-    above = ring(edges, "sa", -1)
-    first, last, depth_rows = call(
-        pack_melt,
-        (array(2, depth, width), array(2, depth, width), array(2, 2 * cells, width)),
-        specs=[VMEM],
-    )(melt)
-    upper = ring(depth_rows[1], "sa", 1)
-    lower = ring(depth_rows[0], "sa", -1)
-    gas_left, gas_right, first, last = lax.optimization_barrier((gas_left, gas_right, first, last))
-    melt_left = ring(last, "gx", 1)
-    melt_right = ring(first, "gx", -1)
-    wide = span + LANES
-    used = rows + 3 * cells * (span // LANES)
-    message_rows = -(-used // SUB) * SUB
-    base, eddy, message = call(
-        germano,
-        (array(4, cells, rows, span), array(4, cells, rows, span), array(message_rows, LANES)),
-        scratch=(
-            pltpu.VMEM((cells + 4, 4, rows + 2 * SUB, wide), jnp.float32),
-            pltpu.VMEM((cells + 2, 3, rows + 2 * SUB, wide), jnp.float32),
-            pltpu.VMEM((cells, rows, span), jnp.float32),
-        ),
-        specs=[VMEM] * 5,
-    )(gas, gas_left, gas_right, below, above)
-    messages = exchange(message, "sa")
+    place = jnp.stack([lax.axis_index("sa"), lax.axis_index("gx")]).astype(jnp.int32)
+    even = place[0] % 2 == 0
+    gas_mate, gas_cross = swap(gas, "gx", 1), swap_across(gas, "gx")
+    side = array(SUB + components * cells * width // LANES, LANES)
+    mate, cross = call(pack_sides, (side, side), [SMEM, VMEM, VMEM])(place, gas, melt)
+    mate, cross = swap(mate, "sa", 1), swap_across(cross, "sa")
+    late = lax.broadcasted_iota(jnp.int32, (SUB, LANES), 1) % EDGE >= EDGE // 2
+    halo = jnp.where(late == even, cross[:SUB], mate[:SUB])
+    halo_mate, halo_cross = swap(halo, "gx", 1), swap_across(halo, "gx")
+    part = array(components, depth, width)
+    beside_mate, beside_cross = call(pack_melt, (part, part), [SMEM, VMEM, ANY])(place, melt, halo)
+    beside_mate, beside_cross = swap(beside_mate, "gx", 1), swap_across(beside_cross, "gx")
+
+    def gas_part(*arrays):
+        wide = span + LANES
+        used = rows + 3 * cells * (span // LANES)
+        message_rows = -(-used // SUB) * SUB
+        base, eddy, message = call(
+            germano,
+            (array(4, cells, rows, span), array(4, cells, rows, span), array(message_rows, LANES)),
+            [SMEM] + [VMEM] * 6,
+            scratch=(
+                pltpu.VMEM((cells + 4, 4, rows + 2 * SUB, wide), jnp.float32),
+                pltpu.VMEM((cells + 2, 3, rows + 2 * SUB, wide), jnp.float32),
+                pltpu.VMEM((cells, rows, span), jnp.float32),
+            ),
+        )(*arrays)
+        return base, eddy, *exchange(message, rows, "sa")
+
+    base, eddy, mine, theirs = fenced(
+        place, gas_part, place, gas, gas_mate, gas_cross, halo, halo_mate, halo_cross
+    )
     gas_rate = call(
-        functools.partial(finish_gas, span_cells, devices),
-        array(4, cells, rows, span),
-        specs=[VMEM] * (2 + devices),
-    )(base, eddy, *messages)
-    place = jnp.stack([lax.axis_index("sa"), devices]).astype(jnp.int32)
+        functools.partial(finish_gas, span_cells), array(4, cells, rows, span), [VMEM] * 4, flops=4000000000
+    )(mine, theirs, base, eddy)
     melt_rate = call(
         functools.partial(finish_melt, span_cells, devices, rows, span),
-        array(2, cells, depth, width),
-        specs=[pl.BlockSpec(memory_space=pltpu.SMEM)] + [VMEM] * (7 + devices),
-    )(place, melt, melt_left, melt_right, upper, lower, surface_mask, melt_level, *messages)
+        array(components, cells, depth, width),
+        [SMEM] + [VMEM] * 9,
+    )(
+        place,
+        mine,
+        theirs,
+        melt,
+        beside_mate,
+        beside_cross,
+        mate,
+        cross,
+        surface_mask,
+        melt_level,
+    )
     return (gas_rate, melt_rate)
 
 

time: 43.6 us -> 36.2 us (0.83)
  the two profiles are of different devices: /device:TPU:0 before, /device:TPU:20 now
where the time goes in v2:
time: 36.2 us; the launch traced here: 35.8 us
  waiting for transfers between devices  12.8 us (35%)
  starting transfers between devices  10.5 us (29%)
  Pallas kernels  10.1 us (28%)
  local copies, waits for them, and re-layouts  1.06 us (3%)
  other arithmetic  0.7 us (2%)
  between operations  0.68 us (2%)
    ppermute x6, waiting for transfers between devices, swap(): lax.ppermute(source, axis, [(i, i ^ mask) for i in range(lax.axis_size(ax...  10.3 us
    ppermute x6, starting transfers between devices, swap(): lax.ppermute(source, axis, [(i, i ^ mask) for i in range(lax.axis_size(ax...  5.28 us
    ppermute x4, starting transfers between devices, swap_across(): return lax.ppermute(source, axis, pairs + [(j, i) for i, j in pairs])  5.21 us
    pallas_call x1, Pallas kernels, gas_part(): call(germano, (array(4, cells, rows, span), array(4, cells, rows, span),...  4.64 us
    ppermute x4, waiting for transfers between devices, swap_across(): return lax.ppermute(source, axis, pairs + [(j, i) for i, j in pairs])  2.56 us
    pallas_call x1, Pallas kernels, on_device(): call(functools.partial(finish_melt, span_cells, devices, rows, span), arr...  2.02 us
    pallas_call x1, Pallas kernels, on_device(): call(functools.partial(finish_gas, span_cells), array(4, cells, rows, spa...  1.67 us
    pallas_call x1, Pallas kernels, on_device(): call(pack_sides, (side, side), [SMEM, VMEM, VMEM])(place, gas, melt)  1.15 us
  transfers between devices with their start and end apart: 10, of which 5 were waited for; matrix products, arithmetic and copies ran while one was open for 2% of the time, Pallas kernels for 22%

profile of v2, /device:TPU:20, one launch (start us, length us, event | category | flops | bytes accessed | tf_op | source)
XLA Modules:
  0.0 35.8 jit_solution(15480361419373634880)
XLA Ops:
  0.6 1.6 %collective-permute-start.3 = (f32[4,2,32,256]{3,2,1,0:T(8,128)}, f32[4,2,32,256]{3,2,1,0:T(8,128)S(1)}, u32[]{:S(2)}, u32[]{:S(2)}) collective-permute-start(f32[4,2,32,256]{3,2,1,0:T(8,128)} %gas_ref.1), channel_id=1, source_target_pairs={{4,8},{12,16},{20,24},{28,0},{8,4},{16,12},{24,20},{0,28},{5,9},{1... | collective-permute-start | bytes 786440 | tf_op jit(solution)/shard_map/ppermute | solution.py:385
  2.2 0.4 %collective-permute-start.2 = (f32[4,2,32,256]{3,2,1,0:T(8,128)}, f32[4,2,32,256]{3,2,1,0:T(8,128)S(1)}, u32[]{:S(2)}, u32[]{:S(2)}) collective-permute-start(f32[4,2,32,256]{3,2,1,0:T(8,128)} %gas_ref.1), channel_id=1, source_target_pairs={{0,4},{4,0},{8,12},{12,8},{16,20},{20,16},{24,28},{28,24},{1,5},{5... | collective-permute-start | bytes 786440 | tf_op jit(solution)/shard_map/ppermute | solution.py:379
  2.6 0.1 pad_add_fusion.place_ref
  2.7 1.0 %copy-done = f32[2,2,32,1024]{3,2,1,0:T(8,128)S(1)} copy-done((f32[2,2,32,1024]{3,2,1,0:T(8,128)S(1)}, f32[2,2,32,1024]{3,2,1,0:T(8,128)}, u32[]{:S(2)}) %copy-start) | copy-done | bytes 524312
  3.7 1.1 %shard_map.59 = (f32[40,128]{1,0:T(8,128)S(1)}, f32[40,128]{1,0:T(8,128)S(1)}) custom-call(s32[2]{0:T(128)S(1)} %pad_add_fusion.place_ref, f32[4,2,32,256]{3,2,1,0:T(8,128)} %gas_ref.1, f32[2,2,32,1024]{3,2,1,0:T(8,128)S(1)} %copy-done), custom_call_target="tpu_custom_call" | custom-call | flops 1 | bytes 1 | tf_op jit(solution)/shard_map/pallas_call | solution.py:433
  4.9 0.4 %collective-permute-start.4 = (f32[40,128]{1,0:T(8,128)S(1)}, f32[40,128]{1,0:T(8,128)S(1)}, u32[]{:S(2)}, u32[]{:S(2)}) collective-permute-start(f32[40,128]{1,0:T(8,128)S(1)} %get-tuple-element.34), channel_id=1, source_target_pairs={{1,2},{3,0},{2,1},{0,3},{5,6},{7,4},{6,5},{4,7},{9,10},{11,8},{10,... | collective-permute-start | bytes 61448 | tf_op jit(solution)/shard_map/ppermute | solution.py:385
  5.3 1.2 %collective-permute-start.5 = (f32[40,128]{1,0:T(8,128)S(1)}, f32[40,128]{1,0:T(8,128)S(1)}, u32[]{:S(2)}, u32[]{:S(2)}) collective-permute-start(f32[40,128]{1,0:T(8,128)S(1)} %get-tuple-element.35), channel_id=1, source_target_pairs={{0,1},{1,0},{2,3},{3,2},{4,5},{5,4},{6,7},{7,6},{8,9},{9,8},{10,11... | collective-permute-start | bytes 61448 | tf_op jit(solution)/shard_map/ppermute | solution.py:379
  6.6 1.8 %collective-permute-done.4.cross_ref = f32[40,128]{1,0:T(8,128)S(1)} collective-permute-done((f32[40,128]{1,0:T(8,128)S(1)}, f32[40,128]{1,0:T(8,128)S(1)}, u32[]{:S(2)}, u32[]{:S(2)}) %collective-permute-start.4) | collective-permute-done | bytes 20512 | tf_op jit(solution)/shard_map/ppermute | solution.py:385
  8.3 0.0 collective-permute-done.5.mate_ref
  8.3 1.2 %collective-permute-start.7 = (f32[8,128]{1,0:T(8,128)S(1)}, f32[8,128]{1,0:T(8,128)S(1)}, u32[]{:S(2)}, u32[]{:S(2)}) collective-permute-start(f32[8,128]{1,0:T(8,128)S(1)} %slice_select_fusion.after_ref), channel_id=1, source_target_pairs={{4,8},{12,16},{20,24},{28,0},{8,4},{16,12},{24,20},{0,28},{5,9},{1... | collective-permute-start | bytes 12296 | tf_op jit(solution)/shard_map/ppermute | solution.py:385
  9.5 0.8 %collective-permute-start.6 = (f32[8,128]{1,0:T(8,128)S(1)}, f32[8,128]{1,0:T(8,128)S(1)}, u32[]{:S(2)}, u32[]{:S(2)}) collective-permute-start(f32[8,128]{1,0:T(8,128)S(1)} %slice_select_fusion.after_ref), channel_id=1, source_target_pairs={{0,4},{4,0},{8,12},{12,8},{16,20},{20,16},{24,28},{28,24},{1,5},{5... | collective-permute-start | bytes 12296 | tf_op jit(solution)/shard_map/ppermute | solution.py:379
  10.3 0.0 copy-done.1
  10.3 0.6 %shard_map.61 = (f32[2,32,1024]{2,1,0:T(8,128)S(1)}, f32[2,32,1024]{2,1,0:T(8,128)S(1)}) custom-call(s32[2]{0:T(128)S(1)} %pad_add_fusion.place_ref, f32[2,2,32,1024]{3,2,1,0:T(8,128)S(1)} %copy-done.1, f32[8,128]{1,0:T(8,128)S(1)} %slice_select_fusion.after_ref), custom_call_target="tpu_custom_call" | custom-call | flops 1 | bytes 1 | tf_op jit(solution)/shard_map/pallas_call | solution.py:439
  10.9 1.3 %collective-permute-start.8 = (f32[2,32,1024]{2,1,0:T(8,128)S(1)}, f32[2,32,1024]{2,1,0:T(8,128)S(1)}, u32[]{:S(2)}, u32[]{:S(2)}) collective-permute-start(f32[2,32,1024]{2,1,0:T(8,128)S(1)} %get-tuple-element.40), channel_id=1, source_target_pairs={{0,4},{4,0},{8,12},{12,8},{16,20},{20,16},{24,28},{28,24},{1,5},{5... | collective-permute-start | bytes 786440 | tf_op jit(solution)/shard_map/ppermute | solution.py:379
  12.2 0.8 %collective-permute-done.7 = f32[8,128]{1,0:T(8,128)S(1)} collective-permute-done((f32[8,128]{1,0:T(8,128)S(1)}, f32[8,128]{1,0:T(8,128)S(1)}, u32[]{:S(2)}, u32[]{:S(2)}) %collective-permute-start.7) | collective-permute-done | bytes 4128 | tf_op jit(solution)/shard_map/ppermute | solution.py:385
  13.0 2.0 %collective-permute-start.9 = (f32[2,32,1024]{2,1,0:T(8,128)S(1)}, f32[2,32,1024]{2,1,0:T(8,128)S(1)}, u32[]{:S(2)}, u32[]{:S(2)}) collective-permute-start(f32[2,32,1024]{2,1,0:T(8,128)S(1)} %get-tuple-element.41), channel_id=1, source_target_pairs={{4,8},{12,16},{20,24},{28,0},{8,4},{16,12},{24,20},{0,28},{5,9},{1... | collective-permute-start | bytes 786440 | tf_op jit(solution)/shard_map/ppermute | solution.py:385
  15.0 6.3 %collective-permute-done.6 = f32[8,128]{1,0:T(8,128)S(1)} collective-permute-done((f32[8,128]{1,0:T(8,128)S(1)}, f32[8,128]{1,0:T(8,128)S(1)}, u32[]{:S(2)}, u32[]{:S(2)}) %collective-permute-start.6) | collective-permute-done | bytes 4128 | tf_op jit(solution)/shard_map/ppermute | solution.py:379
  21.4 0.0 collective-permute-done.3
  21.4 0.0 collective-permute-done.2
  21.4 0.0 copy-done.4
  21.4 10.8 %conditional.1 = (f32[4,2,32,256]{3,2,1,0:T(8,128)S(1)}, f32[4,2,32,256]{3,2,1,0:T(8,128)S(1)}, f32[64,128]{1,0:T(8,128)}, f32[64,128]{1,0:T(8,128)}) conditional(s32[]{:T(128)} %convert_element_type.3, () %tuple.16, (s32[2]{0:T(128)S(1)}, f32[4,2,32,256]{3,2,1,0:T(8,128)S(1)}, f32[4,2,32,256]{3,2,1,0:T(8,128)S(1)}, f32[4,2,32,256]{3,2,1,0:T(8,128)S(1)}, ...), branch_computations={%region_0.1_spmd, %region_1.2_spmd} | conditional | flops 20481 | bytes 589872 | solution.py:404
  21.4 4.6 %branch_1_fun.1 = (f32[4,2,32,256]{3,2,1,0:T(8,128)S(1)}, f32[4,2,32,256]{3,2,1,0:T(8,128)S(1)}, f32[48,128]{1,0:T(8,128)S(1)}) custom-call(s32[2]{0:T(128)S(1)} %get-tuple-element.14.place_ref, f32[4,2,32,256]{3,2,1,0:T(8,128)S(1)} %get-tuple-element.15.own_ref, f32[4,2,32,256]{3,2,1,0:T(8,128)S(1)} %get-tuple-element.16.mate_ref, ...), custom_call_target="tpu_custom_call" | custom-call | flops 1 | bytes 1 | tf_op jit(solution)/shard_map/cond/branch_1_fun/pallas_call | solution.py:446
  26.0 0.1 collective-permute-start
  26.1 1.2 %collective-permute-done = f32[48,128]{1,0:T(8,128)S(1)} collective-permute-done((f32[48,128]{1,0:T(8,128)S(1)}, f32[48,128]{1,0:T(8,128)S(1)}, u32[]{:S(2)}, u32[]{:S(2)}) %collective-permute-start) | collective-permute-done | bytes 24608 | tf_op jit(solution)/shard_map/cond/branch_1_fun/ppermute | solution.py:379
  27.3 0.6 %pad_maximum_fusion = f32[64,128]{1,0:T(8,128)} fusion(f32[16,128]{1,0:T(8,128)S(1)} %slice.21, f32[16,128]{1,0:T(8,128)S(1)} %slice.14, f32[32,128]{1,0:T(8,128)S(1)} %slice_add_fusion), kind=kLoop, calls=%fused_computation | loop fusion | flops 16384 | bytes 65536 | tf_op jit(solution)/shard_map/cond/branch_1_fun/concatenate | solution.py:396
  27.9 1.5 %collective-permute-start.1 = (f32[64,128]{1,0:T(8,128)}, f32[64,128]{1,0:T(8,128)}, u32[]{:S(2)}, u32[]{:S(2)}) collective-permute-start(f32[64,128]{1,0:T(8,128)} %pad_maximum_fusion), channel_id=1, source_target_pairs={{0,2},{1,3},{2,0},{3,1},{4,6},{5,7},{6,4},{7,5},{8,10},{9,11},{10,... | collective-permute-start | bytes 98312 | tf_op jit(solution)/shard_map/cond/branch_1_fun/ppermute | solution.py:379
  29.4 2.7 %collective-permute-done.1 = f32[64,128]{1,0:T(8,128)} collective-permute-done((f32[64,128]{1,0:T(8,128)}, f32[64,128]{1,0:T(8,128)}, u32[]{:S(2)}, u32[]{:S(2)}) %collective-permute-start.1) | collective-permute-done | bytes 32800 | tf_op jit(solution)/shard_map/cond/branch_1_fun/ppermute | solution.py:379
  32.1 1.7 %shard_map.60 = f32[4,2,32,256]{3,2,1,0:T(8,128)} custom-call(f32[64,128]{1,0:T(8,128)} %get-tuple-element.36.mine_ref, f32[64,128]{1,0:T(8,128)} %get-tuple-element.37.theirs_ref, f32[4,2,32,256]{3,2,1,0:T(8,128)S(1)} %get-tuple-element.38.base_ref, f32[4,2,32,256]{3,2,1,0:T(8,128)S(1)} %get-tuple-element.39.eddy_ref), custom_call_target="tpu_custom_call" | custom-call | flops 4000000000 | bytes 1 | tf_op jit(solution)/shard_map/pallas_call | solution.py:461
  33.8 0.0 collective-permute-done.8.beside_mate_ref
  33.8 0.0 collective-permute-done.9.beside_cross_ref
  33.8 0.0 copy-done.2
  33.8 2.0 %shard_map.62 = f32[2,2,32,1024]{3,2,1,0:T(8,128)} custom-call(s32[2]{0:T(128)S(1)} %pad_add_fusion.place_ref, f32[64,128]{1,0:T(8,128)} %get-tuple-element.36.mine_ref, f32[64,128]{1,0:T(8,128)} %get-tuple-element.37.theirs_ref, f32[2,2,32,1024]{3,2,1,0:T(8,128)S(1)} %copy-done.1, f32[2,32,1024]{2,1,0:T(8,128)S(1)} %collective-permute-done.8.beside_mate_ref, ...), custom_call_target="tpu_custom_call" | custom-call | flops 1 | bytes 1 | tf_op jit(solution)/shard_map/pallas_call | solution.py:464
  (12 shorter events, 0.0 us)
Async XLA Ops:
  0.6 20.7 %collective-permute-start.3 = (f32[4,2,32,256]{3,2,1,0:T(8,128)}, f32[4,2,32,256]{3,2,1,0:T(8,128)S(1)}, u32[]{:S(2)}, u32[]{:S(2)}) collective-permute-start(f32[4,2,32,256]{3,2,1,0:T(8,128)} %gas_ref.1), channel_id=1, source_target_pairs={{4,8},{12,16},{20,24},{28,0},{8,4},{16,12},{24,20},{0,28},{5,9},{1... | collective-permute-start | bytes 786440 | tf_op jit(solution)/shard_map/ppermute | solution.py:385
  2.2 19.1 %collective-permute-start.2 = (f32[4,2,32,256]{3,2,1,0:T(8,128)}, f32[4,2,32,256]{3,2,1,0:T(8,128)S(1)}, u32[]{:S(2)}, u32[]{:S(2)}) collective-permute-start(f32[4,2,32,256]{3,2,1,0:T(8,128)} %gas_ref.1), channel_id=1, source_target_pairs={{0,4},{4,0},{8,12},{12,8},{16,20},{20,16},{24,28},{28,24},{1,5},{5... | collective-permute-start | bytes 786440 | tf_op jit(solution)/shard_map/ppermute | solution.py:379
  2.7 1.0 %copy-start = (f32[2,2,32,1024]{3,2,1,0:T(8,128)S(1)}, f32[2,2,32,1024]{3,2,1,0:T(8,128)}, u32[]{:S(2)}) copy-start(f32[2,2,32,1024]{3,2,1,0:T(8,128)} %melt_ref.5) | copy-start | bytes 1572868
  3.7 6.6 %copy-start.1 = (f32[2,2,32,1024]{3,2,1,0:T(8,128)S(1)}, f32[2,2,32,1024]{3,2,1,0:T(8,128)}, u32[]{:S(2)}) copy-start(f32[2,2,32,1024]{3,2,1,0:T(8,128)} %melt_ref.5) | copy-start | bytes 1572868
  4.9 3.4 %collective-permute-start.4 = (f32[40,128]{1,0:T(8,128)S(1)}, f32[40,128]{1,0:T(8,128)S(1)}, u32[]{:S(2)}, u32[]{:S(2)}) collective-permute-start(f32[40,128]{1,0:T(8,128)S(1)} %get-tuple-element.34), channel_id=1, source_target_pairs={{1,2},{3,0},{2,1},{0,3},{5,6},{7,4},{6,5},{4,7},{9,10},{11,8},{10,... | collective-permute-start | bytes 61448 | tf_op jit(solution)/shard_map/ppermute | solution.py:385
  5.3 3.0 %collective-permute-start.5 = (f32[40,128]{1,0:T(8,128)S(1)}, f32[40,128]{1,0:T(8,128)S(1)}, u32[]{:S(2)}, u32[]{:S(2)}) collective-permute-start(f32[40,128]{1,0:T(8,128)S(1)} %get-tuple-element.35), channel_id=1, source_target_pairs={{0,1},{1,0},{2,3},{3,2},{4,5},{5,4},{6,7},{7,6},{8,9},{9,8},{10,11... | collective-permute-start | bytes 61448 | tf_op jit(solution)/shard_map/ppermute | solution.py:379
  8.3 4.7 %collective-permute-start.7 = (f32[8,128]{1,0:T(8,128)S(1)}, f32[8,128]{1,0:T(8,128)S(1)}, u32[]{:S(2)}, u32[]{:S(2)}) collective-permute-start(f32[8,128]{1,0:T(8,128)S(1)} %slice_select_fusion.after_ref), channel_id=1, source_target_pairs={{4,8},{12,16},{20,24},{28,0},{8,4},{16,12},{24,20},{0,28},{5,9},{1... | collective-permute-start | bytes 12296 | tf_op jit(solution)/shard_map/ppermute | solution.py:385
  9.5 11.8 %collective-permute-start.6 = (f32[8,128]{1,0:T(8,128)S(1)}, f32[8,128]{1,0:T(8,128)S(1)}, u32[]{:S(2)}, u32[]{:S(2)}) collective-permute-start(f32[8,128]{1,0:T(8,128)S(1)} %slice_select_fusion.after_ref), channel_id=1, source_target_pairs={{0,4},{4,0},{8,12},{12,8},{16,20},{20,16},{24,28},{28,24},{1,5},{5... | collective-permute-start | bytes 12296 | tf_op jit(solution)/shard_map/ppermute | solution.py:379
  10.3 11.0 %copy-start.4 = (f32[4,2,32,256]{3,2,1,0:T(8,128)S(1)}, f32[4,2,32,256]{3,2,1,0:T(8,128)}, u32[]{:S(2)}) copy-start(f32[4,2,32,256]{3,2,1,0:T(8,128)} %gas_ref.1) | copy-start | bytes 786436
  10.9 22.9 %collective-permute-start.8 = (f32[2,32,1024]{2,1,0:T(8,128)S(1)}, f32[2,32,1024]{2,1,0:T(8,128)S(1)}, u32[]{:S(2)}, u32[]{:S(2)}) collective-permute-start(f32[2,32,1024]{2,1,0:T(8,128)S(1)} %get-tuple-element.40), channel_id=1, source_target_pairs={{0,4},{4,0},{8,12},{12,8},{16,20},{20,16},{24,28},{28,24},{1,5},{5... | collective-permute-start | bytes 786440 | tf_op jit(solution)/shard_map/ppermute | solution.py:379
  13.0 20.8 %collective-permute-start.9 = (f32[2,32,1024]{2,1,0:T(8,128)S(1)}, f32[2,32,1024]{2,1,0:T(8,128)S(1)}, u32[]{:S(2)}, u32[]{:S(2)}) collective-permute-start(f32[2,32,1024]{2,1,0:T(8,128)S(1)} %get-tuple-element.41), channel_id=1, source_target_pairs={{4,8},{12,16},{20,24},{28,0},{8,4},{16,12},{24,20},{0,28},{5,9},{1... | collective-permute-start | bytes 786440 | tf_op jit(solution)/shard_map/ppermute | solution.py:385
  26.0 1.3 %collective-permute-start = (f32[48,128]{1,0:T(8,128)S(1)}, f32[48,128]{1,0:T(8,128)S(1)}, u32[]{:S(2)}, u32[]{:S(2)}) collective-permute-start(f32[48,128]{1,0:T(8,128)S(1)} %get-tuple-element.23), channel_id=1, source_target_pairs={{0,1},{1,0},{2,3},{3,2},{4,5},{5,4},{6,7},{7,6},{8,9},{9,8},{10,11... | collective-permute-start | bytes 73736 | tf_op jit(solution)/shard_map/cond/branch_1_fun/ppermute | solution.py:379
  27.9 4.2 %collective-permute-start.1 = (f32[64,128]{1,0:T(8,128)}, f32[64,128]{1,0:T(8,128)}, u32[]{:S(2)}, u32[]{:S(2)}) collective-permute-start(f32[64,128]{1,0:T(8,128)} %pad_maximum_fusion), channel_id=1, source_target_pairs={{0,2},{1,3},{2,0},{3,1},{4,6},{5,7},{6,4},{7,5},{8,10},{9,11},{10,... | collective-permute-start | bytes 98312 | tf_op jit(solution)/shard_map/cond/branch_1_fun/ppermute | solution.py:379
  32.1 1.7 %copy-start.2 = (s32[2,1024]{1,0:T(2,128)S(1)}, s32[2,1024]{1,0:T(2,128)}, u32[]{:S(2)}) copy-start(s32[2,1024]{1,0:T(2,128)} %mask_ref.1) | copy-start | bytes 24580
  32.1 1.7 %copy-start.3 = (s32[2,1024]{1,0:T(2,128)S(1)}, s32[2,1024]{1,0:T(2,128)}, u32[]{:S(2)}) copy-start(s32[2,1024]{1,0:T(2,128)} %level_ref.1) | copy-start | bytes 24580

commit v3 on v2

--- a/solution.py
+++ b/solution.py
@@ -21,6 +21,7 @@
 VMEM = pl.BlockSpec(memory_space=pltpu.VMEM)
 SMEM = pl.BlockSpec(memory_space=pltpu.SMEM)
 ANY = pl.BlockSpec(memory_space=pl.ANY)
+HBM = pl.BlockSpec(memory_space=pltpu.HBM)
 
 
 def shift_lanes(source, amount):
@@ -32,9 +33,16 @@
     return ((row_block * cells + cell) * 4 + component) * EDGE
 
 
-def pack_sides(place_ref, gas_ref, melt_ref, mate_ref, cross_ref):
+def pack_sides(place_ref, gas_hbm, melt_hbm, mate_ref, cross_ref, gas_ref, ends_ref, sems):
     _, cells, rows, span = gas_ref.shape
-    components, _, depth, width = melt_ref.shape
+    components, _, depth, width = melt_hbm.shape
+    copies = [pltpu.make_async_copy(gas_hbm, gas_ref, sems.at[0])]
+    for end, start in enumerate((0, depth - SUB)):
+        levels = melt_hbm.at[:, :, pl.ds(start, SUB), :]
+        copies.append(pltpu.make_async_copy(levels, ends_ref.at[end], sems.at[end + 1]))
+    for copy in copies:
+        copy.start()
+    copies[0].wait()
     lane = lax.broadcasted_iota(jnp.int32, (SUB, LANES), 1)
     tile = jnp.zeros((SUB, LANES), jnp.float32)
     for block in range(rows // SUB):
@@ -51,10 +59,12 @@
     mate_ref[0:SUB, :] = tile
     cross_ref[0:SUB, :] = tile
     even = place_ref[0] % 2 == 0
+    for copy in copies[1:]:
+        copy.wait()
     for component in range(components):
         for cell in range(cells):
-            first = melt_ref[component, cell, 0:1, :]
-            last = melt_ref[component, cell, depth - 1 : depth, :]
+            first = ends_ref[0, component, cell, 0:1, :]
+            last = ends_ref[1, component, cell, SUB - 1 : SUB, :]
             mate = jnp.where(even, last, first)
             cross = jnp.where(even, first, last)
             for t in range(width // LANES):
@@ -79,15 +89,14 @@
 
 
 def binomial(source):
-    pair = source + shift_lanes(source, 1)
-    return pair + shift_lanes(pair, -1)
+    return (shift_lanes(source, 1) + shift_lanes(source, -1)) + 2.0 * source
 
 
 def germano(
     place_ref,
     own_ref,
+    cross_ref,
     mate_ref,
-    cross_ref,
     halo_ref,
     halo_mate_ref,
     halo_cross_ref,
@@ -219,7 +228,8 @@
             ]
             pair = [values[x] + values[x + 1] for x in range(cells + 1)]
             products.append([binomial(pair[x] + pair[x + 1])[:, :span] for x in range(cells)])
-        tile = jnp.zeros((SUB, LANES), jnp.float32)
+        tile = carry
+        first = block * 2 * cells
         for cell in range(cells):
             points = [around(coarse, cell + 1, c, block) for c in range(3)]
             gradient = [[(p[1 + j][1] - p[1 + j][0])[:, :span] for j in range(3)] for p in points]
@@ -237,13 +247,13 @@
                     off = off + model * model
             denominator = diagonal + 0.5 * off
             total = jnp.sum(numerator, axis=1, keepdims=True) * (1.0 / 512.0)
-            tile = jnp.where(column == cell, total, tile)
+            tile = jnp.where(column == first + cell, total, tile)
             total = jnp.sum(denominator, axis=1, keepdims=True) * (1.0 / 1024.0)
-            tile = jnp.where(column == cells + cell, total, tile)
-        sums_ref[out_rows, :] = tile
-        return carry
-
-    lax.fori_loop(0, rows // SUB, rate_block, 0)
+            tile = jnp.where(column == first + cells + cell, total, tile)
+        return tile
+
+    none = jnp.zeros((SUB, LANES), jnp.float32)
+    sums_ref[0:SUB, :] = lax.fori_loop(0, rows // SUB, rate_block, none)
     tiles = span // LANES
     for cell in range(cells):
         planes = (
@@ -253,11 +263,8 @@
         )
         for p, plane in enumerate(planes):
             for t in range(tiles):
-                at = rows + (p * cells + cell) * tiles + t
+                at = SUB + (p * cells + cell) * tiles + t
                 sums_ref[at : at + 1, :] = plane[:, t * LANES : (t + 1) * LANES]
-    used = rows + 3 * cells * tiles
-    if used < sums_ref.shape[0]:
-        sums_ref[used:, :] = jnp.zeros((sums_ref.shape[0] - used, LANES), jnp.float32)
 
 
 def lilly(total, cells, span_cells):
@@ -266,23 +273,62 @@
     return -mean_numerator / (2.0 * (mean_denominator + epsilon))
 
 
+def merge_messages(mine_ref, theirs_ref, out_ref):
+    held = mine_ref.shape[0]
+    out_ref[0:SUB, :] = mine_ref[0:SUB, :] + theirs_ref[0:SUB, :]
+    out_ref[SUB:held, :] = mine_ref[SUB:held, :]
+    out_ref[held : 2 * held - SUB, :] = theirs_ref[SUB:held, :]
+
+
 def finish_gas(span_cells, mine_ref, theirs_ref, base_ref, eddy_ref, out_ref):
     _, cells, rows, _ = base_ref.shape
-    coefficient = lilly(mine_ref[0:rows, :] + theirs_ref[0:rows, :], cells, span_cells)
+    coefficient = lilly(mine_ref[0:SUB, :] + theirs_ref[0:SUB, :], cells, span_cells)
     for cell in range(cells):
-        factor = coefficient[:, cell : cell + 1]
-        for component in range(4):
-            out_ref[component, cell] = base_ref[component, cell] + factor * eddy_ref[component, cell]
+        for block in range(rows // SUB):
+            at = block * 2 * cells + cell
+            factor = coefficient[:, at : at + 1]
+            here = slice(SUB * block, SUB * (block + 1))
+            for component in range(4):
+                out_ref[component, cell, here, :] = (
+                    base_ref[component, cell, here, :] + factor * eddy_ref[component, cell, here, :]
+                )
+
+
+def wall_fluxes(span_cells, devices, span, mine_ref, theirs_ref, wall_ref):
+    cells = wall_ref.shape[0] // 2
+    coefficient = lilly(mine_ref[0:SUB, :] + theirs_ref[0:SUB, :], cells, span_cells)
+    tiles = span // LANES
+    held = (mine_ref.shape[0] - SUB) // (devices // 2)
+    for cell in range(cells):
+        factor = coefficient[0:1, cell : cell + 1]
+        for device in range(devices):
+            ref = mine_ref if device < devices // 2 else theirs_ref
+            start = SUB + device % (devices // 2) * held
+            for t in range(tiles):
+                strength, speed, heat = (
+                    ref[at : at + 1, :]
+                    for at in (start + (p * cells + cell) * tiles + t for p in range(3))
+                )
+                eddy = factor * strength
+                place = pl.ds((device * tiles + t) * LANES, LANES)
+                wall_ref[cell : cell + 1, place] = (gas_viscosity + eddy) * 2.0 * speed
+                wall_ref[cells + cell : cells + cell + 1, place] = (
+                    (gas_diffusivity + eddy / turbulent_prandtl) * 2.0 * heat
+                )
+
+
+def surface_flux(place_ref, wall_ref, mask_ref, flux_ref):
+    cells = mask_ref.shape[0]
+    top = place_ref[0] == 0
+    shear = mask_ref[...].astype(jnp.float32) * wall_ref[0:cells, :]
+    flux_ref[0:cells, :] = jnp.where(top, shear, 0.0)
+    flux_ref[cells:, :] = jnp.where(top, wall_ref[cells:, :], 0.0)
 
 
 def finish_melt(
-    span_cells,
     devices,
-    rows,
-    span,
     place_ref,
-    mine_ref,
-    theirs_ref,
+    flux_ref,
     melt_ref,
     beside_mate_ref,
     beside_cross_ref,
@@ -290,15 +336,15 @@
     cross_ref,
     mask_ref,
     level_ref,
+    out_hbm,
     out_ref,
+    sems,
 ):
     components, cells, depth, width = melt_ref.shape
     position = place_ref[0]
     even = position % 2 == 0
     even_cell = place_ref[1] % 2 == 0
-    coefficient = lilly(mine_ref[0:SUB, :] + theirs_ref[0:SUB, :], cells, span_cells)
-    tiles = span // LANES
-    held = (mine_ref.shape[0] - rows) // (devices // 2)
+    copies = []
     level_id = lax.broadcasted_iota(jnp.int32, (SUB, width), 0)
 
     def row_of(ref, at):
@@ -308,22 +354,8 @@
         )
 
     for cell in range(cells):
-        factor = coefficient[0:1, cell : cell + 1]
-        planes = []
-        for p in range(3):
-            parts = []
-            for device in range(devices):
-                ref = mine_ref if device < devices // 2 else theirs_ref
-                at = rows + device % (devices // 2) * held + (p * cells + cell) * tiles
-                parts = parts + [ref[at + t : at + t + 1, :] for t in range(tiles)]
-            planes.append(jnp.concatenate(parts, axis=1))
-        eddy = factor * planes[0]
         mask = mask_ref[cell : cell + 1, :]
-        shear = mask.astype(jnp.float32) * ((gas_viscosity + eddy) * 2.0 * planes[1])
-        heat = (gas_diffusivity + eddy / turbulent_prandtl) * 2.0 * planes[2]
         top = position == 0
-        shear = jnp.where(top, shear, 0.0)
-        heat = jnp.where(top, heat, 0.0)
         levels = level_ref[cell : cell + 1, :]
         for component in range(components):
             at = SUB + component * cells + cell
@@ -368,11 +400,19 @@
                 laplace = laplace + (shift_lanes(middle, 1) + shift_lanes(middle, -1)) - 6.0 * middle
                 rate = (melt_viscosity if component == 0 else melt_diffusivity) * laplace
                 if block == 0:
-                    rate = rate + jnp.where(level_id == 0, shear if component == 0 else heat, 0.0)
+                    flux = flux_ref[component * cells + cell : component * cells + cell + 1, :]
+                    rate = rate + jnp.where(level_id == 0, flux, 0.0)
                 if component == 0:
                     index = position * depth + SUB * block + level_id
                     rate = jnp.where(index >= levels, 0.0, rate)
                 out_ref[component, cell, here, :] = rate
+            copy = pltpu.make_async_copy(
+                out_ref.at[component, cell], out_hbm.at[component, cell], sems.at[component, cell]
+            )
+            copy.start()
+            copies = copies + [copy]
+    for copy in copies:
+        copy.wait()
 
 
 def swap(source, axis, mask):
@@ -385,7 +425,18 @@
     return lax.ppermute(source, axis, pairs + [(j, i) for i, j in pairs])
 
 
-def exchange(message, rows, axis):
+def swap_aside(source, first, aside):
+    count, devices = lax.axis_size("gx"), lax.axis_size("sa")
+    pairs = []
+    for i in range(first, count, 2):
+        j = (i + 1) % count
+        for s in range(devices):
+            t = s ^ 2 if aside else s
+            pairs = pairs + [(i * devices + s, j * devices + t), (j * devices + s, i * devices + t)]
+    return lax.ppermute(source, ("gx", "sa"), pairs)
+
+
+def exchange(message, axis):
     count = lax.axis_size(axis)
     mask = 1
     while True:
@@ -393,7 +444,8 @@
         mask = 2 * mask
         if mask == count:
             return message, other
-        message = jnp.concatenate([message[:rows] + other[:rows], message[rows:], other[rows:]])
+        merged = array(2 * message.shape[0] - SUB, LANES)
+        message = call(merge_messages, merged, [VMEM, VMEM])(message, other)
 
 
 def fenced(place, part, *arrays):
@@ -404,12 +456,12 @@
     return lax.cond(place[0] < lax.axis_size("sa"), part, no_part, *arrays)
 
 
-def call(kernel, outs, specs, scratch=(), flops=1):
+def call(kernel, outs, specs, scratch=(), flops=1, out_specs=None):
     return pl.pallas_call(
         kernel,
         out_shape=outs,
         in_specs=specs,
-        out_specs=jax.tree.map(lambda _: VMEM, outs),
+        out_specs=out_specs or jax.tree.map(lambda _: VMEM, outs),
         scratch_shapes=scratch,
         compiler_params=pltpu.CompilerParams(vmem_limit_bytes=24 * 1024 * 1024),
         cost_estimate=pl.CostEstimate(flops=flops, bytes_accessed=1, transcendentals=0),
@@ -430,19 +482,29 @@
     even = place[0] % 2 == 0
     gas_mate, gas_cross = swap(gas, "gx", 1), swap_across(gas, "gx")
     side = array(SUB + components * cells * width // LANES, LANES)
-    mate, cross = call(pack_sides, (side, side), [SMEM, VMEM, VMEM])(place, gas, melt)
+    mate, cross, gas_here = call(
+        pack_sides,
+        (side, side, array(*gas.shape)),
+        [SMEM, HBM, HBM],
+        scratch=(
+            pltpu.VMEM((2, components, cells, SUB, width), jnp.float32),
+            pltpu.SemaphoreType.DMA((3,)),
+        ),
+    )(place, pltpu.with_memory_space_constraint(gas, pltpu.HBM), pltpu.with_memory_space_constraint(melt, pltpu.HBM))
     mate, cross = swap(mate, "sa", 1), swap_across(cross, "sa")
     late = lax.broadcasted_iota(jnp.int32, (SUB, LANES), 1) % EDGE >= EDGE // 2
     halo = jnp.where(late == even, cross[:SUB], mate[:SUB])
-    halo_mate, halo_cross = swap(halo, "gx", 1), swap_across(halo, "gx")
+    aside = devices == 4
+    passed = jnp.where(late == even, mate[:SUB], cross[:SUB]) if aside else halo
+    halo_mate, halo_cross = swap_aside(passed, 0, aside), swap_aside(passed, 1, aside)
     part = array(components, depth, width)
     beside_mate, beside_cross = call(pack_melt, (part, part), [SMEM, VMEM, ANY])(place, melt, halo)
-    beside_mate, beside_cross = swap(beside_mate, "gx", 1), swap_across(beside_cross, "gx")
+    beside_cross = swap_across(beside_cross, "gx")
+    beside_mate = swap(beside_mate, "gx", 1)
 
     def gas_part(*arrays):
         wide = span + LANES
-        used = rows + 3 * cells * (span // LANES)
-        message_rows = -(-used // SUB) * SUB
+        message_rows = SUB + 3 * cells * (span // LANES)
         base, eddy, message = call(
             germano,
             (array(4, cells, rows, span), array(4, cells, rows, span), array(message_rows, LANES)),
@@ -453,30 +515,33 @@
                 pltpu.VMEM((cells, rows, span), jnp.float32),
             ),
         )(*arrays)
-        return base, eddy, *exchange(message, rows, "sa")
-
-    base, eddy, mine, theirs = fenced(
-        place, gas_part, place, gas, gas_mate, gas_cross, halo, halo_mate, halo_cross
+        mine, theirs = exchange(message, "sa")
+        rate = call(
+            functools.partial(finish_gas, span_cells), array(4, cells, rows, span), [VMEM] * 4
+        )(mine, theirs, base, eddy)
+        wall = call(
+            functools.partial(wall_fluxes, span_cells, devices, span),
+            array(2 * cells, width),
+            [VMEM, VMEM],
+        )(mine, theirs)
+        return rate, wall
+
+    gas_rate, wall = fenced(
+        place, gas_part, place, gas_here, gas_cross, gas_mate, halo, halo_mate, halo_cross
     )
-    gas_rate = call(
-        functools.partial(finish_gas, span_cells), array(4, cells, rows, span), [VMEM] * 4, flops=4000000000
-    )(mine, theirs, base, eddy)
+    flux = call(surface_flux, array(2 * cells, width), [SMEM, VMEM, VMEM], flops=4000000000)(
+        place, wall, surface_mask
+    )
     melt_rate = call(
-        functools.partial(finish_melt, span_cells, devices, rows, span),
+        functools.partial(finish_melt, devices),
         array(components, cells, depth, width),
-        [SMEM] + [VMEM] * 9,
-    )(
-        place,
-        mine,
-        theirs,
-        melt,
-        beside_mate,
-        beside_cross,
-        mate,
-        cross,
-        surface_mask,
-        melt_level,
-    )
+        [SMEM] + [VMEM] * 8,
+        scratch=(
+            pltpu.VMEM((components, cells, depth, width), jnp.float32),
+            pltpu.SemaphoreType.DMA((components, cells)),
+        ),
+        out_specs=HBM,
+    )(place, flux, melt, beside_mate, beside_cross, mate, cross, surface_mask, melt_level)
     return (gas_rate, melt_rate)
 
 

time: 36.2 us -> 32.3 us (0.89)
  the two profiles are of different devices: /device:TPU:20 before, /device:TPU:0 now
where the time goes in v3:
time: 32.3 us; the launch traced here: 32.1 us
  starting transfers between devices  15 us (46%)
  Pallas kernels  8.31 us (26%)
  waiting for transfers between devices  7.84 us (24%)
  between operations  0.72 us (2%)
    ppermute x5, starting transfers between devices, swap(): lax.ppermute(source, axis, [(i, i ^ mask) for i in range(lax.axis_size(ax...  7.9 us
    ppermute x3, starting transfers between devices, swap_across(): return lax.ppermute(source, axis, pairs + [(j, i) for i, j in pairs])  5.06 us
    ppermute x5, waiting for transfers between devices, swap(): lax.ppermute(source, axis, [(i, i ^ mask) for i in range(lax.axis_size(ax...  3.53 us
    pallas_call x1, Pallas kernels, gas_part(): call(germano, (array(4, cells, rows, span), array(4, cells, rows, span),...  3.51 us
    ppermute x2, waiting for transfers between devices, swap_aside(): return lax.ppermute(source, ('gx', 'sa'), pairs)  2.54 us
    ppermute x2, starting transfers between devices, swap_aside(): return lax.ppermute(source, ('gx', 'sa'), pairs)  2 us
    ppermute x3, waiting for transfers between devices, swap_across(): return lax.ppermute(source, axis, pairs + [(j, i) for i, j in pairs])  1.77 us
    pallas_call x1, Pallas kernels, on_device(): call(pack_sides, (side, side, array(*gas.shape)), [SMEM, HBM, HBM], scrat...  1.68 us
  transfers between devices with their start and end apart: 10, of which 4 were waited for; matrix products, arithmetic and copies ran while one was open for 0% of the time, Pallas kernels for 21%

profile of v3, /device:TPU:0, one launch (start us, length us, event | category | flops | bytes accessed | tf_op | source)
XLA Modules:
  0.0 32.1 jit_solution(16790177270369815584)
XLA Ops:
  0.6 0.0 copy-start
  0.6 3.0 %collective-permute-start.3 = (f32[4,2,32,256]{3,2,1,0:T(8,128)}, f32[4,2,32,256]{3,2,1,0:T(8,128)S(1)}, u32[]{:S(2)}, u32[]{:S(2)}) collective-permute-start(f32[4,2,32,256]{3,2,1,0:T(8,128)} %gas_hbm.1), channel_id=1, source_target_pairs={{0,4},{4,0},{8,12},{12,8},{16,20},{20,16},{24,28},{28,24},{1,5},{5... | collective-permute-start | bytes 786440 | tf_op jit(solution)/shard_map/ppermute | solution.py:419
  3.7 3.5 %collective-permute-start.2 = (f32[4,2,32,256]{3,2,1,0:T(8,128)}, f32[4,2,32,256]{3,2,1,0:T(8,128)S(1)}, u32[]{:S(2)}, u32[]{:S(2)}) collective-permute-start(f32[4,2,32,256]{3,2,1,0:T(8,128)} %gas_hbm.1), channel_id=1, source_target_pairs={{4,8},{12,16},{20,24},{28,0},{8,4},{16,12},{24,20},{0,28},{5,9},{1... | collective-permute-start | bytes 786440 | tf_op jit(solution)/shard_map/ppermute | solution.py:425
  7.2 0.1 pad_add_fusion.place_ref
  7.3 1.7 %shard_map.59 = (f32[40,128]{1,0:T(8,128)S(1)}, f32[40,128]{1,0:T(8,128)S(1)}, f32[4,2,32,256]{3,2,1,0:T(8,128)S(1)}) custom-call(s32[2]{0:T(128)S(1)} %pad_add_fusion.place_ref, f32[4,2,32,256]{3,2,1,0:T(8,128)} %gas_hbm.1, f32[2,2,32,1024]{3,2,1,0:T(8,128)} %melt_ref.3), custom_call_target="tpu_custom_call" | custom-call | flops 1 | bytes 1 | tf_op jit(solution)/shard_map/pallas_call | solution.py:485
  9.0 0.4 %collective-permute-start.4 = (f32[40,128]{1,0:T(8,128)S(1)}, f32[40,128]{1,0:T(8,128)S(1)}, u32[]{:S(2)}, u32[]{:S(2)}) collective-permute-start(f32[40,128]{1,0:T(8,128)S(1)} %get-tuple-element.34), channel_id=1, source_target_pairs={{1,2},{3,0},{2,1},{0,3},{5,6},{7,4},{6,5},{4,7},{9,10},{11,8},{10,... | collective-permute-start | bytes 61448 | tf_op jit(solution)/shard_map/ppermute | solution.py:425
  9.4 1.2 %collective-permute-start.5 = (f32[40,128]{1,0:T(8,128)S(1)}, f32[40,128]{1,0:T(8,128)S(1)}, u32[]{:S(2)}, u32[]{:S(2)}) collective-permute-start(f32[40,128]{1,0:T(8,128)S(1)} %get-tuple-element.35), channel_id=1, source_target_pairs={{0,1},{1,0},{2,3},{3,2},{4,5},{5,4},{6,7},{7,6},{8,9},{9,8},{10,11... | collective-permute-start | bytes 61448 | tf_op jit(solution)/shard_map/ppermute | solution.py:419
  10.7 1.8 %collective-permute-done.4.cross_ref = f32[40,128]{1,0:T(8,128)S(1)} collective-permute-done((f32[40,128]{1,0:T(8,128)S(1)}, f32[40,128]{1,0:T(8,128)S(1)}, u32[]{:S(2)}, u32[]{:S(2)}) %collective-permute-start.4) | collective-permute-done | bytes 20512 | tf_op jit(solution)/shard_map/ppermute | solution.py:425
  12.4 0.0 collective-permute-done.5.mate_ref
  12.4 2.0 %collective-permute-start.7 = (f32[8,128]{1,0:T(8,128)S(1)}, f32[8,128]{1,0:T(8,128)S(1)}, u32[]{:S(2)}, u32[]{:S(2)}) collective-permute-start(f32[8,128]{1,0:T(8,128)S(1)} %get-tuple-element.40), channel_id=1, source_target_pairs={{4,10},{8,6},{5,11},{9,7},{6,8},{10,4},{7,9},{11,5},{12,18},{16,14... | collective-permute-start | bytes 12296 | tf_op jit(solution)/shard_map/ppermute | solution.py:436
  14.4 0.0 collective-permute-start.6
  14.4 0.6 %shard_map.61 = (f32[2,32,1024]{2,1,0:T(8,128)S(1)}, f32[2,32,1024]{2,1,0:T(8,128)S(1)}) custom-call(s32[2]{0:T(128)S(1)} %pad_add_fusion.place_ref, f32[2,2,32,1024]{3,2,1,0:T(8,128)S(1)} %copy-done, f32[8,128]{1,0:T(8,128)S(1)} %get-tuple-element.41.after_ref), custom_call_target="tpu_custom_call" | custom-call | flops 1 | bytes 1 | tf_op jit(solution)/shard_map/pallas_call | solution.py:501
  15.0 2.2 %collective-permute-start.8 = (f32[2,32,1024]{2,1,0:T(8,128)S(1)}, f32[2,32,1024]{2,1,0:T(8,128)S(1)}, u32[]{:S(2)}, u32[]{:S(2)}) collective-permute-start(f32[2,32,1024]{2,1,0:T(8,128)S(1)} %get-tuple-element.38), channel_id=1, source_target_pairs={{0,4},{4,0},{8,12},{12,8},{16,20},{20,16},{24,28},{28,24},{1,5},{5... | collective-permute-start | bytes 786440 | tf_op jit(solution)/shard_map/ppermute | solution.py:419
  17.3 2.5 %collective-permute-done.7 = f32[8,128]{1,0:T(8,128)S(1)} collective-permute-done((f32[8,128]{1,0:T(8,128)S(1)}, f32[8,128]{1,0:T(8,128)S(1)}, u32[]{:S(2)}, u32[]{:S(2)}) %collective-permute-start.7) | collective-permute-done | bytes 4128 | tf_op jit(solution)/shard_map/ppermute | solution.py:436
  19.8 1.1 %collective-permute-start.9 = (f32[2,32,1024]{2,1,0:T(8,128)S(1)}, f32[2,32,1024]{2,1,0:T(8,128)S(1)}, u32[]{:S(2)}, u32[]{:S(2)}) collective-permute-start(f32[2,32,1024]{2,1,0:T(8,128)S(1)} %get-tuple-element.39), channel_id=1, source_target_pairs={{4,8},{12,16},{20,24},{28,0},{8,4},{16,12},{24,20},{0,28},{5,9},{1... | collective-permute-start | bytes 786440 | tf_op jit(solution)/shard_map/ppermute | solution.py:425
  20.9 0.0 collective-permute-done.3
  20.9 0.0 collective-permute-done.2
  20.9 0.0 copy-start.1
  20.9 8.8 %conditional.1 = (f32[4,2,32,256]{3,2,1,0:T(8,128)S(1)}, f32[4,1024]{1,0:T(4,128)S(1)}) conditional(s32[]{:T(128)} %convert_element_type.3, () %tuple.16, (s32[2]{0:T(128)S(1)}, f32[4,2,32,256]{3,2,1,0:T(8,128)S(1)}, f32[4,2,32,256]{3,2,1,0:T(8,128)S(1)}, f32[4,2,32,256]{3,2,1,0:T(8,128)S(1)}, f32[8,128]{1,0:T(8,128)S(1)}, ...), branch_computations={%region_0.1_spmd, %region_1.2_spmd} | conditional | flops 4 | bytes 278552 | solution.py:456
  20.9 3.5 %branch_1_fun.4 = (f32[4,2,32,256]{3,2,1,0:T(8,128)S(1)}, f32[4,2,32,256]{3,2,1,0:T(8,128)S(1)}, f32[20,128]{1,0:T(8,128)S(1)}) custom-call(s32[2]{0:T(128)S(1)} %get-tuple-element.14.place_ref, f32[4,2,32,256]{3,2,1,0:T(8,128)S(1)} %get-tuple-element.15.own_ref, f32[4,2,32,256]{3,2,1,0:T(8,128)S(1)} %get-tuple-element.16.cross_ref, ...), custom_call_target="tpu_custom_call" | custom-call | flops 1 | bytes 1 | tf_op jit(solution)/shard_map/cond/branch_1_fun/pallas_call | solution.py:508
  24.4 0.0 collective-permute-start
  24.5 1.2 %collective-permute-done.theirs_ref = f32[20,128]{1,0:T(8,128)S(1)} collective-permute-done((f32[20,128]{1,0:T(8,128)S(1)}, f32[20,128]{1,0:T(8,128)S(1)}, u32[]{:S(2)}, u32[]{:S(2)}) %collective-permute-start) | collective-permute-done | bytes 10272 | tf_op jit(solution)/shard_map/cond/branch_1_fun/ppermute | solution.py:419
  25.6 1.4 %collective-permute-start.1 = (f32[32,128]{1,0:T(8,128)S(1)}, f32[32,128]{1,0:T(8,128)S(1)}, u32[]{:S(2)}, u32[]{:S(2)}) collective-permute-start(f32[32,128]{1,0:T(8,128)S(1)} %branch_1_fun.5.mine_ref), channel_id=1, source_target_pairs={{0,2},{1,3},{2,0},{3,1},{4,6},{5,7},{6,4},{7,5},{8,10},{9,11},{10,... | collective-permute-start | bytes 49160 | tf_op jit(solution)/shard_map/cond/branch_1_fun/ppermute | solution.py:419
  27.0 2.4 %collective-permute-done.1.theirs_ref = f32[32,128]{1,0:T(8,128)S(1)} collective-permute-done((f32[32,128]{1,0:T(8,128)S(1)}, f32[32,128]{1,0:T(8,128)S(1)}, u32[]{:S(2)}, u32[]{:S(2)}) %collective-permute-start.1) | collective-permute-done | bytes 16416 | tf_op jit(solution)/shard_map/cond/branch_1_fun/ppermute | solution.py:419
  29.4 0.2 branch_1_fun.7
  29.5 0.2 branch_1_fun.6
  29.7 0.0 copy-start.3
  29.7 0.0 copy-start.2
  29.8 0.6 %shard_map.60.flux_ref = f32[4,1024]{1,0:T(4,128)S(1)} custom-call(s32[2]{0:T(128)S(1)} %pad_add_fusion.place_ref, f32[4,1024]{1,0:T(4,128)S(1)} %get-tuple-element.37.wall_ref, s32[2,1024]{1,0:T(2,128)S(1)} %copy-done.1), custom_call_target="tpu_custom_call" | custom-call | flops 4000000000 | bytes 1 | tf_op jit(solution)/shard_map/pallas_call | solution.py:532
  30.3 0.1 copy-done.3
  30.4 0.1 copy-done.2
  30.5 1.6 %shard_map.62 = f32[2,2,32,1024]{3,2,1,0:T(8,128)} custom-call(s32[2]{0:T(128)S(1)} %pad_add_fusion.place_ref, f32[4,1024]{1,0:T(4,128)S(1)} %shard_map.60.flux_ref, f32[2,2,32,1024]{3,2,1,0:T(8,128)S(1)} %copy-done, f32[2,32,1024]{2,1,0:T(8,128)S(1)} %collective-permute-done.8.beside_mate_ref, f32[2,32,1024]{2,1,0:T(8,128)S(1)} %collective-permute-done.9.beside_cross_ref, ...), custom_call_target="tpu_custom_call" | custom-call | flops 1 | bytes 1 | tf_op jit(solution)/shard_map/pallas_call | solution.py:535
  (9 shorter events, 0.0 us)
Async XLA Ops:
  0.6 13.8 %copy-start = (f32[2,2,32,1024]{3,2,1,0:T(8,128)S(1)}, f32[2,2,32,1024]{3,2,1,0:T(8,128)}, u32[]{:S(2)}) copy-start(f32[2,2,32,1024]{3,2,1,0:T(8,128)} %melt_ref.3) | copy-start | bytes 1572868
  0.6 20.3 %collective-permute-start.3 = (f32[4,2,32,256]{3,2,1,0:T(8,128)}, f32[4,2,32,256]{3,2,1,0:T(8,128)S(1)}, u32[]{:S(2)}, u32[]{:S(2)}) collective-permute-start(f32[4,2,32,256]{3,2,1,0:T(8,128)} %gas_hbm.1), channel_id=1, source_target_pairs={{0,4},{4,0},{8,12},{12,8},{16,20},{20,16},{24,28},{28,24},{1,5},{5... | collective-permute-start | bytes 786440 | tf_op jit(solution)/shard_map/ppermute | solution.py:419
  3.7 17.2 %collective-permute-start.2 = (f32[4,2,32,256]{3,2,1,0:T(8,128)}, f32[4,2,32,256]{3,2,1,0:T(8,128)S(1)}, u32[]{:S(2)}, u32[]{:S(2)}) collective-permute-start(f32[4,2,32,256]{3,2,1,0:T(8,128)} %gas_hbm.1), channel_id=1, source_target_pairs={{4,8},{12,16},{20,24},{28,0},{8,4},{16,12},{24,20},{0,28},{5,9},{1... | collective-permute-start | bytes 786440 | tf_op jit(solution)/shard_map/ppermute | solution.py:425
  9.0 3.4 %collective-permute-start.4 = (f32[40,128]{1,0:T(8,128)S(1)}, f32[40,128]{1,0:T(8,128)S(1)}, u32[]{:S(2)}, u32[]{:S(2)}) collective-permute-start(f32[40,128]{1,0:T(8,128)S(1)} %get-tuple-element.34), channel_id=1, source_target_pairs={{1,2},{3,0},{2,1},{0,3},{5,6},{7,4},{6,5},{4,7},{9,10},{11,8},{10,... | collective-permute-start | bytes 61448 | tf_op jit(solution)/shard_map/ppermute | solution.py:425
  9.4 3.0 %collective-permute-start.5 = (f32[40,128]{1,0:T(8,128)S(1)}, f32[40,128]{1,0:T(8,128)S(1)}, u32[]{:S(2)}, u32[]{:S(2)}) collective-permute-start(f32[40,128]{1,0:T(8,128)S(1)} %get-tuple-element.35), channel_id=1, source_target_pairs={{0,1},{1,0},{2,3},{3,2},{4,5},{5,4},{6,7},{7,6},{8,9},{9,8},{10,11... | collective-permute-start | bytes 61448 | tf_op jit(solution)/shard_map/ppermute | solution.py:419
  12.4 7.4 %collective-permute-start.7 = (f32[8,128]{1,0:T(8,128)S(1)}, f32[8,128]{1,0:T(8,128)S(1)}, u32[]{:S(2)}, u32[]{:S(2)}) collective-permute-start(f32[8,128]{1,0:T(8,128)S(1)} %get-tuple-element.40), channel_id=1, source_target_pairs={{4,10},{8,6},{5,11},{9,7},{6,8},{10,4},{7,9},{11,5},{12,18},{16,14... | collective-permute-start | bytes 12296 | tf_op jit(solution)/shard_map/ppermute | solution.py:436
  14.4 6.4 %collective-permute-start.6 = (f32[8,128]{1,0:T(8,128)S(1)}, f32[8,128]{1,0:T(8,128)S(1)}, u32[]{:S(2)}, u32[]{:S(2)}) collective-permute-start(f32[8,128]{1,0:T(8,128)S(1)} %get-tuple-element.40), channel_id=1, source_target_pairs={{0,6},{4,2},{1,7},{5,3},{2,4},{6,0},{3,5},{7,1},{8,14},{12,10},{9,... | collective-permute-start | bytes 12296 | tf_op jit(solution)/shard_map/ppermute | solution.py:436
  15.0 15.4 %collective-permute-start.8 = (f32[2,32,1024]{2,1,0:T(8,128)S(1)}, f32[2,32,1024]{2,1,0:T(8,128)S(1)}, u32[]{:S(2)}, u32[]{:S(2)}) collective-permute-start(f32[2,32,1024]{2,1,0:T(8,128)S(1)} %get-tuple-element.38), channel_id=1, source_target_pairs={{0,4},{4,0},{8,12},{12,8},{16,20},{20,16},{24,28},{28,24},{1,5},{5... | collective-permute-start | bytes 786440 | tf_op jit(solution)/shard_map/ppermute | solution.py:419
  19.8 10.6 %collective-permute-start.9 = (f32[2,32,1024]{2,1,0:T(8,128)S(1)}, f32[2,32,1024]{2,1,0:T(8,128)S(1)}, u32[]{:S(2)}, u32[]{:S(2)}) collective-permute-start(f32[2,32,1024]{2,1,0:T(8,128)S(1)} %get-tuple-element.39), channel_id=1, source_target_pairs={{4,8},{12,16},{20,24},{28,0},{8,4},{16,12},{24,20},{0,28},{5,9},{1... | collective-permute-start | bytes 786440 | tf_op jit(solution)/shard_map/ppermute | solution.py:425
  20.9 8.8 %copy-start.1 = (s32[2,1024]{1,0:T(2,128)S(1)}, s32[2,1024]{1,0:T(2,128)}, u32[]{:S(2)}) copy-start(s32[2,1024]{1,0:T(2,128)} %mask_ref.3) | copy-start | bytes 24580
  24.4 1.2 %collective-permute-start = (f32[20,128]{1,0:T(8,128)S(1)}, f32[20,128]{1,0:T(8,128)S(1)}, u32[]{:S(2)}, u32[]{:S(2)}) collective-permute-start(f32[20,128]{1,0:T(8,128)S(1)} %get-tuple-element.21.mine_ref), channel_id=1, source_target_pairs={{0,1},{1,0},{2,3},{3,2},{4,5},{5,4},{6,7},{7,6},{8,9},{9,8},{10,11... | collective-permute-start | bytes 30728 | tf_op jit(solution)/shard_map/cond/branch_1_fun/ppermute | solution.py:419
  25.6 3.7 %collective-permute-start.1 = (f32[32,128]{1,0:T(8,128)S(1)}, f32[32,128]{1,0:T(8,128)S(1)}, u32[]{:S(2)}, u32[]{:S(2)}) collective-permute-start(f32[32,128]{1,0:T(8,128)S(1)} %branch_1_fun.5.mine_ref), channel_id=1, source_target_pairs={{0,2},{1,3},{2,0},{3,1},{4,6},{5,7},{6,4},{7,5},{8,10},{9,11},{10,... | collective-permute-start | bytes 49160 | tf_op jit(solution)/shard_map/cond/branch_1_fun/ppermute | solution.py:419
  29.7 0.7 %copy-start.3 = (f32[4,2,32,256]{3,2,1,0:T(8,128)}, f32[4,2,32,256]{3,2,1,0:T(8,128)S(1)}, u32[]{:S(2)}) copy-start(f32[4,2,32,256]{3,2,1,0:T(8,128)S(1)} %get-tuple-element.31) | copy-start | bytes 786436
  29.7 0.7 %copy-start.2 = (s32[2,1024]{1,0:T(2,128)S(1)}, s32[2,1024]{1,0:T(2,128)}, u32[]{:S(2)}) copy-start(s32[2,1024]{1,0:T(2,128)} %level_ref.1) | copy-start | bytes 24580

commit v4 on v3

--- a/solution.py
+++ b/solution.py
@@ -19,7 +19,6 @@
 EDGE = 4
 PAIRS = ((0, 0), (1, 1), (2, 2), (0, 1), (0, 2), (1, 2))
 VMEM = pl.BlockSpec(memory_space=pltpu.VMEM)
-SMEM = pl.BlockSpec(memory_space=pltpu.SMEM)
 ANY = pl.BlockSpec(memory_space=pl.ANY)
 HBM = pl.BlockSpec(memory_space=pltpu.HBM)
 
@@ -33,7 +32,7 @@
     return ((row_block * cells + cell) * 4 + component) * EDGE
 
 
-def pack_sides(place_ref, gas_hbm, melt_hbm, mate_ref, cross_ref, gas_ref, ends_ref, sems):
+def pack_sides(gas_hbm, melt_hbm, mate_ref, cross_ref, gas_ref, ends_ref, sems):
     _, cells, rows, span = gas_ref.shape
     components, _, depth, width = melt_hbm.shape
     copies = [pltpu.make_async_copy(gas_hbm, gas_ref, sems.at[0])]
@@ -58,7 +57,7 @@
                 )
     mate_ref[0:SUB, :] = tile
     cross_ref[0:SUB, :] = tile
-    even = place_ref[0] % 2 == 0
+    even = lax.axis_index("sa") % 2 == 0
     for copy in copies[1:]:
         copy.wait()
     for component in range(components):
@@ -73,19 +72,18 @@
                 cross_ref[at : at + 1, :] = cross[:, t * LANES : (t + 1) * LANES]
 
 
-def pack_melt(place_ref, melt_ref, after_ref, mate_ref, cross_ref):
+def pack_melt(first, melt_ref, *refs):
+    out_ref = refs[-1]
     last = melt_ref.shape[1] - 1
-    even = place_ref[1] % 2 == 0
-
-    @pl.when(even)
+    lower = lax.axis_index("gx") % 2 == first
+
+    @pl.when(lower)
     def _():
-        mate_ref[...] = melt_ref[:, last]
-        cross_ref[...] = melt_ref[:, 0]
-
-    @pl.when(jnp.logical_not(even))
+        out_ref[...] = melt_ref[:, last]
+
+    @pl.when(jnp.logical_not(lower))
     def _():
-        mate_ref[...] = melt_ref[:, 0]
-        cross_ref[...] = melt_ref[:, last]
+        out_ref[...] = melt_ref[:, 0]
 
 
 def binomial(source):
@@ -93,7 +91,6 @@
 
 
 def germano(
-    place_ref,
     own_ref,
     cross_ref,
     mate_ref,
@@ -110,7 +107,7 @@
     _, cells, rows, span = own_ref.shape
     wide = span + LANES
     lane = lax.broadcasted_iota(jnp.int32, (SUB, LANES), 1)
-    even = place_ref[1] % 2 == 0
+    even = lax.axis_index("gx") % 2 == 0
     halo = halo_ref[...]
     halo_left = jnp.where(even, halo_cross_ref[...], halo_mate_ref[...])
     halo_right = jnp.where(even, halo_mate_ref[...], halo_cross_ref[...])
@@ -317,34 +314,71 @@
                 )
 
 
-def surface_flux(place_ref, wall_ref, mask_ref, flux_ref):
+def surface_flux(wall_ref, mask_ref, flux_ref):
     cells = mask_ref.shape[0]
-    top = place_ref[0] == 0
+    top = lax.axis_index("sa") == 0
     shear = mask_ref[...].astype(jnp.float32) * wall_ref[0:cells, :]
     flux_ref[0:cells, :] = jnp.where(top, shear, 0.0)
     flux_ref[cells:, :] = jnp.where(top, wall_ref[cells:, :], 0.0)
 
 
 def finish_melt(
-    devices,
-    place_ref,
     flux_ref,
-    melt_ref,
+    inside_ref,
     beside_mate_ref,
-    beside_cross_ref,
-    mate_ref,
-    cross_ref,
-    mask_ref,
+    beside_ends_ref,
+    beside_between_ref,
     level_ref,
     out_hbm,
     out_ref,
     sems,
 ):
+    components, cells, depth, width = inside_ref.shape
+    position = lax.axis_index("sa")
+    place = lax.axis_index("gx")
+    even = place % 2 == 0
+    at_end = (place == 0) | (place == lax.axis_size("gx") - 1)
+    level_id = lax.broadcasted_iota(jnp.int32, (SUB, width), 0)
+    copies = []
+    for cell in range(cells):
+        levels = level_ref[cell : cell + 1, :]
+        for component in range(components):
+            share = melt_viscosity if component == 0 else melt_diffusivity
+            for block in range(depth // SUB):
+                here = slice(SUB * block, SUB * (block + 1))
+                rate = inside_ref[component, cell, here, :]
+                if cell in (0, cells - 1):
+                    from_mate = beside_mate_ref[component, here, :]
+                    from_cross = jnp.where(
+                        at_end,
+                        beside_ends_ref[component, here, :],
+                        beside_between_ref[component, here, :],
+                    )
+                    outer = jnp.where(even == (cell == 0), from_cross, from_mate)
+                    rate = rate + share * outer
+                if block == 0:
+                    flux = flux_ref[component * cells + cell : component * cells + cell + 1, :]
+                    rate = rate + jnp.where(level_id == 0, flux, 0.0)
+                if component == 0:
+                    index = position * depth + SUB * block + level_id
+                    rate = jnp.where(index >= levels, 0.0, rate)
+                out_ref[component, cell, here, :] = rate
+            copy = pltpu.make_async_copy(
+                out_ref.at[component, cell], out_hbm.at[component, cell], sems.at[component, cell]
+            )
+            copy.start()
+            copies = copies + [copy]
+    for copy in copies:
+        copy.wait()
+
+
+def melt_inside(devices, melt_ref, mate_ref, cross_ref, mask_ref, after_ref, part_ref, inside_ref):
     components, cells, depth, width = melt_ref.shape
-    position = place_ref[0]
+    assert cells > 1
+    pack_melt(0, melt_ref, part_ref)
+    position = lax.axis_index("sa")
     even = position % 2 == 0
-    even_cell = place_ref[1] % 2 == 0
-    copies = []
+    top = position == 0
     level_id = lax.broadcasted_iota(jnp.int32, (SUB, width), 0)
 
     def row_of(ref, at):
@@ -355,8 +389,6 @@
 
     for cell in range(cells):
         mask = mask_ref[cell : cell + 1, :]
-        top = position == 0
-        levels = level_ref[cell : cell + 1, :]
         for component in range(components):
             at = SUB + component * cells + cell
             from_mate, from_cross = row_of(mate_ref, at), row_of(cross_ref, at)
@@ -378,41 +410,14 @@
                     if block == depth // SUB - 1
                     else melt_ref[component, cell, SUB * block + 1 : SUB * (block + 1) + 1, :]
                 )
-                before = (
-                    jnp.where(
-                        even_cell,
-                        beside_cross_ref[component, here, :],
-                        beside_mate_ref[component, here, :],
-                    )
-                    if cell == 0
-                    else melt_ref[component, cell - 1, here, :]
-                )
-                after = (
-                    jnp.where(
-                        even_cell,
-                        beside_mate_ref[component, here, :],
-                        beside_cross_ref[component, here, :],
-                    )
-                    if cell == cells - 1
-                    else melt_ref[component, cell + 1, here, :]
-                )
-                laplace = (before + after) + (over + under)
-                laplace = laplace + (shift_lanes(middle, 1) + shift_lanes(middle, -1)) - 6.0 * middle
-                rate = (melt_viscosity if component == 0 else melt_diffusivity) * laplace
-                if block == 0:
-                    flux = flux_ref[component * cells + cell : component * cells + cell + 1, :]
-                    rate = rate + jnp.where(level_id == 0, flux, 0.0)
-                if component == 0:
-                    index = position * depth + SUB * block + level_id
-                    rate = jnp.where(index >= levels, 0.0, rate)
-                out_ref[component, cell, here, :] = rate
-            copy = pltpu.make_async_copy(
-                out_ref.at[component, cell], out_hbm.at[component, cell], sems.at[component, cell]
-            )
-            copy.start()
-            copies = copies + [copy]
-    for copy in copies:
-        copy.wait()
+                laplace = (over + under) + (shift_lanes(middle, 1) + shift_lanes(middle, -1))
+                for near in (cell - 1, cell + 1):
+                    if 0 <= near < cells:
+                        laplace = laplace + melt_ref[component, near, here, :]
+                laplace = laplace - 6.0 * middle
+                inside_ref[component, cell, here, :] = (
+                    melt_viscosity if component == 0 else melt_diffusivity
+                ) * laplace
 
 
 def swap(source, axis, mask):
@@ -423,6 +428,17 @@
     count = lax.axis_size(axis)
     pairs = [(i, (i + 1) % count) for i in range(1, count, 2)]
     return lax.ppermute(source, axis, pairs + [(j, i) for i, j in pairs])
+
+
+def swap_between(source, axis):
+    count = lax.axis_size(axis)
+    pairs = [(i, i + 1) for i in range(1, count - 1, 2)]
+    return lax.ppermute(source, axis, pairs + [(j, i) for i, j in pairs])
+
+
+def swap_ends(source, axis):
+    last = lax.axis_size(axis) - 1
+    return lax.ppermute(source, axis, [(0, last), (last, 0)])
 
 
 def swap_aside(source, first, aside):
@@ -448,12 +464,12 @@
         message = call(merge_messages, merged, [VMEM, VMEM])(message, other)
 
 
-def fenced(place, part, *arrays):
+def fenced(part, *arrays):
     def no_part(*arrays):
         shapes = jax.eval_shape(part, *arrays)
         return jax.tree.map(lambda leaf: jnp.zeros(leaf.shape, leaf.dtype), shapes)
 
-    return lax.cond(place[0] < lax.axis_size("sa"), part, no_part, *arrays)
+    return lax.cond(lax.axis_index("sa") < lax.axis_size("sa"), part, no_part, *arrays)
 
 
 def call(kernel, outs, specs, scratch=(), flops=1, out_specs=None):
@@ -478,29 +494,34 @@
     devices = lax.axis_size("sa")
     assert devices & (devices - 1) == 0 and devices > 1
     span_cells = float(span * devices)
-    place = jnp.stack([lax.axis_index("sa"), lax.axis_index("gx")]).astype(jnp.int32)
-    even = place[0] % 2 == 0
-    gas_mate, gas_cross = swap(gas, "gx", 1), swap_across(gas, "gx")
+    even = lax.axis_index("sa") % 2 == 0
+    gas_mate = swap(gas, "gx", 1)
     side = array(SUB + components * cells * width // LANES, LANES)
     mate, cross, gas_here = call(
         pack_sides,
         (side, side, array(*gas.shape)),
-        [SMEM, HBM, HBM],
+        [HBM, HBM],
         scratch=(
             pltpu.VMEM((2, components, cells, SUB, width), jnp.float32),
             pltpu.SemaphoreType.DMA((3,)),
         ),
-    )(place, pltpu.with_memory_space_constraint(gas, pltpu.HBM), pltpu.with_memory_space_constraint(melt, pltpu.HBM))
+    )(pltpu.with_memory_space_constraint(gas, pltpu.HBM), pltpu.with_memory_space_constraint(melt, pltpu.HBM))
+    gas_cross = swap_across(gas_here, "gx")
     mate, cross = swap(mate, "sa", 1), swap_across(cross, "sa")
     late = lax.broadcasted_iota(jnp.int32, (SUB, LANES), 1) % EDGE >= EDGE // 2
     halo = jnp.where(late == even, cross[:SUB], mate[:SUB])
     aside = devices == 4
     passed = jnp.where(late == even, mate[:SUB], cross[:SUB]) if aside else halo
     halo_mate, halo_cross = swap_aside(passed, 0, aside), swap_aside(passed, 1, aside)
-    part = array(components, depth, width)
-    beside_mate, beside_cross = call(pack_melt, (part, part), [SMEM, VMEM, ANY])(place, melt, halo)
-    beside_cross = swap_across(beside_cross, "gx")
-    beside_mate = swap(beside_mate, "gx", 1)
+    part, whole = array(components, depth, width), array(components, cells, depth, width)
+    mate_part, inside = call(
+        functools.partial(melt_inside, devices), (part, whole), [VMEM] * 4 + [ANY]
+    )(melt, mate, cross, surface_mask, halo_mate)
+    ends_part = call(functools.partial(pack_melt, 1), part, [VMEM, ANY])(melt, halo_mate)
+    cross_part = call(functools.partial(pack_melt, 1), part, [VMEM, ANY])(melt, halo_cross)
+    beside_mate = swap(mate_part, "gx", 1)
+    beside_ends = swap_ends(ends_part, "gx")
+    beside_between = swap_between(cross_part, "gx")
 
     def gas_part(*arrays):
         wide = span + LANES
@@ -508,7 +529,7 @@
         base, eddy, message = call(
             germano,
             (array(4, cells, rows, span), array(4, cells, rows, span), array(message_rows, LANES)),
-            [SMEM] + [VMEM] * 6,
+            [VMEM] * 6,
             scratch=(
                 pltpu.VMEM((cells + 4, 4, rows + 2 * SUB, wide), jnp.float32),
                 pltpu.VMEM((cells + 2, 3, rows + 2 * SUB, wide), jnp.float32),
@@ -527,21 +548,21 @@
         return rate, wall
 
     gas_rate, wall = fenced(
-        place, gas_part, place, gas_here, gas_cross, gas_mate, halo, halo_mate, halo_cross
+        gas_part, gas_here, gas_cross, gas_mate, halo, halo_mate, halo_cross
     )
-    flux = call(surface_flux, array(2 * cells, width), [SMEM, VMEM, VMEM], flops=4000000000)(
-        place, wall, surface_mask
+    flux = call(surface_flux, array(2 * cells, width), [VMEM, VMEM], flops=4000000000)(
+        wall, surface_mask
     )
     melt_rate = call(
-        functools.partial(finish_melt, devices),
-        array(components, cells, depth, width),
-        [SMEM] + [VMEM] * 8,
+        finish_melt,
+        whole,
+        [VMEM] * 6,
         scratch=(
             pltpu.VMEM((components, cells, depth, width), jnp.float32),
             pltpu.SemaphoreType.DMA((components, cells)),
         ),
         out_specs=HBM,
-    )(place, flux, melt, beside_mate, beside_cross, mate, cross, surface_mask, melt_level)
+    )(flux, inside, beside_mate, beside_ends, beside_between, melt_level)
     return (gas_rate, melt_rate)
 
 

time: 32.3 us -> 31.4 us (0.972)
  starting transfers between devices: 15 us -> 19.7 us
  waiting for transfers between devices: 7.84 us -> 3.98 us
  Pallas kernels: 8.31 us -> 5.92 us
  local copies, waits for them, and re-layouts: 0.19 us -> 0.7 us
    ppermute x0 -> x2, starting transfers between devices: none -> 5.76 us  [the longest x1 5.08 us: swap_ends(): return lax.ppermute(source, axis, [(0, last), (last, 0)])]
    ppermute x5, starting transfers between devices: 7.9 us -> 4.68 us  [swap(): lax.ppermute(source, axis, [(i, i ^ mask) for i in range(lax.axis_size(ax...]
    ppermute x2, starting transfers between devices: 2 us -> 4.1 us  [swap_aside(): return lax.ppermute(source, ('gx', 'sa'), pairs)]
    ppermute x2, waiting for transfers between devices: 2.54 us -> 0.55 us  [swap_aside(): return lax.ppermute(source, ('gx', 'sa'), pairs)]
    pallas_call x4 -> x6, Pallas kernels: 4.46 us -> 2.6 us  [the longest x1 1.17 us: on_device(): call(pack_sides, (side, side, array(*gas.shape)), [HBM, HBM], scratch=(pl...]
    ppermute x3 -> x2, waiting for transfers between devices: 1.77 us -> 0.01 us  [swap_across(): return lax.ppermute(source, axis, pairs + [(j, i) for i, j in pairs])]
    pallas_call x1, Pallas kernels: 3.51 us -> 2.98 us  [gas_part(): call(germano, (array(4, cells, rows, span), array(4, cells, rows, span),...]
    unnamed x8, local copies, waits for them, and re-layouts: 0.19 us -> 0.7 us
  transfers between devices with their start and end apart: 10 -> 11, of which waited for: 4 -> 3; matrix products, arithmetic and copies ran while one was open for 0% -> 0% of each run, Pallas kernels for 21% -> 16%
where the time goes in v4:
time: 31.4 us; the launch traced here: 31.1 us
  starting transfers between devices  19.7 us (63%)
  Pallas kernels  5.92 us (19%)
  waiting for transfers between devices  3.98 us (13%)
  between operations  0.8 us (3%)
  local copies, waits for them, and re-layouts  0.7 us (2%)
    ppermute x2, starting transfers between devices, swap_across(): return lax.ppermute(source, axis, pairs + [(j, i) for i, j in pairs])  5.15 us
    ppermute x1, starting transfers between devices, swap_ends(): return lax.ppermute(source, axis, [(0, last), (last, 0)])  5.08 us
    ppermute x5, starting transfers between devices, swap(): lax.ppermute(source, axis, [(i, i ^ mask) for i in range(lax.axis_size(ax...  4.68 us
    ppermute x2, starting transfers between devices, swap_aside(): return lax.ppermute(source, ('gx', 'sa'), pairs)  4.1 us
    ppermute x5, waiting for transfers between devices, swap(): lax.ppermute(source, axis, [(i, i ^ mask) for i in range(lax.axis_size(ax...  3.42 us
    pallas_call x1, Pallas kernels, gas_part(): call(germano, (array(4, cells, rows, span), array(4, cells, rows, span),...  2.98 us
    pallas_call x1, Pallas kernels, on_device(): call(pack_sides, (side, side, array(*gas.shape)), [HBM, HBM], scratch=(pl...  1.17 us
    pallas_call x1, Pallas kernels, on_device(): call(finish_melt, whole, [VMEM] * 6, scratch=(pltpu.VMEM((components, cel...  0.86 us
  transfers between devices with their start and end apart: 11, of which 3 were waited for; matrix products, arithmetic and copies ran while one was open for 0% of the time, Pallas kernels for 16%

profile of v4, /device:TPU:0, one launch (start us, length us, event | category | flops | bytes accessed | tf_op | source)
XLA Modules:
  0.0 31.1 jit_solution(13439105526260967324)
XLA Ops:
  0.6 3.0 %collective-permute-start.5 = (f32[4,2,32,256]{3,2,1,0:T(8,128)}, f32[4,2,32,256]{3,2,1,0:T(8,128)S(1)}, u32[]{:S(2)}, u32[]{:S(2)}) collective-permute-start(f32[4,2,32,256]{3,2,1,0:T(8,128)} %gas_hbm.1), channel_id=1, source_target_pairs={{0,4},{4,0},{8,12},{12,8},{16,20},{20,16},{24,28},{28,24},{1,5},{5... | collective-permute-start | bytes 786440 | tf_op jit(solution)/shard_map/ppermute | solution.py:424
  3.7 1.2 %shard_map.59 = (f32[40,128]{1,0:T(8,128)S(1)}, f32[40,128]{1,0:T(8,128)S(1)}, f32[4,2,32,256]{3,2,1,0:T(8,128)S(1)}) custom-call(f32[4,2,32,256]{3,2,1,0:T(8,128)} %gas_hbm.1, f32[2,2,32,1024]{3,2,1,0:T(8,128)} %melt_ref.5), custom_call_target="tpu_custom_call" | custom-call | flops 1 | bytes 1 | tf_op jit(solution)/shard_map/pallas_call | solution.py:500
  4.9 0.1 collective-permute-start.3
  4.9 1.6 %collective-permute-start.2 = (f32[40,128]{1,0:T(8,128)S(1)}, f32[40,128]{1,0:T(8,128)S(1)}, u32[]{:S(2)}, u32[]{:S(2)}) collective-permute-start(f32[40,128]{1,0:T(8,128)S(1)} %get-tuple-element.37), channel_id=1, source_target_pairs={{1,2},{3,0},{2,1},{0,3},{5,6},{7,4},{6,5},{4,7},{9,10},{11,8},{10,... | collective-permute-start | bytes 61448 | tf_op jit(solution)/shard_map/ppermute | solution.py:430
  6.5 3.5 %collective-permute-start.4 = (f32[4,2,32,256]{3,2,1,0:T(8,128)S(1)}, f32[4,2,32,256]{3,2,1,0:T(8,128)S(1)}, u32[]{:S(2)}, u32[]{:S(2)}) collective-permute-start(f32[4,2,32,256]{3,2,1,0:T(8,128)S(1)} %get-tuple-element.39), channel_id=1, source_target_pairs={{4,8},{12,16},{20,24},{28,0},{8,4},{16,12},{24,20},{0,28},{5,9},{1... | collective-permute-start | bytes 786440 | tf_op jit(solution)/shard_map/ppermute | solution.py:430
  10.1 0.0 collective-permute-done.3.mate_ref
  10.1 0.0 collective-permute-done.2.cross_ref
  10.1 0.0 copy-start.1
  10.1 0.1 collective-permute-start.6
  10.2 4.0 %collective-permute-start.7 = (f32[8,128]{1,0:T(8,128)S(1)}, f32[8,128]{1,0:T(8,128)S(1)}, u32[]{:S(2)}, u32[]{:S(2)}) collective-permute-start(f32[8,128]{1,0:T(8,128)S(1)} %get-tuple-element.44), channel_id=1, source_target_pairs={{4,10},{8,6},{5,11},{9,7},{6,8},{10,4},{7,9},{11,5},{12,18},{16,14... | collective-permute-start | bytes 12296 | tf_op jit(solution)/shard_map/ppermute | solution.py:452
  14.2 0.5 %collective-permute-done.6.after_ref.refs_0_ = f32[8,128]{1,0:T(8,128)S(1)} collective-permute-done((f32[8,128]{1,0:T(8,128)S(1)}, f32[8,128]{1,0:T(8,128)S(1)}, u32[]{:S(2)}, u32[]{:S(2)}) %collective-permute-start.6) | collective-permute-done | bytes 4128 | tf_op jit(solution)/shard_map/ppermute | solution.py:452
  14.8 0.5 %shard_map.61 = (f32[2,32,1024]{2,1,0:T(8,128)S(1)}, f32[2,2,32,1024]{3,2,1,0:T(8,128)S(1)}) custom-call(f32[2,2,32,1024]{3,2,1,0:T(8,128)S(1)} %copy-done, f32[40,128]{1,0:T(8,128)S(1)} %collective-permute-done.3.mate_ref, f32[40,128]{1,0:T(8,128)S(1)} %collective-permute-done.2.cross_ref, s32[2,1024]{1,0:T(2,128)S(1)} %copy-done.1, ...), custom_call_target="tpu_custom_call" | custom-call | flops 1 | bytes 1 | tf_op jit(solution)/shard_map/pallas_call | solution.py:517
  15.3 0.1 collective-permute-start.8
  15.4 5.1 %collective-permute-start.9 = (f32[2,32,1024]{2,1,0:T(8,128)S(1)}, f32[2,32,1024]{2,1,0:T(8,128)S(1)}, u32[]{:S(2)}, u32[]{:S(2)}) collective-permute-start(f32[2,32,1024]{2,1,0:T(8,128)S(1)} %shard_map.62), channel_id=1, source_target_pairs={{0,28},{28,0},{1,29},{29,1},{2,30},{30,2},{3,31},{31,3}} | collective-permute-start | bytes 786440 | tf_op jit(solution)/shard_map/ppermute | solution.py:441
  20.5 0.0 collective-permute-done.7.refs_0_
  20.5 0.7 %collective-permute-start.10 = (f32[2,32,1024]{2,1,0:T(8,128)S(1)}, f32[2,32,1024]{2,1,0:T(8,128)S(1)}, u32[]{:S(2)}, u32[]{:S(2)}) collective-permute-start(f32[2,32,1024]{2,1,0:T(8,128)S(1)} %shard_map.63), channel_id=1, source_target_pairs={{4,8},{12,16},{20,24},{8,4},{16,12},{24,20},{5,9},{13,17},{21,25},... | collective-permute-start | bytes 786440 | tf_op jit(solution)/shard_map/ppermute | solution.py:436
  21.2 0.0 collective-permute-done.4
  21.2 0.0 collective-permute-done.5
  21.3 8.3 %conditional.1 = (f32[4,2,32,256]{3,2,1,0:T(8,128)S(1)}, f32[4,1024]{1,0:T(4,128)S(1)}) conditional(s32[]{:T(128)} %convert_element_type.3, () %tuple.16, (pred[8,128]{1,0:T(8,128)(4,1)S(1)}, f32[8,128]{1,0:T(8,128)S(1)}, f32[8,128]{1,0:T(8,128)S(1)}, f32[4,2,32,256]{3,2,1,0:T(8,128)S(1)}, f32[4,2,32,256]{3,2,1,0:T(8,128)S(1)}, ...), branch_computations={%region_0.1_spmd, %region_1.2_spmd} | conditional | flops 1028 | bytes 278552 | solution.py:472
  21.3 3.0 %branch_1_fun.4 = (f32[4,2,32,256]{3,2,1,0:T(8,128)S(1)}, f32[4,2,32,256]{3,2,1,0:T(8,128)S(1)}, f32[20,128]{1,0:T(8,128)S(1)}) custom-call(f32[4,2,32,256]{3,2,1,0:T(8,128)S(1)} %get-tuple-element.17.own_ref, f32[4,2,32,256]{3,2,1,0:T(8,128)S(1)} %get-tuple-element.18.cross_ref, f32[4,2,32,256]{3,2,1,0:T(8,128)S(1)} %get-tuple-element.19.mate_ref, ...), custom_call_target="tpu_custom_call" | custom-call | flops 1 | bytes 1 | tf_op jit(solution)/shard_map/cond/branch_1_fun/pallas_call | solution.py:529
  24.3 0.0 collective-permute-start
  24.3 1.2 %collective-permute-done.theirs_ref = f32[20,128]{1,0:T(8,128)S(1)} collective-permute-done((f32[20,128]{1,0:T(8,128)S(1)}, f32[20,128]{1,0:T(8,128)S(1)}, u32[]{:S(2)}, u32[]{:S(2)}) %collective-permute-start) | collective-permute-done | bytes 10272 | tf_op jit(solution)/shard_map/cond/branch_1_fun/ppermute | solution.py:424
  25.4 1.5 %collective-permute-start.1 = (f32[32,128]{1,0:T(8,128)S(1)}, f32[32,128]{1,0:T(8,128)S(1)}, u32[]{:S(2)}, u32[]{:S(2)}) collective-permute-start(f32[32,128]{1,0:T(8,128)S(1)} %branch_1_fun.5.mine_ref), channel_id=1, source_target_pairs={{0,2},{1,3},{2,0},{3,1},{4,6},{5,7},{6,4},{7,5},{8,10},{9,11},{10,... | collective-permute-start | bytes 49160 | tf_op jit(solution)/shard_map/cond/branch_1_fun/ppermute | solution.py:424
  26.9 2.2 %collective-permute-done.1.theirs_ref = f32[32,128]{1,0:T(8,128)S(1)} collective-permute-done((f32[32,128]{1,0:T(8,128)S(1)}, f32[32,128]{1,0:T(8,128)S(1)}, u32[]{:S(2)}, u32[]{:S(2)}) %collective-permute-start.1) | collective-permute-done | bytes 16416 | tf_op jit(solution)/shard_map/cond/branch_1_fun/ppermute | solution.py:424
  29.2 0.2 branch_1_fun.7
  29.4 0.2 branch_1_fun.6
  29.5 0.0 copy-start.3
  29.6 0.0 copy-start.2
  29.6 0.7 %copy-done.3 = f32[4,2,32,256]{3,2,1,0:T(8,128)} copy-done((f32[4,2,32,256]{3,2,1,0:T(8,128)}, f32[4,2,32,256]{3,2,1,0:T(8,128)S(1)}, u32[]{:S(2)}) %copy-start.3) | copy-done | bytes 262168
  30.2 0.0 collective-permute-done.8.beside_mate_ref
  30.3 0.0 copy-done.2
  30.3 0.9 %shard_map.64 = f32[2,2,32,1024]{3,2,1,0:T(8,128)} custom-call(f32[4,1024]{1,0:T(4,128)S(1)} %shard_map.60.flux_ref, f32[2,2,32,1024]{3,2,1,0:T(8,128)S(1)} %get-tuple-element.42.inside_ref, f32[2,32,1024]{2,1,0:T(8,128)S(1)} %collective-permute-done.8.beside_mate_ref, f32[2,32,1024]{2,1,0:T(8,128)S(1)} %collective-permute-done.9.beside_ends_ref, ...), custom_call_target="tpu_custom_call" | custom-call | flops 1 | bytes 1 | tf_op jit(solution)/shard_map/pallas_call | solution.py:556
  (13 shorter events, 0.1 us)
Async XLA Ops:
  0.6 14.2 %copy-start = (f32[2,2,32,1024]{3,2,1,0:T(8,128)S(1)}, f32[2,2,32,1024]{3,2,1,0:T(8,128)}, u32[]{:S(2)}) copy-start(f32[2,2,32,1024]{3,2,1,0:T(8,128)} %melt_ref.5) | copy-start | bytes 1572868
  0.6 20.6 %collective-permute-start.5 = (f32[4,2,32,256]{3,2,1,0:T(8,128)}, f32[4,2,32,256]{3,2,1,0:T(8,128)S(1)}, u32[]{:S(2)}, u32[]{:S(2)}) collective-permute-start(f32[4,2,32,256]{3,2,1,0:T(8,128)} %gas_hbm.1), channel_id=1, source_target_pairs={{0,4},{4,0},{8,12},{12,8},{16,20},{20,16},{24,28},{28,24},{1,5},{5... | collective-permute-start | bytes 786440 | tf_op jit(solution)/shard_map/ppermute | solution.py:424
  4.9 5.2 %collective-permute-start.3 = (f32[40,128]{1,0:T(8,128)S(1)}, f32[40,128]{1,0:T(8,128)S(1)}, u32[]{:S(2)}, u32[]{:S(2)}) collective-permute-start(f32[40,128]{1,0:T(8,128)S(1)} %get-tuple-element.38), channel_id=1, source_target_pairs={{0,1},{1,0},{2,3},{3,2},{4,5},{5,4},{6,7},{7,6},{8,9},{9,8},{10,11... | collective-permute-start | bytes 61448 | tf_op jit(solution)/shard_map/ppermute | solution.py:424
  4.9 5.2 %collective-permute-start.2 = (f32[40,128]{1,0:T(8,128)S(1)}, f32[40,128]{1,0:T(8,128)S(1)}, u32[]{:S(2)}, u32[]{:S(2)}) collective-permute-start(f32[40,128]{1,0:T(8,128)S(1)} %get-tuple-element.37), channel_id=1, source_target_pairs={{1,2},{3,0},{2,1},{0,3},{5,6},{7,4},{6,5},{4,7},{9,10},{11,8},{10,... | collective-permute-start | bytes 61448 | tf_op jit(solution)/shard_map/ppermute | solution.py:430
  6.5 14.7 %collective-permute-start.4 = (f32[4,2,32,256]{3,2,1,0:T(8,128)S(1)}, f32[4,2,32,256]{3,2,1,0:T(8,128)S(1)}, u32[]{:S(2)}, u32[]{:S(2)}) collective-permute-start(f32[4,2,32,256]{3,2,1,0:T(8,128)S(1)} %get-tuple-element.39), channel_id=1, source_target_pairs={{4,8},{12,16},{20,24},{28,0},{8,4},{16,12},{24,20},{0,28},{5,9},{1... | collective-permute-start | bytes 786440 | tf_op jit(solution)/shard_map/ppermute | solution.py:430
  10.1 4.7 %copy-start.1 = (s32[2,1024]{1,0:T(2,128)S(1)}, s32[2,1024]{1,0:T(2,128)}, u32[]{:S(2)}) copy-start(s32[2,1024]{1,0:T(2,128)} %mask_ref.3) | copy-start | bytes 24580
  10.1 4.7 %collective-permute-start.6 = (f32[8,128]{1,0:T(8,128)S(1)}, f32[8,128]{1,0:T(8,128)S(1)}, u32[]{:S(2)}, u32[]{:S(2)}) collective-permute-start(f32[8,128]{1,0:T(8,128)S(1)} %get-tuple-element.44), channel_id=1, source_target_pairs={{0,6},{4,2},{1,7},{5,3},{2,4},{6,0},{3,5},{7,1},{8,14},{12,10},{9,... | collective-permute-start | bytes 12296 | tf_op jit(solution)/shard_map/ppermute | solution.py:452
  10.2 10.3 %collective-permute-start.7 = (f32[8,128]{1,0:T(8,128)S(1)}, f32[8,128]{1,0:T(8,128)S(1)}, u32[]{:S(2)}, u32[]{:S(2)}) collective-permute-start(f32[8,128]{1,0:T(8,128)S(1)} %get-tuple-element.44), channel_id=1, source_target_pairs={{4,10},{8,6},{5,11},{9,7},{6,8},{10,4},{7,9},{11,5},{12,18},{16,14... | collective-permute-start | bytes 12296 | tf_op jit(solution)/shard_map/ppermute | solution.py:452
  15.3 15.0 %collective-permute-start.8 = (f32[2,32,1024]{2,1,0:T(8,128)S(1)}, f32[2,32,1024]{2,1,0:T(8,128)S(1)}, u32[]{:S(2)}, u32[]{:S(2)}) collective-permute-start(f32[2,32,1024]{2,1,0:T(8,128)S(1)} %get-tuple-element.43), channel_id=1, source_target_pairs={{0,4},{4,0},{8,12},{12,8},{16,20},{20,16},{24,28},{28,24},{1,5},{5... | collective-permute-start | bytes 786440 | tf_op jit(solution)/shard_map/ppermute | solution.py:424
  15.4 14.8 %collective-permute-start.9 = (f32[2,32,1024]{2,1,0:T(8,128)S(1)}, f32[2,32,1024]{2,1,0:T(8,128)S(1)}, u32[]{:S(2)}, u32[]{:S(2)}) collective-permute-start(f32[2,32,1024]{2,1,0:T(8,128)S(1)} %shard_map.62), channel_id=1, source_target_pairs={{0,28},{28,0},{1,29},{29,1},{2,30},{30,2},{3,31},{31,3}} | collective-permute-start | bytes 786440 | tf_op jit(solution)/shard_map/ppermute | solution.py:441
  20.5 9.7 %collective-permute-start.10 = (f32[2,32,1024]{2,1,0:T(8,128)S(1)}, f32[2,32,1024]{2,1,0:T(8,128)S(1)}, u32[]{:S(2)}, u32[]{:S(2)}) collective-permute-start(f32[2,32,1024]{2,1,0:T(8,128)S(1)} %shard_map.63), channel_id=1, source_target_pairs={{4,8},{12,16},{20,24},{8,4},{16,12},{24,20},{5,9},{13,17},{21,25},... | collective-permute-start | bytes 786440 | tf_op jit(solution)/shard_map/ppermute | solution.py:436
  24.3 1.2 %collective-permute-start = (f32[20,128]{1,0:T(8,128)S(1)}, f32[20,128]{1,0:T(8,128)S(1)}, u32[]{:S(2)}, u32[]{:S(2)}) collective-permute-start(f32[20,128]{1,0:T(8,128)S(1)} %get-tuple-element.25.mine_ref), channel_id=1, source_target_pairs={{0,1},{1,0},{2,3},{3,2},{4,5},{5,4},{6,7},{7,6},{8,9},{9,8},{10,11... | collective-permute-start | bytes 30728 | tf_op jit(solution)/shard_map/cond/branch_1_fun/ppermute | solution.py:424
  25.4 3.7 %collective-permute-start.1 = (f32[32,128]{1,0:T(8,128)S(1)}, f32[32,128]{1,0:T(8,128)S(1)}, u32[]{:S(2)}, u32[]{:S(2)}) collective-permute-start(f32[32,128]{1,0:T(8,128)S(1)} %branch_1_fun.5.mine_ref), channel_id=1, source_target_pairs={{0,2},{1,3},{2,0},{3,1},{4,6},{5,7},{6,4},{7,5},{8,10},{9,11},{10,... | collective-permute-start | bytes 49160 | tf_op jit(solution)/shard_map/cond/branch_1_fun/ppermute | solution.py:424
  29.5 0.7 %copy-start.3 = (f32[4,2,32,256]{3,2,1,0:T(8,128)}, f32[4,2,32,256]{3,2,1,0:T(8,128)S(1)}, u32[]{:S(2)}) copy-start(f32[4,2,32,256]{3,2,1,0:T(8,128)S(1)} %get-tuple-element.35) | copy-start | bytes 786436
  29.6 0.7 %copy-start.2 = (s32[2,1024]{1,0:T(2,128)S(1)}, s32[2,1024]{1,0:T(2,128)}, u32[]{:S(2)}) copy-start(s32[2,1024]{1,0:T(2,128)} %level_ref.1) | copy-start | bytes 24580

commit v5 on v4

--- a/solution.py
+++ b/solution.py
@@ -322,24 +322,25 @@
     flux_ref[cells:, :] = jnp.where(top, wall_ref[cells:, :], 0.0)
 
 
-def finish_melt(
+def finish(
+    rate_ref,
     flux_ref,
     inside_ref,
     beside_mate_ref,
-    beside_ends_ref,
-    beside_between_ref,
+    beside_cross_ref,
     level_ref,
+    gas_hbm,
     out_hbm,
     out_ref,
+    gas_sem,
     sems,
 ):
     components, cells, depth, width = inside_ref.shape
     position = lax.axis_index("sa")
-    place = lax.axis_index("gx")
-    even = place % 2 == 0
-    at_end = (place == 0) | (place == lax.axis_size("gx") - 1)
+    even = lax.axis_index("gx") % 2 == 0
     level_id = lax.broadcasted_iota(jnp.int32, (SUB, width), 0)
-    copies = []
+    copies = [pltpu.make_async_copy(rate_ref, gas_hbm, gas_sem)]
+    copies[0].start()
     for cell in range(cells):
         levels = level_ref[cell : cell + 1, :]
         for component in range(components):
@@ -349,11 +350,7 @@
                 rate = inside_ref[component, cell, here, :]
                 if cell in (0, cells - 1):
                     from_mate = beside_mate_ref[component, here, :]
-                    from_cross = jnp.where(
-                        at_end,
-                        beside_ends_ref[component, here, :],
-                        beside_between_ref[component, here, :],
-                    )
+                    from_cross = beside_cross_ref[component, here, :]
                     outer = jnp.where(even == (cell == 0), from_cross, from_mate)
                     rate = rate + share * outer
                 if block == 0:
@@ -372,10 +369,11 @@
         copy.wait()
 
 
-def melt_inside(devices, melt_ref, mate_ref, cross_ref, mask_ref, after_ref, part_ref, inside_ref):
+def melt_inside(devices, melt_ref, mate_ref, cross_ref, mask_ref, level_ref, after_ref, part_ref, inside_ref, levels_ref):
     components, cells, depth, width = melt_ref.shape
     assert cells > 1
     pack_melt(0, melt_ref, part_ref)
+    levels_ref[...] = level_ref[...]
     position = lax.axis_index("sa")
     even = position % 2 == 0
     top = position == 0
@@ -428,17 +426,6 @@
     count = lax.axis_size(axis)
     pairs = [(i, (i + 1) % count) for i in range(1, count, 2)]
     return lax.ppermute(source, axis, pairs + [(j, i) for i, j in pairs])
-
-
-def swap_between(source, axis):
-    count = lax.axis_size(axis)
-    pairs = [(i, i + 1) for i in range(1, count - 1, 2)]
-    return lax.ppermute(source, axis, pairs + [(j, i) for i, j in pairs])
-
-
-def swap_ends(source, axis):
-    last = lax.axis_size(axis) - 1
-    return lax.ppermute(source, axis, [(0, last), (last, 0)])
 
 
 def swap_aside(source, first, aside):
@@ -514,14 +501,15 @@
     passed = jnp.where(late == even, mate[:SUB], cross[:SUB]) if aside else halo
     halo_mate, halo_cross = swap_aside(passed, 0, aside), swap_aside(passed, 1, aside)
     part, whole = array(components, depth, width), array(components, cells, depth, width)
-    mate_part, inside = call(
-        functools.partial(melt_inside, devices), (part, whole), [VMEM] * 4 + [ANY]
-    )(melt, mate, cross, surface_mask, halo_mate)
-    ends_part = call(functools.partial(pack_melt, 1), part, [VMEM, ANY])(melt, halo_mate)
-    cross_part = call(functools.partial(pack_melt, 1), part, [VMEM, ANY])(melt, halo_cross)
+    levels = jax.ShapeDtypeStruct(melt_level.shape, jnp.int32)
+    mate_part, inside, levels = call(
+        functools.partial(melt_inside, devices), (part, whole, levels), [VMEM] * 5 + [ANY]
+    )(melt, mate, cross, surface_mask, melt_level, halo_mate)
+    cross_part = call(functools.partial(pack_melt, 1), part, [VMEM, ANY, ANY])(
+        melt, gas_mate, mate_part
+    )
     beside_mate = swap(mate_part, "gx", 1)
-    beside_ends = swap_ends(ends_part, "gx")
-    beside_between = swap_between(cross_part, "gx")
+    beside_cross = swap_across(cross_part, "gx")
 
     def gas_part(*arrays):
         wide = span + LANES
@@ -553,17 +541,17 @@
     flux = call(surface_flux, array(2 * cells, width), [VMEM, VMEM], flops=4000000000)(
         wall, surface_mask
     )
-    melt_rate = call(
-        finish_melt,
-        whole,
+    return call(
+        finish,
+        (array(4, cells, rows, span), whole),
         [VMEM] * 6,
         scratch=(
             pltpu.VMEM((components, cells, depth, width), jnp.float32),
+            pltpu.SemaphoreType.DMA,
             pltpu.SemaphoreType.DMA((components, cells)),
         ),
-        out_specs=HBM,
-    )(flux, inside, beside_mate, beside_ends, beside_between, melt_level)
-    return (gas_rate, melt_rate)
+        out_specs=(HBM, HBM),
+    )(gas_rate, flux, inside, beside_mate, beside_cross, levels)
 
 
 def solution(mesh):

time: 31.4 us -> 30.1 us (0.959)
  local copies, waits for them, and re-layouts: 0.7 us -> 0.02 us
  waiting for transfers between devices: 3.98 us -> 3.35 us
    ppermute x2 -> x0, starting transfers between devices: 5.76 us -> none  [the longest x1 5.08 us: swap_ends(): return lax.ppermute(source, axis, [(0, last), (last, 0)])]
    ppermute x5, starting transfers between devices: 4.68 us -> 7.72 us  [swap(): lax.ppermute(source, axis, [(i, i ^ mask) for i in range(lax.axis_size(ax...]
    ppermute x2 -> x3, starting transfers between devices: 5.15 us -> 7.88 us  [swap_across(): return lax.ppermute(source, axis, pairs + [(j, i) for i, j in pairs])]
    unnamed x8 -> x6, local copies, waits for them, and re-layouts: 0.7 us -> 0.02 us
    ppermute x5, waiting for transfers between devices: 3.42 us -> 2.9 us  [swap(): lax.ppermute(source, axis, [(i, i ^ mask) for i in range(lax.axis_size(ax...]
    pallas_call x4 -> x3, Pallas kernels: 1.41 us -> 1.45 us  [the longest x1 0.93 us: on_device(): call(finish, (array(4, cells, rows, span), whole), [VMEM] * 6, scratch=(p...]
  transfers between devices with their start and end apart: 11 -> 10, of which waited for: 3 -> 3; matrix products, arithmetic and copies ran while one was open for 0% -> 0% of each run, Pallas kernels for 16% -> 17%
where the time goes in v5:
time: 30.1 us; the launch traced here: 29.9 us
  starting transfers between devices  19.8 us (66%)
  Pallas kernels  5.96 us (20%)
  waiting for transfers between devices  3.35 us (11%)
  between operations  0.75 us (2%)
    ppermute x3, starting transfers between devices, swap_across(): return lax.ppermute(source, axis, pairs + [(j, i) for i, j in pairs])  7.88 us
    ppermute x5, starting transfers between devices, swap(): lax.ppermute(source, axis, [(i, i ^ mask) for i in range(lax.axis_size(ax...  7.72 us
    ppermute x2, starting transfers between devices, swap_aside(): return lax.ppermute(source, ('gx', 'sa'), pairs)  4.2 us
    pallas_call x1, Pallas kernels, gas_part(): call(germano, (array(4, cells, rows, span), array(4, cells, rows, span),...  2.97 us
    ppermute x5, waiting for transfers between devices, swap(): lax.ppermute(source, axis, [(i, i ^ mask) for i in range(lax.axis_size(ax...  2.9 us
    pallas_call x1, Pallas kernels, on_device(): call(pack_sides, (side, side, array(*gas.shape)), [HBM, HBM], scratch=(pl...  1.17 us
    pallas_call x1, Pallas kernels, on_device(): call(finish, (array(4, cells, rows, span), whole), [VMEM] * 6, scratch=(p...  0.93 us
  transfers between devices with their start and end apart: 10, of which 3 were waited for; matrix products, arithmetic and copies ran while one was open for 0% of the time, Pallas kernels for 17%

profile of v5, /device:TPU:0, one launch (start us, length us, event | category | flops | bytes accessed | tf_op | source)
XLA Modules:
  0.0 29.9 jit_solution(1195884413439219296)
XLA Ops:
  0.6 0.0 copy-start
  0.6 3.0 %collective-permute-start.5 = (f32[4,2,32,256]{3,2,1,0:T(8,128)}, f32[4,2,32,256]{3,2,1,0:T(8,128)S(1)}, u32[]{:S(2)}, u32[]{:S(2)}) collective-permute-start(f32[4,2,32,256]{3,2,1,0:T(8,128)} %gas_hbm.1), channel_id=1, source_target_pairs={{0,4},{4,0},{8,12},{12,8},{16,20},{20,16},{24,28},{28,24},{1,5},{5... | collective-permute-start | bytes 786440 | tf_op jit(solution)/shard_map/ppermute | solution.py:422
  3.7 1.2 %shard_map.59 = (f32[40,128]{1,0:T(8,128)S(1)}, f32[40,128]{1,0:T(8,128)S(1)}, f32[4,2,32,256]{3,2,1,0:T(8,128)S(1)}) custom-call(f32[4,2,32,256]{3,2,1,0:T(8,128)} %gas_hbm.1, f32[2,2,32,1024]{3,2,1,0:T(8,128)} %melt_ref.3), custom_call_target="tpu_custom_call" | custom-call | flops 1 | bytes 1 | tf_op jit(solution)/shard_map/pallas_call | solution.py:487
  4.9 0.7 %collective-permute-start.2 = (f32[40,128]{1,0:T(8,128)S(1)}, f32[40,128]{1,0:T(8,128)S(1)}, u32[]{:S(2)}, u32[]{:S(2)}) collective-permute-start(f32[40,128]{1,0:T(8,128)S(1)} %get-tuple-element.38), channel_id=1, source_target_pairs={{1,2},{3,0},{2,1},{0,3},{5,6},{7,4},{6,5},{4,7},{9,10},{11,8},{10,... | collective-permute-start | bytes 61448 | tf_op jit(solution)/shard_map/ppermute | solution.py:428
  5.6 1.0 %collective-permute-start.3 = (f32[40,128]{1,0:T(8,128)S(1)}, f32[40,128]{1,0:T(8,128)S(1)}, u32[]{:S(2)}, u32[]{:S(2)}) collective-permute-start(f32[40,128]{1,0:T(8,128)S(1)} %get-tuple-element.39), channel_id=1, source_target_pairs={{0,1},{1,0},{2,3},{3,2},{4,5},{5,4},{6,7},{7,6},{8,9},{9,8},{10,11... | collective-permute-start | bytes 61448 | tf_op jit(solution)/shard_map/ppermute | solution.py:422
  6.5 3.5 %collective-permute-start.4 = (f32[4,2,32,256]{3,2,1,0:T(8,128)S(1)}, f32[4,2,32,256]{3,2,1,0:T(8,128)S(1)}, u32[]{:S(2)}, u32[]{:S(2)}) collective-permute-start(f32[4,2,32,256]{3,2,1,0:T(8,128)S(1)} %get-tuple-element.40), channel_id=1, source_target_pairs={{4,8},{12,16},{20,24},{28,0},{8,4},{16,12},{24,20},{0,28},{5,9},{1... | collective-permute-start | bytes 786440 | tf_op jit(solution)/shard_map/ppermute | solution.py:428
  10.1 0.0 collective-permute-done.2.cross_ref
  10.1 0.0 collective-permute-done.3.mate_ref
  10.1 0.0 copy-start.1
  10.1 0.0 copy-start.2
  10.1 0.1 collective-permute-start.6
  10.2 4.1 %collective-permute-start.7 = (f32[8,128]{1,0:T(8,128)S(1)}, f32[8,128]{1,0:T(8,128)S(1)}, u32[]{:S(2)}, u32[]{:S(2)}) collective-permute-start(f32[8,128]{1,0:T(8,128)S(1)} %get-tuple-element.46), channel_id=1, source_target_pairs={{4,10},{8,6},{5,11},{9,7},{6,8},{10,4},{7,9},{11,5},{12,18},{16,14... | collective-permute-start | bytes 12296 | tf_op jit(solution)/shard_map/ppermute | solution.py:439
  14.3 0.4 %collective-permute-done.6.after_ref = f32[8,128]{1,0:T(8,128)S(1)} collective-permute-done((f32[8,128]{1,0:T(8,128)S(1)}, f32[8,128]{1,0:T(8,128)S(1)}, u32[]{:S(2)}, u32[]{:S(2)}) %collective-permute-start.6) | collective-permute-done | bytes 4128 | tf_op jit(solution)/shard_map/ppermute | solution.py:439
  14.8 0.0 copy-done
  14.8 0.0 copy-done.1
  14.8 0.5 %shard_map.61 = (f32[2,32,1024]{2,1,0:T(8,128)S(1)}, f32[2,2,32,1024]{3,2,1,0:T(8,128)S(1)}, s32[2,1024]{1,0:T(2,128)S(1)}) custom-call(f32[2,2,32,1024]{3,2,1,0:T(8,128)S(1)} %copy-done, f32[40,128]{1,0:T(8,128)S(1)} %collective-permute-done.3.mate_ref, f32[40,128]{1,0:T(8,128)S(1)} %collective-permute-done.2.cross_ref, s32[2,1024]{1,0:T(2,128)S(1)} %copy-done.2, ...), custom_call_target="tpu_custom_call" | custom-call | flops 1 | bytes 1 | tf_op jit(solution)/shard_map/pallas_call | solution.py:505
  15.3 0.1 collective-permute-start.8
  15.4 0.0 collective-permute-done.5.refs_0_
  15.4 3.6 %collective-permute-start.9 = (f32[2,32,1024]{2,1,0:T(8,128)S(1)}, f32[2,32,1024]{2,1,0:T(8,128)S(1)}, u32[]{:S(2)}, u32[]{:S(2)}) collective-permute-start(f32[2,32,1024]{2,1,0:T(8,128)S(1)} %shard_map.62), channel_id=1, source_target_pairs={{4,8},{12,16},{20,24},{28,0},{8,4},{16,12},{24,20},{0,28},{5,9},{1... | collective-permute-start | bytes 786440 | tf_op jit(solution)/shard_map/ppermute | solution.py:428
  19.1 0.0 collective-permute-done.7
  19.1 0.0 collective-permute-done.4
  19.1 9.9 %conditional.1 = (f32[4,2,32,256]{3,2,1,0:T(8,128)S(1)}, f32[4,1024]{1,0:T(4,128)S(1)}) conditional(s32[]{:T(128)} %convert_element_type.3, () %tuple.15, (pred[8,128]{1,0:T(8,128)(4,1)S(1)}, f32[8,128]{1,0:T(8,128)S(1)}, f32[8,128]{1,0:T(8,128)S(1)}, f32[4,2,32,256]{3,2,1,0:T(8,128)S(1)}, f32[4,2,32,256]{3,2,1,0:T(8,128)S(1)}, ...), branch_computations={%region_0.1_spmd, %region_1.2_spmd} | conditional | flops 1028 | bytes 278552 | solution.py:459
  19.1 3.0 %branch_1_fun.4 = (f32[4,2,32,256]{3,2,1,0:T(8,128)S(1)}, f32[4,2,32,256]{3,2,1,0:T(8,128)S(1)}, f32[20,128]{1,0:T(8,128)S(1)}) custom-call(f32[4,2,32,256]{3,2,1,0:T(8,128)S(1)} %get-tuple-element.17.own_ref, f32[4,2,32,256]{3,2,1,0:T(8,128)S(1)} %get-tuple-element.18.cross_ref, f32[4,2,32,256]{3,2,1,0:T(8,128)S(1)} %get-tuple-element.19.mate_ref, ...), custom_call_target="tpu_custom_call" | custom-call | flops 1 | bytes 1 | tf_op jit(solution)/shard_map/cond/branch_1_fun/pallas_call | solution.py:517
  22.0 0.0 collective-permute-start
  22.1 1.2 %collective-permute-done.theirs_ref = f32[20,128]{1,0:T(8,128)S(1)} collective-permute-done((f32[20,128]{1,0:T(8,128)S(1)}, f32[20,128]{1,0:T(8,128)S(1)}, u32[]{:S(2)}, u32[]{:S(2)}) %collective-permute-start) | collective-permute-done | bytes 10272 | tf_op jit(solution)/shard_map/cond/branch_1_fun/ppermute | solution.py:422
  23.2 3.6 %collective-permute-start.1 = (f32[32,128]{1,0:T(8,128)S(1)}, f32[32,128]{1,0:T(8,128)S(1)}, u32[]{:S(2)}, u32[]{:S(2)}) collective-permute-start(f32[32,128]{1,0:T(8,128)S(1)} %branch_1_fun.5.mine_ref), channel_id=1, source_target_pairs={{0,2},{1,3},{2,0},{3,1},{4,6},{5,7},{6,4},{7,5},{8,10},{9,11},{10,... | collective-permute-start | bytes 49160 | tf_op jit(solution)/shard_map/cond/branch_1_fun/ppermute | solution.py:422
  26.9 1.7 %collective-permute-done.1.theirs_ref = f32[32,128]{1,0:T(8,128)S(1)} collective-permute-done((f32[32,128]{1,0:T(8,128)S(1)}, f32[32,128]{1,0:T(8,128)S(1)}, u32[]{:S(2)}, u32[]{:S(2)}) %collective-permute-start.1) | collective-permute-done | bytes 16416 | tf_op jit(solution)/shard_map/cond/branch_1_fun/ppermute | solution.py:422
  28.6 0.2 branch_1_fun.7
  28.8 0.2 branch_1_fun.6
  29.0 0.0 collective-permute-done.8.beside_mate_ref
  29.0 0.0 collective-permute-done.9.beside_cross_ref
  29.0 0.9 %shard_map.63 = (f32[4,2,32,256]{3,2,1,0:T(8,128)}, f32[2,2,32,1024]{3,2,1,0:T(8,128)}) custom-call(f32[4,2,32,256]{3,2,1,0:T(8,128)S(1)} %get-tuple-element.41.rate_ref, f32[4,1024]{1,0:T(4,128)S(1)} %shard_map.60.flux_ref, f32[2,2,32,1024]{3,2,1,0:T(8,128)S(1)} %get-tuple-element.43.inside_ref, f32[2,32,1024]{2,1,0:T(8,128)S(1)} %collective-permute-done.8.beside_mate_ref, ...), custom_call_target="tpu_custom_call" | custom-call | flops 1 | bytes 1 | tf_op jit(solution)/shard_map/pallas_call | solution.py:544
  (8 shorter events, 0.1 us)
Async XLA Ops:
  0.6 14.2 %copy-start = (f32[2,2,32,1024]{3,2,1,0:T(8,128)S(1)}, f32[2,2,32,1024]{3,2,1,0:T(8,128)}, u32[]{:S(2)}) copy-start(f32[2,2,32,1024]{3,2,1,0:T(8,128)} %melt_ref.3) | copy-start | bytes 1572868
  0.6 14.8 %collective-permute-start.5 = (f32[4,2,32,256]{3,2,1,0:T(8,128)}, f32[4,2,32,256]{3,2,1,0:T(8,128)S(1)}, u32[]{:S(2)}, u32[]{:S(2)}) collective-permute-start(f32[4,2,32,256]{3,2,1,0:T(8,128)} %gas_hbm.1), channel_id=1, source_target_pairs={{0,4},{4,0},{8,12},{12,8},{16,20},{20,16},{24,28},{28,24},{1,5},{5... | collective-permute-start | bytes 786440 | tf_op jit(solution)/shard_map/ppermute | solution.py:422
  4.9 5.2 %collective-permute-start.2 = (f32[40,128]{1,0:T(8,128)S(1)}, f32[40,128]{1,0:T(8,128)S(1)}, u32[]{:S(2)}, u32[]{:S(2)}) collective-permute-start(f32[40,128]{1,0:T(8,128)S(1)} %get-tuple-element.38), channel_id=1, source_target_pairs={{1,2},{3,0},{2,1},{0,3},{5,6},{7,4},{6,5},{4,7},{9,10},{11,8},{10,... | collective-permute-start | bytes 61448 | tf_op jit(solution)/shard_map/ppermute | solution.py:428
  5.6 4.5 %collective-permute-start.3 = (f32[40,128]{1,0:T(8,128)S(1)}, f32[40,128]{1,0:T(8,128)S(1)}, u32[]{:S(2)}, u32[]{:S(2)}) collective-permute-start(f32[40,128]{1,0:T(8,128)S(1)} %get-tuple-element.39), channel_id=1, source_target_pairs={{0,1},{1,0},{2,3},{3,2},{4,5},{5,4},{6,7},{7,6},{8,9},{9,8},{10,11... | collective-permute-start | bytes 61448 | tf_op jit(solution)/shard_map/ppermute | solution.py:422
  6.5 12.5 %collective-permute-start.4 = (f32[4,2,32,256]{3,2,1,0:T(8,128)S(1)}, f32[4,2,32,256]{3,2,1,0:T(8,128)S(1)}, u32[]{:S(2)}, u32[]{:S(2)}) collective-permute-start(f32[4,2,32,256]{3,2,1,0:T(8,128)S(1)} %get-tuple-element.40), channel_id=1, source_target_pairs={{4,8},{12,16},{20,24},{28,0},{8,4},{16,12},{24,20},{0,28},{5,9},{1... | collective-permute-start | bytes 786440 | tf_op jit(solution)/shard_map/ppermute | solution.py:428
  10.1 4.7 %copy-start.1 = (s32[2,1024]{1,0:T(2,128)S(1)}, s32[2,1024]{1,0:T(2,128)}, u32[]{:S(2)}) copy-start(s32[2,1024]{1,0:T(2,128)} %level_ref.1) | copy-start | bytes 24580
  10.1 4.7 %copy-start.2 = (s32[2,1024]{1,0:T(2,128)S(1)}, s32[2,1024]{1,0:T(2,128)}, u32[]{:S(2)}) copy-start(s32[2,1024]{1,0:T(2,128)} %mask_ref.3) | copy-start | bytes 24580
  10.1 4.7 %collective-permute-start.6 = (f32[8,128]{1,0:T(8,128)S(1)}, f32[8,128]{1,0:T(8,128)S(1)}, u32[]{:S(2)}, u32[]{:S(2)}) collective-permute-start(f32[8,128]{1,0:T(8,128)S(1)} %get-tuple-element.46), channel_id=1, source_target_pairs={{0,6},{4,2},{1,7},{5,3},{2,4},{6,0},{3,5},{7,1},{8,14},{12,10},{9,... | collective-permute-start | bytes 12296 | tf_op jit(solution)/shard_map/ppermute | solution.py:439
  10.2 8.8 %collective-permute-start.7 = (f32[8,128]{1,0:T(8,128)S(1)}, f32[8,128]{1,0:T(8,128)S(1)}, u32[]{:S(2)}, u32[]{:S(2)}) collective-permute-start(f32[8,128]{1,0:T(8,128)S(1)} %get-tuple-element.46), channel_id=1, source_target_pairs={{4,10},{8,6},{5,11},{9,7},{6,8},{10,4},{7,9},{11,5},{12,18},{16,14... | collective-permute-start | bytes 12296 | tf_op jit(solution)/shard_map/ppermute | solution.py:439
  15.3 13.7 %collective-permute-start.8 = (f32[2,32,1024]{2,1,0:T(8,128)S(1)}, f32[2,32,1024]{2,1,0:T(8,128)S(1)}, u32[]{:S(2)}, u32[]{:S(2)}) collective-permute-start(f32[2,32,1024]{2,1,0:T(8,128)S(1)} %get-tuple-element.44.refs_1_), channel_id=1, source_target_pairs={{0,4},{4,0},{8,12},{12,8},{16,20},{20,16},{24,28},{28,24},{1,5},{5... | collective-permute-start | bytes 786440 | tf_op jit(solution)/shard_map/ppermute | solution.py:422
  15.4 13.6 %collective-permute-start.9 = (f32[2,32,1024]{2,1,0:T(8,128)S(1)}, f32[2,32,1024]{2,1,0:T(8,128)S(1)}, u32[]{:S(2)}, u32[]{:S(2)}) collective-permute-start(f32[2,32,1024]{2,1,0:T(8,128)S(1)} %shard_map.62), channel_id=1, source_target_pairs={{4,8},{12,16},{20,24},{28,0},{8,4},{16,12},{24,20},{0,28},{5,9},{1... | collective-permute-start | bytes 786440 | tf_op jit(solution)/shard_map/ppermute | solution.py:428
  22.0 1.2 %collective-permute-start = (f32[20,128]{1,0:T(8,128)S(1)}, f32[20,128]{1,0:T(8,128)S(1)}, u32[]{:S(2)}, u32[]{:S(2)}) collective-permute-start(f32[20,128]{1,0:T(8,128)S(1)} %get-tuple-element.25.mine_ref), channel_id=1, source_target_pairs={{0,1},{1,0},{2,3},{3,2},{4,5},{5,4},{6,7},{7,6},{8,9},{9,8},{10,11... | collective-permute-start | bytes 30728 | tf_op jit(solution)/shard_map/cond/branch_1_fun/ppermute | solution.py:422
  23.2 5.4 %collective-permute-start.1 = (f32[32,128]{1,0:T(8,128)S(1)}, f32[32,128]{1,0:T(8,128)S(1)}, u32[]{:S(2)}, u32[]{:S(2)}) collective-permute-start(f32[32,128]{1,0:T(8,128)S(1)} %branch_1_fun.5.mine_ref), channel_id=1, source_target_pairs={{0,2},{1,3},{2,0},{3,1},{4,6},{5,7},{6,4},{7,5},{8,10},{9,11},{10,... | collective-permute-start | bytes 49160 | tf_op jit(solution)/shard_map/cond/branch_1_fun/ppermute | solution.py:422

commit v6 on v5

--- a/solution.py
+++ b/solution.py
@@ -150,7 +150,7 @@
                 coarse[i, component, place, :] = binomial(pair[i] + pair[i + 1])
         return carry
 
-    lax.fori_loop(0, rows // SUB, filter_block, 0)
+    lax.fori_loop(0, rows // SUB, filter_block, 0, unroll=2)
     for i in range(cells + 2):
         for component in range(3):
             coarse[i, component, SUB - 1 : SUB, :] = -coarse[i, component, SUB : SUB + 1, :]

time: 30.1 us -> 29.9 us (level)
  transfers between devices with their start and end apart: 10 -> 10, of which waited for: 3 -> 3; matrix products, arithmetic and copies ran while one was open for 0% -> 0% of each run, Pallas kernels for 17% -> 16%
where the time goes in v6:
time: 29.9 us; the launch traced here: 29.8 us
  starting transfers between devices  19.8 us (66%)
  Pallas kernels  5.82 us (19%)
  waiting for transfers between devices  3.38 us (11%)
  between operations  0.73 us (2%)
    ppermute x3, starting transfers between devices, swap_across(): return lax.ppermute(source, axis, pairs + [(j, i) for i, j in pairs])  7.88 us
    ppermute x5, starting transfers between devices, swap(): lax.ppermute(source, axis, [(i, i ^ mask) for i in range(lax.axis_size(ax...  7.71 us
    ppermute x2, starting transfers between devices, swap_aside(): return lax.ppermute(source, ('gx', 'sa'), pairs)  4.2 us
    ppermute x5, waiting for transfers between devices, swap(): lax.ppermute(source, axis, [(i, i ^ mask) for i in range(lax.axis_size(ax...  2.92 us
    pallas_call x1, Pallas kernels, gas_part(): call(germano, (array(4, cells, rows, span), array(4, cells, rows, span),...  2.83 us
    pallas_call x1, Pallas kernels, on_device(): call(pack_sides, (side, side, array(*gas.shape)), [HBM, HBM], scratch=(pl...  1.17 us
    pallas_call x1, Pallas kernels, on_device(): call(finish, (array(4, cells, rows, span), whole), [VMEM] * 6, scratch=(p...  0.93 us
  transfers between devices with their start and end apart: 10, of which 3 were waited for; matrix products, arithmetic and copies ran while one was open for 0% of the time, Pallas kernels for 16%

profile of v6, /device:TPU:0, one launch (start us, length us, event | category | flops | bytes accessed | tf_op | source)
XLA Modules:
  0.0 29.8 jit_solution(16515454969614731350)
XLA Ops:
  0.6 0.0 copy-start
  0.6 3.0 %collective-permute-start.5 = (f32[4,2,32,256]{3,2,1,0:T(8,128)}, f32[4,2,32,256]{3,2,1,0:T(8,128)S(1)}, u32[]{:S(2)}, u32[]{:S(2)}) collective-permute-start(f32[4,2,32,256]{3,2,1,0:T(8,128)} %gas_hbm.1), channel_id=1, source_target_pairs={{0,4},{4,0},{8,12},{12,8},{16,20},{20,16},{24,28},{28,24},{1,5},{5... | collective-permute-start | bytes 786440 | tf_op jit(solution)/shard_map/ppermute | solution.py:422
  3.7 1.2 %shard_map.59 = (f32[40,128]{1,0:T(8,128)S(1)}, f32[40,128]{1,0:T(8,128)S(1)}, f32[4,2,32,256]{3,2,1,0:T(8,128)S(1)}) custom-call(f32[4,2,32,256]{3,2,1,0:T(8,128)} %gas_hbm.1, f32[2,2,32,1024]{3,2,1,0:T(8,128)} %melt_ref.3), custom_call_target="tpu_custom_call" | custom-call | flops 1 | bytes 1 | tf_op jit(solution)/shard_map/pallas_call | solution.py:487
  4.9 0.7 %collective-permute-start.2 = (f32[40,128]{1,0:T(8,128)S(1)}, f32[40,128]{1,0:T(8,128)S(1)}, u32[]{:S(2)}, u32[]{:S(2)}) collective-permute-start(f32[40,128]{1,0:T(8,128)S(1)} %get-tuple-element.38), channel_id=1, source_target_pairs={{1,2},{3,0},{2,1},{0,3},{5,6},{7,4},{6,5},{4,7},{9,10},{11,8},{10,... | collective-permute-start | bytes 61448 | tf_op jit(solution)/shard_map/ppermute | solution.py:428
  5.6 1.0 %collective-permute-start.3 = (f32[40,128]{1,0:T(8,128)S(1)}, f32[40,128]{1,0:T(8,128)S(1)}, u32[]{:S(2)}, u32[]{:S(2)}) collective-permute-start(f32[40,128]{1,0:T(8,128)S(1)} %get-tuple-element.39), channel_id=1, source_target_pairs={{0,1},{1,0},{2,3},{3,2},{4,5},{5,4},{6,7},{7,6},{8,9},{9,8},{10,11... | collective-permute-start | bytes 61448 | tf_op jit(solution)/shard_map/ppermute | solution.py:422
  6.5 3.5 %collective-permute-start.4 = (f32[4,2,32,256]{3,2,1,0:T(8,128)S(1)}, f32[4,2,32,256]{3,2,1,0:T(8,128)S(1)}, u32[]{:S(2)}, u32[]{:S(2)}) collective-permute-start(f32[4,2,32,256]{3,2,1,0:T(8,128)S(1)} %get-tuple-element.40), channel_id=1, source_target_pairs={{4,8},{12,16},{20,24},{28,0},{8,4},{16,12},{24,20},{0,28},{5,9},{1... | collective-permute-start | bytes 786440 | tf_op jit(solution)/shard_map/ppermute | solution.py:428
  10.1 0.0 collective-permute-done.2.cross_ref
  10.1 0.0 collective-permute-done.3.mate_ref
  10.1 0.0 copy-start.1
  10.1 0.0 copy-start.2
  10.1 0.1 collective-permute-start.6
  10.2 4.1 %collective-permute-start.7 = (f32[8,128]{1,0:T(8,128)S(1)}, f32[8,128]{1,0:T(8,128)S(1)}, u32[]{:S(2)}, u32[]{:S(2)}) collective-permute-start(f32[8,128]{1,0:T(8,128)S(1)} %get-tuple-element.46), channel_id=1, source_target_pairs={{4,10},{8,6},{5,11},{9,7},{6,8},{10,4},{7,9},{11,5},{12,18},{16,14... | collective-permute-start | bytes 12296 | tf_op jit(solution)/shard_map/ppermute | solution.py:439
  14.3 0.4 %collective-permute-done.6.after_ref = f32[8,128]{1,0:T(8,128)S(1)} collective-permute-done((f32[8,128]{1,0:T(8,128)S(1)}, f32[8,128]{1,0:T(8,128)S(1)}, u32[]{:S(2)}, u32[]{:S(2)}) %collective-permute-start.6) | collective-permute-done | bytes 4128 | tf_op jit(solution)/shard_map/ppermute | solution.py:439
  14.8 0.0 copy-done
  14.8 0.0 copy-done.2
  14.8 0.5 %shard_map.61 = (f32[2,32,1024]{2,1,0:T(8,128)S(1)}, f32[2,2,32,1024]{3,2,1,0:T(8,128)S(1)}, s32[2,1024]{1,0:T(2,128)S(1)}) custom-call(f32[2,2,32,1024]{3,2,1,0:T(8,128)S(1)} %copy-done, f32[40,128]{1,0:T(8,128)S(1)} %collective-permute-done.3.mate_ref, f32[40,128]{1,0:T(8,128)S(1)} %collective-permute-done.2.cross_ref, s32[2,1024]{1,0:T(2,128)S(1)} %copy-done.2, ...), custom_call_target="tpu_custom_call" | custom-call | flops 1 | bytes 1 | tf_op jit(solution)/shard_map/pallas_call | solution.py:505
  15.3 0.1 collective-permute-start.8
  15.4 0.0 collective-permute-done.5.refs_0_
  15.4 3.6 %collective-permute-start.9 = (f32[2,32,1024]{2,1,0:T(8,128)S(1)}, f32[2,32,1024]{2,1,0:T(8,128)S(1)}, u32[]{:S(2)}, u32[]{:S(2)}) collective-permute-start(f32[2,32,1024]{2,1,0:T(8,128)S(1)} %shard_map.62), channel_id=1, source_target_pairs={{4,8},{12,16},{20,24},{28,0},{8,4},{16,12},{24,20},{0,28},{5,9},{1... | collective-permute-start | bytes 786440 | tf_op jit(solution)/shard_map/ppermute | solution.py:428
  19.1 0.0 collective-permute-done.7
  19.1 0.0 collective-permute-done.4
  19.1 9.7 %conditional.1 = (f32[4,2,32,256]{3,2,1,0:T(8,128)S(1)}, f32[4,1024]{1,0:T(4,128)S(1)}) conditional(s32[]{:T(128)} %convert_element_type.3, () %tuple.15, (pred[8,128]{1,0:T(8,128)(4,1)S(1)}, f32[8,128]{1,0:T(8,128)S(1)}, f32[8,128]{1,0:T(8,128)S(1)}, f32[4,2,32,256]{3,2,1,0:T(8,128)S(1)}, f32[4,2,32,256]{3,2,1,0:T(8,128)S(1)}, ...), branch_computations={%region_0.1_spmd, %region_1.2_spmd} | conditional | flops 1028 | bytes 278552 | solution.py:459
  19.1 2.8 %branch_1_fun.4 = (f32[4,2,32,256]{3,2,1,0:T(8,128)S(1)}, f32[4,2,32,256]{3,2,1,0:T(8,128)S(1)}, f32[20,128]{1,0:T(8,128)S(1)}) custom-call(f32[4,2,32,256]{3,2,1,0:T(8,128)S(1)} %get-tuple-element.17.own_ref, f32[4,2,32,256]{3,2,1,0:T(8,128)S(1)} %get-tuple-element.18.cross_ref, f32[4,2,32,256]{3,2,1,0:T(8,128)S(1)} %get-tuple-element.19.mate_ref, ...), custom_call_target="tpu_custom_call" | custom-call | flops 1 | bytes 1 | tf_op jit(solution)/shard_map/cond/branch_1_fun/pallas_call | solution.py:517
  21.9 0.0 collective-permute-start
  21.9 1.2 %collective-permute-done.theirs_ref = f32[20,128]{1,0:T(8,128)S(1)} collective-permute-done((f32[20,128]{1,0:T(8,128)S(1)}, f32[20,128]{1,0:T(8,128)S(1)}, u32[]{:S(2)}, u32[]{:S(2)}) %collective-permute-start) | collective-permute-done | bytes 10272 | tf_op jit(solution)/shard_map/cond/branch_1_fun/ppermute | solution.py:422
  23.1 3.6 %collective-permute-start.1 = (f32[32,128]{1,0:T(8,128)S(1)}, f32[32,128]{1,0:T(8,128)S(1)}, u32[]{:S(2)}, u32[]{:S(2)}) collective-permute-start(f32[32,128]{1,0:T(8,128)S(1)} %branch_1_fun.5.mine_ref), channel_id=1, source_target_pairs={{0,2},{1,3},{2,0},{3,1},{4,6},{5,7},{6,4},{7,5},{8,10},{9,11},{10,... | collective-permute-start | bytes 49160 | tf_op jit(solution)/shard_map/cond/branch_1_fun/ppermute | solution.py:422
  26.7 1.7 %collective-permute-done.1.theirs_ref = f32[32,128]{1,0:T(8,128)S(1)} collective-permute-done((f32[32,128]{1,0:T(8,128)S(1)}, f32[32,128]{1,0:T(8,128)S(1)}, u32[]{:S(2)}, u32[]{:S(2)}) %collective-permute-start.1) | collective-permute-done | bytes 16416 | tf_op jit(solution)/shard_map/cond/branch_1_fun/ppermute | solution.py:422
  28.4 0.2 branch_1_fun.7
  28.6 0.2 branch_1_fun.6
  28.8 0.0 collective-permute-done.8.beside_mate_ref
  28.8 0.0 collective-permute-done.9.beside_cross_ref
  28.9 0.9 %shard_map.63 = (f32[4,2,32,256]{3,2,1,0:T(8,128)}, f32[2,2,32,1024]{3,2,1,0:T(8,128)}) custom-call(f32[4,2,32,256]{3,2,1,0:T(8,128)S(1)} %get-tuple-element.41.rate_ref, f32[4,1024]{1,0:T(4,128)S(1)} %shard_map.60.flux_ref, f32[2,2,32,1024]{3,2,1,0:T(8,128)S(1)} %get-tuple-element.43.inside_ref, f32[2,32,1024]{2,1,0:T(8,128)S(1)} %collective-permute-done.8.beside_mate_ref, ...), custom_call_target="tpu_custom_call" | custom-call | flops 1 | bytes 1 | tf_op jit(solution)/shard_map/pallas_call | solution.py:544
  (8 shorter events, 0.1 us)
Async XLA Ops:
  0.6 14.2 %copy-start = (f32[2,2,32,1024]{3,2,1,0:T(8,128)S(1)}, f32[2,2,32,1024]{3,2,1,0:T(8,128)}, u32[]{:S(2)}) copy-start(f32[2,2,32,1024]{3,2,1,0:T(8,128)} %melt_ref.3) | copy-start | bytes 1572868
  0.6 14.8 %collective-permute-start.5 = (f32[4,2,32,256]{3,2,1,0:T(8,128)}, f32[4,2,32,256]{3,2,1,0:T(8,128)S(1)}, u32[]{:S(2)}, u32[]{:S(2)}) collective-permute-start(f32[4,2,32,256]{3,2,1,0:T(8,128)} %gas_hbm.1), channel_id=1, source_target_pairs={{0,4},{4,0},{8,12},{12,8},{16,20},{20,16},{24,28},{28,24},{1,5},{5... | collective-permute-start | bytes 786440 | tf_op jit(solution)/shard_map/ppermute | solution.py:422
  4.9 5.2 %collective-permute-start.2 = (f32[40,128]{1,0:T(8,128)S(1)}, f32[40,128]{1,0:T(8,128)S(1)}, u32[]{:S(2)}, u32[]{:S(2)}) collective-permute-start(f32[40,128]{1,0:T(8,128)S(1)} %get-tuple-element.38), channel_id=1, source_target_pairs={{1,2},{3,0},{2,1},{0,3},{5,6},{7,4},{6,5},{4,7},{9,10},{11,8},{10,... | collective-permute-start | bytes 61448 | tf_op jit(solution)/shard_map/ppermute | solution.py:428
  5.6 4.5 %collective-permute-start.3 = (f32[40,128]{1,0:T(8,128)S(1)}, f32[40,128]{1,0:T(8,128)S(1)}, u32[]{:S(2)}, u32[]{:S(2)}) collective-permute-start(f32[40,128]{1,0:T(8,128)S(1)} %get-tuple-element.39), channel_id=1, source_target_pairs={{0,1},{1,0},{2,3},{3,2},{4,5},{5,4},{6,7},{7,6},{8,9},{9,8},{10,11... | collective-permute-start | bytes 61448 | tf_op jit(solution)/shard_map/ppermute | solution.py:422
  6.5 12.5 %collective-permute-start.4 = (f32[4,2,32,256]{3,2,1,0:T(8,128)S(1)}, f32[4,2,32,256]{3,2,1,0:T(8,128)S(1)}, u32[]{:S(2)}, u32[]{:S(2)}) collective-permute-start(f32[4,2,32,256]{3,2,1,0:T(8,128)S(1)} %get-tuple-element.40), channel_id=1, source_target_pairs={{4,8},{12,16},{20,24},{28,0},{8,4},{16,12},{24,20},{0,28},{5,9},{1... | collective-permute-start | bytes 786440 | tf_op jit(solution)/shard_map/ppermute | solution.py:428
  10.1 4.7 %copy-start.1 = (s32[2,1024]{1,0:T(2,128)S(1)}, s32[2,1024]{1,0:T(2,128)}, u32[]{:S(2)}) copy-start(s32[2,1024]{1,0:T(2,128)} %level_ref.1) | copy-start | bytes 24580
  10.1 4.7 %copy-start.2 = (s32[2,1024]{1,0:T(2,128)S(1)}, s32[2,1024]{1,0:T(2,128)}, u32[]{:S(2)}) copy-start(s32[2,1024]{1,0:T(2,128)} %mask_ref.3) | copy-start | bytes 24580
  10.1 4.7 %collective-permute-start.6 = (f32[8,128]{1,0:T(8,128)S(1)}, f32[8,128]{1,0:T(8,128)S(1)}, u32[]{:S(2)}, u32[]{:S(2)}) collective-permute-start(f32[8,128]{1,0:T(8,128)S(1)} %get-tuple-element.46), channel_id=1, source_target_pairs={{0,6},{4,2},{1,7},{5,3},{2,4},{6,0},{3,5},{7,1},{8,14},{12,10},{9,... | collective-permute-start | bytes 12296 | tf_op jit(solution)/shard_map/ppermute | solution.py:439
  10.2 8.8 %collective-permute-start.7 = (f32[8,128]{1,0:T(8,128)S(1)}, f32[8,128]{1,0:T(8,128)S(1)}, u32[]{:S(2)}, u32[]{:S(2)}) collective-permute-start(f32[8,128]{1,0:T(8,128)S(1)} %get-tuple-element.46), channel_id=1, source_target_pairs={{4,10},{8,6},{5,11},{9,7},{6,8},{10,4},{7,9},{11,5},{12,18},{16,14... | collective-permute-start | bytes 12296 | tf_op jit(solution)/shard_map/ppermute | solution.py:439
  15.3 13.5 %collective-permute-start.8 = (f32[2,32,1024]{2,1,0:T(8,128)S(1)}, f32[2,32,1024]{2,1,0:T(8,128)S(1)}, u32[]{:S(2)}, u32[]{:S(2)}) collective-permute-start(f32[2,32,1024]{2,1,0:T(8,128)S(1)} %get-tuple-element.44.refs_1_), channel_id=1, source_target_pairs={{0,4},{4,0},{8,12},{12,8},{16,20},{20,16},{24,28},{28,24},{1,5},{5... | collective-permute-start | bytes 786440 | tf_op jit(solution)/shard_map/ppermute | solution.py:422
  15.4 13.4 %collective-permute-start.9 = (f32[2,32,1024]{2,1,0:T(8,128)S(1)}, f32[2,32,1024]{2,1,0:T(8,128)S(1)}, u32[]{:S(2)}, u32[]{:S(2)}) collective-permute-start(f32[2,32,1024]{2,1,0:T(8,128)S(1)} %shard_map.62), channel_id=1, source_target_pairs={{4,8},{12,16},{20,24},{28,0},{8,4},{16,12},{24,20},{0,28},{5,9},{1... | collective-permute-start | bytes 786440 | tf_op jit(solution)/shard_map/ppermute | solution.py:428
  21.9 1.2 %collective-permute-start = (f32[20,128]{1,0:T(8,128)S(1)}, f32[20,128]{1,0:T(8,128)S(1)}, u32[]{:S(2)}, u32[]{:S(2)}) collective-permute-start(f32[20,128]{1,0:T(8,128)S(1)} %get-tuple-element.25.mine_ref), channel_id=1, source_target_pairs={{0,1},{1,0},{2,3},{3,2},{4,5},{5,4},{6,7},{7,6},{8,9},{9,8},{10,11... | collective-permute-start | bytes 30728 | tf_op jit(solution)/shard_map/cond/branch_1_fun/ppermute | solution.py:422
  23.1 5.4 %collective-permute-start.1 = (f32[32,128]{1,0:T(8,128)S(1)}, f32[32,128]{1,0:T(8,128)S(1)}, u32[]{:S(2)}, u32[]{:S(2)}) collective-permute-start(f32[32,128]{1,0:T(8,128)S(1)} %branch_1_fun.5.mine_ref), channel_id=1, source_target_pairs={{0,2},{1,3},{2,0},{3,1},{4,6},{5,7},{6,4},{7,5},{8,10},{9,11},{10,... | collective-permute-start | bytes 49160 | tf_op jit(solution)/shard_map/cond/branch_1_fun/ppermute | solution.py:422

commit v7 on v6

--- a/solution.py
+++ b/solution.py
@@ -32,16 +32,28 @@
     return ((row_block * cells + cell) * 4 + component) * EDGE
 
 
-def pack_sides(gas_hbm, melt_hbm, mate_ref, cross_ref, gas_ref, ends_ref, sems):
-    _, cells, rows, span = gas_ref.shape
+def pack_sides(
+    gas_hbm, melt_hbm, mate_ref, cross_ref, velocity_ref, heat_ref, ends_ref, sems
+):
+    cells, rows, span = heat_ref.shape
     components, _, depth, width = melt_hbm.shape
-    copies = [pltpu.make_async_copy(gas_hbm, gas_ref, sems.at[0])]
+    copies = [pltpu.make_async_copy(gas_hbm.at[3], heat_ref, sems.at[2])]
+    for component in range(3):
+        place = pl.ds(component * cells, cells)
+        copies.append(
+            pltpu.make_async_copy(
+                gas_hbm.at[component], velocity_ref.at[place], sems.at[3 + component]
+            )
+        )
     for end, start in enumerate((0, depth - SUB)):
         levels = melt_hbm.at[:, :, pl.ds(start, SUB), :]
-        copies.append(pltpu.make_async_copy(levels, ends_ref.at[end], sems.at[end + 1]))
+        copies.append(pltpu.make_async_copy(levels, ends_ref.at[end], sems.at[end]))
     for copy in copies:
         copy.start()
-    copies[0].wait()
+    for copy in copies[:4]:
+        copy.wait()
+    lower = lax.axis_index("gx") % 2 == 1
+    velocity_ref[3 * cells] = jnp.where(lower, heat_ref[cells - 1], heat_ref[0])
     lane = lax.broadcasted_iota(jnp.int32, (SUB, LANES), 1)
     tile = jnp.zeros((SUB, LANES), jnp.float32)
     for block in range(rows // SUB):
@@ -49,8 +61,9 @@
             for component in range(4):
                 at = slot(block, cell, component, cells)
                 here = pl.ds(SUB * block, SUB)
-                first = gas_ref[component, cell, here, 0:LANES]
-                last = gas_ref[component, cell, here, span - LANES : span]
+                source = velocity_ref.at[component * cells + cell] if component < 3 else heat_ref.at[cell]
+                first = source[here, 0:LANES]
+                last = source[here, span - LANES : span]
                 tile = jnp.where((lane >= at) & (lane < at + 2), shift_lanes(first, at), tile)
                 tile = jnp.where(
                     (lane >= at + 2) & (lane < at + 4), shift_lanes(last, at + 4), tile
@@ -58,7 +71,7 @@
     mate_ref[0:SUB, :] = tile
     cross_ref[0:SUB, :] = tile
     even = lax.axis_index("sa") % 2 == 0
-    for copy in copies[1:]:
+    for copy in copies[4:]:
         copy.wait()
     for component in range(components):
         for cell in range(cells):
@@ -74,16 +87,20 @@
 
 def pack_melt(first, melt_ref, *refs):
     out_ref = refs[-1]
-    last = melt_ref.shape[1] - 1
+    components, cells, depth, _ = melt_ref.shape
     lower = lax.axis_index("gx") % 2 == first
+
+    def put(cell):
+        for component in range(components):
+            out_ref[component * depth : (component + 1) * depth, :] = melt_ref[component, cell]
 
     @pl.when(lower)
     def _():
-        out_ref[...] = melt_ref[:, last]
+        put(cells - 1)
 
     @pl.when(jnp.logical_not(lower))
     def _():
-        out_ref[...] = melt_ref[:, 0]
+        put(0)
 
 
 def binomial(source):
@@ -94,17 +111,18 @@
     own_ref,
     cross_ref,
     mate_ref,
+    heat_ref,
     halo_ref,
     halo_mate_ref,
     halo_cross_ref,
     base_ref,
     eddy_ref,
+    strength,
     sums_ref,
     field,
     coarse,
-    strength,
 ):
-    _, cells, rows, span = own_ref.shape
+    cells, rows, span = heat_ref.shape
     wide = span + LANES
     lane = lax.broadcasted_iota(jnp.int32, (SUB, LANES), 1)
     even = lax.axis_index("gx") % 2 == 0
@@ -121,14 +139,18 @@
         else:
             columns, cell = halo_right, index - cells - 2
             sources = mate_ref, cross_ref
-        for component in range(4 if 1 <= index <= cells + 2 else 3):
+        for component in range(3):
             for block in range(rows // SUB):
                 at = slot(block, cell, component, cells)
                 place = pl.ds(SUB * (block + 1), SUB)
                 here = slice(SUB * block, SUB * (block + 1))
-                field[index, component, place, 0:span] = jnp.where(
-                    even, sources[0][component, cell, here, :], sources[1][component, cell, here, :]
-                )
+                parts = [
+                    ref[component, cell, here, :]
+                    if ref is mate_ref
+                    else ref[component * cells + cell, here, :]
+                    for ref in sources
+                ]
+                field[index, component, place, 0:span] = jnp.where(even, parts[0], parts[1])
                 field[index, component, place, span:wide] = jnp.where(
                     lane < LANES // 2,
                     shift_lanes(columns, -at),
@@ -195,12 +217,10 @@
             stressed.append([magnitude * part for part in parts])
             if 2 <= index < cells + 2:
                 cell = index - 2
-                points = points + [around(field, index, 3, block)]
-                gradient = gradient + [[points[3][1 + j][1] - points[3][1 + j][0] for j in range(3)]]
                 speed = [0.5 * points[j][0][:, :span] for j in range(3)]
                 own_magnitude = magnitude[:, :span]
                 strength[cell, out_rows, :] = own_magnitude
-                for c in range(4):
+                for c in range(3):
                     middle, along, across, upward = points[c]
                     laplace = (
                         (along[0] + along[1]) + (across[0] + across[1]) + (upward[0] + upward[1])
@@ -210,10 +230,8 @@
                         + speed[1] * gradient[c][1][:, :span]
                         + speed[2] * gradient[c][2][:, :span]
                     )
-                    molecular = gas_viscosity if c < 3 else gas_diffusivity
-                    base_ref[c, cell, out_rows, :] = molecular * laplace - advection
-                    eddy = own_magnitude * laplace
-                    eddy_ref[c, cell, out_rows, :] = eddy if c < 3 else eddy * (1.0 / turbulent_prandtl)
+                    base_ref[c, cell, out_rows, :] = gas_viscosity * laplace - advection
+                    eddy_ref[c, cell, out_rows, :] = own_magnitude * laplace
         filtered = []
         for k, (i, j) in enumerate(PAIRS):
             pair = [stressed[x][k] + stressed[x + 1][k] for x in range(cells + 1)]
@@ -255,8 +273,8 @@
     for cell in range(cells):
         planes = (
             strength[cell, 0:1, :],
-            own_ref[0, cell, 0:1, :],
-            own_ref[3, cell, 0:1, :],
+            own_ref[cell, 0:1, :],
+            heat_ref[cell, 0:1, :],
         )
         for p, plane in enumerate(planes):
             for t in range(tiles):
@@ -277,18 +295,61 @@
     out_ref[held : 2 * held - SUB, :] = theirs_ref[SUB:held, :]
 
 
-def finish_gas(span_cells, mine_ref, theirs_ref, base_ref, eddy_ref, out_ref):
-    _, cells, rows, _ = base_ref.shape
+def finish_gas(
+    span_cells,
+    mine_ref,
+    theirs_ref,
+    base_ref,
+    eddy_ref,
+    strength_ref,
+    own_ref,
+    heat_ref,
+    halo_ref,
+    rate_ref,
+    inside_ref,
+    share_ref,
+):
+    _, cells, rows, span = base_ref.shape
     coefficient = lilly(mine_ref[0:SUB, :] + theirs_ref[0:SUB, :], cells, span_cells)
+    row = lax.broadcasted_iota(jnp.int32, (SUB, span), 0)
+    lane = lax.broadcasted_iota(jnp.int32, (SUB, span), 1)
     for cell in range(cells):
         for block in range(rows // SUB):
             at = block * 2 * cells + cell
             factor = coefficient[:, at : at + 1]
             here = slice(SUB * block, SUB * (block + 1))
-            for component in range(4):
-                out_ref[component, cell, here, :] = (
+            for component in range(3):
+                rate_ref[component, cell, here, :] = (
                     base_ref[component, cell, here, :] + factor * eddy_ref[component, cell, here, :]
                 )
+            middle = heat_ref[cell, here, :]
+            at = slot(block, cell, 3, cells)
+            behind = jnp.where(lane == 0, halo_ref[:, at + 3 : at + 4], shift_lanes(middle, 1))
+            ahead = jnp.where(lane == span - 1, halo_ref[:, at : at + 1], shift_lanes(middle, -1))
+            below = (
+                jnp.where(row == 0, -middle, pltpu.roll(middle, 1, 0))
+                if block == 0
+                else heat_ref[cell, SUB * block - 1 : SUB * (block + 1) - 1, :]
+            )
+            above = (
+                jnp.where(row == SUB - 1, middle, pltpu.roll(middle, SUB - 1, 0))
+                if block == rows // SUB - 1
+                else heat_ref[cell, SUB * block + 1 : SUB * (block + 1) + 1, :]
+            )
+            speed = [0.5 * own_ref[j * cells + cell, here, :] for j in range(3)]
+            diffusivity = gas_diffusivity + factor * strength_ref[cell, here, :] * (
+                1.0 / turbulent_prandtl
+            )
+            laplace = (behind + ahead) + (below + above) - 6.0 * middle
+            advection = speed[1] * (ahead - behind) + speed[2] * (above - below)
+            for near, sign in ((cell - 1, -1.0), (cell + 1, 1.0)):
+                if 0 <= near < cells:
+                    value = heat_ref[near, here, :]
+                    laplace = laplace + value
+                    advection = advection + sign * speed[0] * value
+                else:
+                    share_ref[0 if near < 0 else 1, here, :] = diffusivity - sign * speed[0]
+            inside_ref[cell, here, :] = diffusivity * laplace - advection
 
 
 def wall_fluxes(span_cells, devices, span, mine_ref, theirs_ref, wall_ref):
@@ -323,56 +384,90 @@
 
 
 def finish(
-    rate_ref,
     flux_ref,
     inside_ref,
     beside_mate_ref,
     beside_cross_ref,
     level_ref,
+    rate_ref,
+    heat_ref,
+    share_ref,
+    gas_mate_ref,
+    gas_cross_ref,
     gas_hbm,
-    out_hbm,
-    out_ref,
-    gas_sem,
+    melt_hbm,
+    heat_out,
+    melt_out,
     sems,
 ):
     components, cells, depth, width = inside_ref.shape
+    _, rows, span = heat_ref.shape
     position = lax.axis_index("sa")
     even = lax.axis_index("gx") % 2 == 0
     level_id = lax.broadcasted_iota(jnp.int32, (SUB, width), 0)
-    copies = [pltpu.make_async_copy(rate_ref, gas_hbm, gas_sem)]
+    copies = [pltpu.make_async_copy(rate_ref, gas_hbm.at[pl.ds(0, 3)], sems.at[0])]
     copies[0].start()
+
+    def beside(cell, here):
+        from_mate = beside_mate_ref[here, :]
+        return jnp.where(even == (cell == 0), beside_cross_ref[here, :], from_mate)
+
     for cell in range(cells):
-        levels = level_ref[cell : cell + 1, :]
         for component in range(components):
             share = melt_viscosity if component == 0 else melt_diffusivity
             for block in range(depth // SUB):
                 here = slice(SUB * block, SUB * (block + 1))
                 rate = inside_ref[component, cell, here, :]
                 if cell in (0, cells - 1):
-                    from_mate = beside_mate_ref[component, here, :]
-                    from_cross = beside_cross_ref[component, here, :]
-                    outer = jnp.where(even == (cell == 0), from_cross, from_mate)
-                    rate = rate + share * outer
+                    start = component * depth + SUB * block
+                    rate = rate + share * beside(cell, slice(start, start + SUB))
                 if block == 0:
                     flux = flux_ref[component * cells + cell : component * cells + cell + 1, :]
                     rate = rate + jnp.where(level_id == 0, flux, 0.0)
                 if component == 0:
                     index = position * depth + SUB * block + level_id
-                    rate = jnp.where(index >= levels, 0.0, rate)
-                out_ref[component, cell, here, :] = rate
-            copy = pltpu.make_async_copy(
-                out_ref.at[component, cell], out_hbm.at[component, cell], sems.at[component, cell]
+                    rate = jnp.where(index >= level_ref[cell : cell + 1, :], 0.0, rate)
+                melt_out[component, cell, here, :] = rate
+            copies.append(
+                pltpu.make_async_copy(
+                    melt_out.at[component, cell],
+                    melt_hbm.at[component, cell],
+                    sems.at[2 + component * cells + cell],
+                )
             )
-            copy.start()
-            copies = copies + [copy]
+            copies[-1].start()
+    for cell in range(cells):
+        for block in range(rows // SUB):
+            here = slice(SUB * block, SUB * (block + 1))
+            rate = heat_ref[cell, here, :]
+            if cell in (0, cells - 1):
+                share = share_ref[0 if cell == 0 else 1, here, :]
+                from_cross = gas_cross_ref[gas_cross_ref.shape[0] - 1, here, :]
+                from_mate = gas_mate_ref[3, cells - 1 if cell == 0 else 0, here, :]
+                rate = rate + share * jnp.where(even == (cell == 0), from_cross, from_mate)
+            heat_out[cell, here, :] = rate
+    copies.append(pltpu.make_async_copy(heat_out, gas_hbm.at[3], sems.at[1]))
+    copies[-1].start()
     for copy in copies:
         copy.wait()
 
 
-def melt_inside(devices, melt_ref, mate_ref, cross_ref, mask_ref, level_ref, after_ref, part_ref, inside_ref, levels_ref):
+def melt_inside(
+    devices,
+    melt_ref,
+    heat_ref,
+    mate_ref,
+    cross_ref,
+    mask_ref,
+    level_ref,
+    after_ref,
+    part_ref,
+    inside_ref,
+    levels_ref,
+):
     components, cells, depth, width = melt_ref.shape
     assert cells > 1
-    pack_melt(0, melt_ref, part_ref)
+    pack_melt(0, melt_ref, heat_ref, part_ref)
     levels_ref[...] = level_ref[...]
     position = lax.axis_index("sa")
     even = position % 2 == 0
@@ -482,61 +577,65 @@
     assert devices & (devices - 1) == 0 and devices > 1
     span_cells = float(span * devices)
     even = lax.axis_index("sa") % 2 == 0
-    gas_mate = swap(gas, "gx", 1)
     side = array(SUB + components * cells * width // LANES, LANES)
-    mate, cross, gas_here = call(
+    mate, cross, velocity, heat = call(
         pack_sides,
-        (side, side, array(*gas.shape)),
+        (side, side, array(3 * cells + 1, rows, span), array(cells, rows, span)),
         [HBM, HBM],
         scratch=(
             pltpu.VMEM((2, components, cells, SUB, width), jnp.float32),
-            pltpu.SemaphoreType.DMA((3,)),
+            pltpu.SemaphoreType.DMA((6,)),
         ),
-    )(pltpu.with_memory_space_constraint(gas, pltpu.HBM), pltpu.with_memory_space_constraint(melt, pltpu.HBM))
-    gas_cross = swap_across(gas_here, "gx")
+    )(
+        pltpu.with_memory_space_constraint(gas, pltpu.HBM),
+        pltpu.with_memory_space_constraint(melt, pltpu.HBM),
+    )
+    gas_mate, gas_cross = swap(gas, "gx", 1), swap_across(velocity, "gx")
     mate, cross = swap(mate, "sa", 1), swap_across(cross, "sa")
     late = lax.broadcasted_iota(jnp.int32, (SUB, LANES), 1) % EDGE >= EDGE // 2
     halo = jnp.where(late == even, cross[:SUB], mate[:SUB])
     aside = devices == 4
     passed = jnp.where(late == even, mate[:SUB], cross[:SUB]) if aside else halo
     halo_mate, halo_cross = swap_aside(passed, 0, aside), swap_aside(passed, 1, aside)
-    part, whole = array(components, depth, width), array(components, cells, depth, width)
+    part = array(components * depth, width)
+    whole = array(components, cells, depth, width)
     levels = jax.ShapeDtypeStruct(melt_level.shape, jnp.int32)
     mate_part, inside, levels = call(
-        functools.partial(melt_inside, devices), (part, whole, levels), [VMEM] * 5 + [ANY]
-    )(melt, mate, cross, surface_mask, melt_level, halo_mate)
-    cross_part = call(functools.partial(pack_melt, 1), part, [VMEM, ANY, ANY])(
-        melt, gas_mate, mate_part
+        functools.partial(melt_inside, devices), (part, whole, levels), [VMEM] * 6 + [ANY]
+    )(melt, heat, mate, cross, surface_mask, melt_level, halo_mate)
+    cross_part = call(functools.partial(pack_melt, 1), part, [VMEM, VMEM, ANY, ANY])(
+        melt, heat, gas_mate, mate_part
     )
-    beside_mate = swap(mate_part, "gx", 1)
-    beside_cross = swap_across(cross_part, "gx")
-
-    def gas_part(*arrays):
+    beside_mate, beside_cross = swap(mate_part, "gx", 1), swap_across(cross_part, "gx")
+
+    def gas_part(velocity, gas_cross, gas_mate, heat, halo, halo_mate, halo_cross):
         wide = span + LANES
         message_rows = SUB + 3 * cells * (span // LANES)
-        base, eddy, message = call(
+        vector, scalar = array(3, cells, rows, span), array(cells, rows, span)
+        base, eddy, strength, message = call(
             germano,
-            (array(4, cells, rows, span), array(4, cells, rows, span), array(message_rows, LANES)),
-            [VMEM] * 6,
+            (vector, vector, scalar, array(message_rows, LANES)),
+            [VMEM] * 7,
             scratch=(
-                pltpu.VMEM((cells + 4, 4, rows + 2 * SUB, wide), jnp.float32),
+                pltpu.VMEM((cells + 4, 3, rows + 2 * SUB, wide), jnp.float32),
                 pltpu.VMEM((cells + 2, 3, rows + 2 * SUB, wide), jnp.float32),
-                pltpu.VMEM((cells, rows, span), jnp.float32),
             ),
-        )(*arrays)
+        )(velocity, gas_cross, gas_mate, heat, halo, halo_mate, halo_cross)
         mine, theirs = exchange(message, "sa")
-        rate = call(
-            functools.partial(finish_gas, span_cells), array(4, cells, rows, span), [VMEM] * 4
-        )(mine, theirs, base, eddy)
+        rates = call(
+            functools.partial(finish_gas, span_cells),
+            (vector, scalar, array(2, rows, span)),
+            [VMEM] * 8,
+        )(mine, theirs, base, eddy, strength, velocity, heat, halo)
         wall = call(
             functools.partial(wall_fluxes, span_cells, devices, span),
             array(2 * cells, width),
             [VMEM, VMEM],
         )(mine, theirs)
-        return rate, wall
-
-    gas_rate, wall = fenced(
-        gas_part, gas_here, gas_cross, gas_mate, halo, halo_mate, halo_cross
+        return *rates, wall
+
+    rate, heat_inside, share, wall = fenced(
+        gas_part, velocity, gas_cross, gas_mate, heat, halo, halo_mate, halo_cross
     )
     flux = call(surface_flux, array(2 * cells, width), [VMEM, VMEM], flops=4000000000)(
         wall, surface_mask
@@ -544,14 +643,25 @@
     return call(
         finish,
         (array(4, cells, rows, span), whole),
-        [VMEM] * 6,
+        [VMEM] * 10,
         scratch=(
+            pltpu.VMEM((cells, rows, span), jnp.float32),
             pltpu.VMEM((components, cells, depth, width), jnp.float32),
-            pltpu.SemaphoreType.DMA,
-            pltpu.SemaphoreType.DMA((components, cells)),
+            pltpu.SemaphoreType.DMA((2 + components * cells,)),
         ),
         out_specs=(HBM, HBM),
-    )(gas_rate, flux, inside, beside_mate, beside_cross, levels)
+    )(
+        flux,
+        inside,
+        beside_mate,
+        beside_cross,
+        levels,
+        rate,
+        heat_inside,
+        share,
+        gas_mate,
+        gas_cross,
+    )
 
 
 def solution(mesh):

time: 29.9 us -> 29.5 us (0.987)
  starting transfers between devices: 19.8 us -> 19.1 us
  waiting for transfers between devices: 3.38 us -> 3.68 us
    ppermute x5, starting transfers between devices: 7.71 us -> 7.3 us  [swap(): lax.ppermute(source, axis, [(i, i ^ mask) for i in range(lax.axis_size(ax...]
    ppermute x5, waiting for transfers between devices: 2.92 us -> 3.23 us  [swap(): lax.ppermute(source, axis, [(i, i ^ mask) for i in range(lax.axis_size(ax...]
  transfers between devices with their start and end apart: 10 -> 10, of which waited for: 3 -> 4; matrix products, arithmetic and copies ran while one was open for 0% -> 0% of each run, Pallas kernels for 16% -> 16%
where the time goes in v7:
time: 29.5 us; the launch traced here: 29.3 us
  starting transfers between devices  19.1 us (65%)
  Pallas kernels  5.75 us (19%)
  waiting for transfers between devices  3.68 us (12%)
  between operations  0.74 us (3%)
    ppermute x3, starting transfers between devices, swap_across(): return lax.ppermute(source, axis, pairs + [(j, i) for i, j in pairs])  7.59 us
    ppermute x5, starting transfers between devices, swap(): lax.ppermute(source, axis, [(i, i ^ mask) for i in range(lax.axis_size(ax...  7.3 us
    ppermute x2, starting transfers between devices, swap_aside(): return lax.ppermute(source, ('gx', 'sa'), pairs)  4.21 us
    ppermute x5, waiting for transfers between devices, swap(): lax.ppermute(source, axis, [(i, i ^ mask) for i in range(lax.axis_size(ax...  3.23 us
    pallas_call x1, Pallas kernels, gas_part(): call(germano, (vector, vector, scalar, array(message_rows, LANES)), [VMEM...  2.75 us
    pallas_call x1, Pallas kernels, on_device(): call(pack_sides, (side, side, array(3 * cells + 1, rows, span), array(cel...  1.17 us
    pallas_call x1, Pallas kernels, on_device(): call(finish, (array(4, cells, rows, span), whole), [VMEM] * 10, scratch=(...  0.92 us
  transfers between devices with their start and end apart: 10, of which 4 were waited for; matrix products, arithmetic and copies ran while one was open for 0% of the time, Pallas kernels for 16%

profile of v7, /device:TPU:0, one launch (start us, length us, event | category | flops | bytes accessed | tf_op | source)
XLA Modules:
  0.0 29.3 jit_solution(4062552058439067978)
XLA Ops:
  0.6 0.0 copy-start
  0.6 3.0 %collective-permute-start.5 = (f32[4,2,32,256]{3,2,1,0:T(8,128)}, f32[4,2,32,256]{3,2,1,0:T(8,128)S(1)}, u32[]{:S(2)}, u32[]{:S(2)}) collective-permute-start(f32[4,2,32,256]{3,2,1,0:T(8,128)} %gas_hbm.1), channel_id=1, source_target_pairs={{0,4},{4,0},{8,12},{12,8},{16,20},{20,16},{24,28},{28,24},{1,5},{5... | collective-permute-start | bytes 786440 | tf_op jit(solution)/shard_map/ppermute | solution.py:517
  3.7 1.2 %shard_map.59 = (f32[40,128]{1,0:T(8,128)S(1)}, f32[40,128]{1,0:T(8,128)S(1)}, f32[7,32,256]{2,1,0:T(8,128)S(1)}, f32[2,32,256]{2,1,0:T(8,128)S(1)}) custom-call(f32[4,2,32,256]{3,2,1,0:T(8,128)} %gas_hbm.1, f32[2,2,32,1024]{3,2,1,0:T(8,128)} %melt_ref.3), custom_call_target="tpu_custom_call" | custom-call | flops 1 | bytes 1 | tf_op jit(solution)/shard_map/pallas_call | solution.py:581
  4.9 0.7 %collective-permute-start.2 = (f32[40,128]{1,0:T(8,128)S(1)}, f32[40,128]{1,0:T(8,128)S(1)}, u32[]{:S(2)}, u32[]{:S(2)}) collective-permute-start(f32[40,128]{1,0:T(8,128)S(1)} %get-tuple-element.48), channel_id=1, source_target_pairs={{1,2},{3,0},{2,1},{0,3},{5,6},{7,4},{6,5},{4,7},{9,10},{11,8},{10,... | collective-permute-start | bytes 61448 | tf_op jit(solution)/shard_map/ppermute | solution.py:523
  5.6 1.0 %collective-permute-start.3 = (f32[40,128]{1,0:T(8,128)S(1)}, f32[40,128]{1,0:T(8,128)S(1)}, u32[]{:S(2)}, u32[]{:S(2)}) collective-permute-start(f32[40,128]{1,0:T(8,128)S(1)} %get-tuple-element.49), channel_id=1, source_target_pairs={{0,1},{1,0},{2,3},{3,2},{4,5},{5,4},{6,7},{7,6},{8,9},{9,8},{10,11... | collective-permute-start | bytes 61448 | tf_op jit(solution)/shard_map/ppermute | solution.py:517
  6.5 3.5 %collective-permute-start.4 = (f32[7,32,256]{2,1,0:T(8,128)S(1)}, f32[7,32,256]{2,1,0:T(8,128)S(1)}, u32[]{:S(2)}, u32[]{:S(2)}) collective-permute-start(f32[7,32,256]{2,1,0:T(8,128)S(1)} %get-tuple-element.50), channel_id=1, source_target_pairs={{4,8},{12,16},{20,24},{28,0},{8,4},{16,12},{24,20},{0,28},{5,9},{1... | collective-permute-start | bytes 688136 | tf_op jit(solution)/shard_map/ppermute | solution.py:523
  10.1 0.0 collective-permute-done.2.cross_ref
  10.1 0.0 collective-permute-done.3.mate_ref
  10.1 0.0 copy-start.2
  10.1 0.0 copy-start.1
  10.1 0.1 collective-permute-start.6
  10.2 4.1 %collective-permute-start.7 = (f32[8,128]{1,0:T(8,128)S(1)}, f32[8,128]{1,0:T(8,128)S(1)}, u32[]{:S(2)}, u32[]{:S(2)}) collective-permute-start(f32[8,128]{1,0:T(8,128)S(1)} %get-tuple-element.59), channel_id=1, source_target_pairs={{4,10},{8,6},{5,11},{9,7},{6,8},{10,4},{7,9},{11,5},{12,18},{16,14... | collective-permute-start | bytes 12296 | tf_op jit(solution)/shard_map/ppermute | solution.py:534
  14.4 0.4 %collective-permute-done.6.after_ref = f32[8,128]{1,0:T(8,128)S(1)} collective-permute-done((f32[8,128]{1,0:T(8,128)S(1)}, f32[8,128]{1,0:T(8,128)S(1)}, u32[]{:S(2)}, u32[]{:S(2)}) %collective-permute-start.6) | collective-permute-done | bytes 4128 | tf_op jit(solution)/shard_map/ppermute | solution.py:534
  14.8 0.0 copy-done
  14.8 0.0 copy-done.2
  14.8 0.5 %shard_map.61 = (f32[64,1024]{1,0:T(8,128)S(1)}, f32[2,2,32,1024]{3,2,1,0:T(8,128)S(1)}, s32[2,1024]{1,0:T(2,128)S(1)}) custom-call(f32[2,2,32,1024]{3,2,1,0:T(8,128)S(1)} %copy-done, f32[2,32,256]{2,1,0:T(8,128)S(1)} %get-tuple-element.51.heat_ref.refs_0_, f32[40,128]{1,0:T(8,128)S(1)} %collective-permute-done.3.mate_ref, ...), custom_call_target="tpu_custom_call" | custom-call | flops 1 | bytes 1 | tf_op jit(solution)/shard_map/pallas_call | solution.py:603
  15.3 0.1 collective-permute-start.8
  15.4 0.0 collective-permute-done.5.refs_1_.gas_mate_ref
  15.4 3.3 %collective-permute-start.9 = (f32[64,1024]{1,0:T(8,128)S(1)}, f32[64,1024]{1,0:T(8,128)S(1)}, u32[]{:S(2)}, u32[]{:S(2)}) collective-permute-start(f32[64,1024]{1,0:T(8,128)S(1)} %shard_map.62), channel_id=1, source_target_pairs={{4,8},{12,16},{20,24},{28,0},{8,4},{16,12},{24,20},{0,28},{5,9},{1... | collective-permute-start | bytes 786440 | tf_op jit(solution)/shard_map/ppermute | solution.py:523
  18.8 0.0 collective-permute-done.7
  18.8 0.0 collective-permute-done.4.gas_cross_ref
  18.8 9.3 %conditional.1 = (f32[3,2,32,256]{3,2,1,0:T(8,128)S(1)}, f32[2,32,256]{2,1,0:T(8,128)S(1)}, f32[2,32,256]{2,1,0:T(8,128)S(1)}, f32[4,1024]{1,0:T(4,128)S(1)}) conditional(s32[]{:T(128)} %convert_element_type.3, () %tuple.15, (pred[8,128]{1,0:T(8,128)(4,1)S(1)}, f32[8,128]{1,0:T(8,128)S(1)}, f32[8,128]{1,0:T(8,128)S(1)}, f32[7,32,256]{2,1,0:T(8,128)S(1)}, ...), branch_computations={%region_0.1_spmd, %region_1.2_spmd} | conditional | flops 1028 | bytes 344112 | solution.py:554
  18.8 2.8 %branch_1_fun.4 = (f32[3,2,32,256]{3,2,1,0:T(8,128)S(1)}, f32[3,2,32,256]{3,2,1,0:T(8,128)S(1)}, f32[2,32,256]{2,1,0:T(8,128)S(1)}, f32[20,128]{1,0:T(8,128)S(1)}) custom-call(f32[7,32,256]{2,1,0:T(8,128)S(1)} %get-tuple-element.19.own_ref, f32[7,32,256]{2,1,0:T(8,128)S(1)} %get-tuple-element.20.cross_ref, f32[4,2,32,256]{3,2,1,0:T(8,128)S(1)} %get-tuple-element.21.mate_ref, ...), custom_call_target="tpu_custom_call" | custom-call | flops 1 | bytes 1 | tf_op jit(solution)/shard_map/cond/branch_1_fun/pallas_call | solution.py:615
  21.5 0.0 collective-permute-start
  21.6 1.2 %collective-permute-done.theirs_ref = f32[20,128]{1,0:T(8,128)S(1)} collective-permute-done((f32[20,128]{1,0:T(8,128)S(1)}, f32[20,128]{1,0:T(8,128)S(1)}, u32[]{:S(2)}, u32[]{:S(2)}) %collective-permute-start) | collective-permute-done | bytes 10272 | tf_op jit(solution)/shard_map/cond/branch_1_fun/ppermute | solution.py:517
  22.7 3.2 %collective-permute-start.1 = (f32[32,128]{1,0:T(8,128)S(1)}, f32[32,128]{1,0:T(8,128)S(1)}, u32[]{:S(2)}, u32[]{:S(2)}) collective-permute-start(f32[32,128]{1,0:T(8,128)S(1)} %branch_1_fun.5.mine_ref), channel_id=1, source_target_pairs={{0,2},{1,3},{2,0},{3,1},{4,6},{5,7},{6,4},{7,5},{8,10},{9,11},{10,... | collective-permute-start | bytes 49160 | tf_op jit(solution)/shard_map/cond/branch_1_fun/ppermute | solution.py:517
  26.0 1.7 %collective-permute-done.1.theirs_ref = f32[32,128]{1,0:T(8,128)S(1)} collective-permute-done((f32[32,128]{1,0:T(8,128)S(1)}, f32[32,128]{1,0:T(8,128)S(1)}, u32[]{:S(2)}, u32[]{:S(2)}) %collective-permute-start.1) | collective-permute-done | bytes 16416 | tf_op jit(solution)/shard_map/cond/branch_1_fun/ppermute | solution.py:517
  27.7 0.2 branch_1_fun.7
  27.8 0.2 branch_1_fun.6
  28.1 0.3 %collective-permute-done.8.beside_mate_ref = f32[64,1024]{1,0:T(8,128)S(1)} collective-permute-done((f32[64,1024]{1,0:T(8,128)S(1)}, f32[64,1024]{1,0:T(8,128)S(1)}, u32[]{:S(2)}, u32[]{:S(2)}) %collective-permute-start.8) | collective-permute-done | bytes 262176 | tf_op jit(solution)/shard_map/ppermute | solution.py:517
  28.4 0.0 collective-permute-done.9.beside_cross_ref
  28.4 0.9 %shard_map.63 = (f32[4,2,32,256]{3,2,1,0:T(8,128)}, f32[2,2,32,1024]{3,2,1,0:T(8,128)}) custom-call(f32[4,1024]{1,0:T(4,128)S(1)} %shard_map.60.flux_ref, f32[2,2,32,1024]{3,2,1,0:T(8,128)S(1)} %get-tuple-element.53.inside_ref, f32[64,1024]{1,0:T(8,128)S(1)} %collective-permute-done.8.beside_mate_ref, ...), custom_call_target="tpu_custom_call" | custom-call | flops 1 | bytes 1 | tf_op jit(solution)/shard_map/pallas_call | solution.py:643
  (8 shorter events, 0.1 us)
Async XLA Ops:
  0.6 14.2 %copy-start = (f32[2,2,32,1024]{3,2,1,0:T(8,128)S(1)}, f32[2,2,32,1024]{3,2,1,0:T(8,128)}, u32[]{:S(2)}) copy-start(f32[2,2,32,1024]{3,2,1,0:T(8,128)} %melt_ref.3) | copy-start | bytes 1572868
  0.6 14.7 %collective-permute-start.5 = (f32[4,2,32,256]{3,2,1,0:T(8,128)}, f32[4,2,32,256]{3,2,1,0:T(8,128)S(1)}, u32[]{:S(2)}, u32[]{:S(2)}) collective-permute-start(f32[4,2,32,256]{3,2,1,0:T(8,128)} %gas_hbm.1), channel_id=1, source_target_pairs={{0,4},{4,0},{8,12},{12,8},{16,20},{20,16},{24,28},{28,24},{1,5},{5... | collective-permute-start | bytes 786440 | tf_op jit(solution)/shard_map/ppermute | solution.py:517
  4.9 5.2 %collective-permute-start.2 = (f32[40,128]{1,0:T(8,128)S(1)}, f32[40,128]{1,0:T(8,128)S(1)}, u32[]{:S(2)}, u32[]{:S(2)}) collective-permute-start(f32[40,128]{1,0:T(8,128)S(1)} %get-tuple-element.48), channel_id=1, source_target_pairs={{1,2},{3,0},{2,1},{0,3},{5,6},{7,4},{6,5},{4,7},{9,10},{11,8},{10,... | collective-permute-start | bytes 61448 | tf_op jit(solution)/shard_map/ppermute | solution.py:523
  5.6 4.5 %collective-permute-start.3 = (f32[40,128]{1,0:T(8,128)S(1)}, f32[40,128]{1,0:T(8,128)S(1)}, u32[]{:S(2)}, u32[]{:S(2)}) collective-permute-start(f32[40,128]{1,0:T(8,128)S(1)} %get-tuple-element.49), channel_id=1, source_target_pairs={{0,1},{1,0},{2,3},{3,2},{4,5},{5,4},{6,7},{7,6},{8,9},{9,8},{10,11... | collective-permute-start | bytes 61448 | tf_op jit(solution)/shard_map/ppermute | solution.py:517
  6.5 12.3 %collective-permute-start.4 = (f32[7,32,256]{2,1,0:T(8,128)S(1)}, f32[7,32,256]{2,1,0:T(8,128)S(1)}, u32[]{:S(2)}, u32[]{:S(2)}) collective-permute-start(f32[7,32,256]{2,1,0:T(8,128)S(1)} %get-tuple-element.50), channel_id=1, source_target_pairs={{4,8},{12,16},{20,24},{28,0},{8,4},{16,12},{24,20},{0,28},{5,9},{1... | collective-permute-start | bytes 688136 | tf_op jit(solution)/shard_map/ppermute | solution.py:523
  10.1 4.7 %copy-start.2 = (s32[2,1024]{1,0:T(2,128)S(1)}, s32[2,1024]{1,0:T(2,128)}, u32[]{:S(2)}) copy-start(s32[2,1024]{1,0:T(2,128)} %mask_ref.3) | copy-start | bytes 24580
  10.1 4.7 %copy-start.1 = (s32[2,1024]{1,0:T(2,128)S(1)}, s32[2,1024]{1,0:T(2,128)}, u32[]{:S(2)}) copy-start(s32[2,1024]{1,0:T(2,128)} %level_ref.1) | copy-start | bytes 24580
  10.1 4.7 %collective-permute-start.6 = (f32[8,128]{1,0:T(8,128)S(1)}, f32[8,128]{1,0:T(8,128)S(1)}, u32[]{:S(2)}, u32[]{:S(2)}) collective-permute-start(f32[8,128]{1,0:T(8,128)S(1)} %get-tuple-element.59), channel_id=1, source_target_pairs={{0,6},{4,2},{1,7},{5,3},{2,4},{6,0},{3,5},{7,1},{8,14},{12,10},{9,... | collective-permute-start | bytes 12296 | tf_op jit(solution)/shard_map/ppermute | solution.py:534
  10.2 8.6 %collective-permute-start.7 = (f32[8,128]{1,0:T(8,128)S(1)}, f32[8,128]{1,0:T(8,128)S(1)}, u32[]{:S(2)}, u32[]{:S(2)}) collective-permute-start(f32[8,128]{1,0:T(8,128)S(1)} %get-tuple-element.59), channel_id=1, source_target_pairs={{4,10},{8,6},{5,11},{9,7},{6,8},{10,4},{7,9},{11,5},{12,18},{16,14... | collective-permute-start | bytes 12296 | tf_op jit(solution)/shard_map/ppermute | solution.py:534
  15.3 13.1 %collective-permute-start.8 = (f32[64,1024]{1,0:T(8,128)S(1)}, f32[64,1024]{1,0:T(8,128)S(1)}, u32[]{:S(2)}, u32[]{:S(2)}) collective-permute-start(f32[64,1024]{1,0:T(8,128)S(1)} %get-tuple-element.54.refs_2_), channel_id=1, source_target_pairs={{0,4},{4,0},{8,12},{12,8},{16,20},{20,16},{24,28},{28,24},{1,5},{5... | collective-permute-start | bytes 786440 | tf_op jit(solution)/shard_map/ppermute | solution.py:517
  15.4 13.0 %collective-permute-start.9 = (f32[64,1024]{1,0:T(8,128)S(1)}, f32[64,1024]{1,0:T(8,128)S(1)}, u32[]{:S(2)}, u32[]{:S(2)}) collective-permute-start(f32[64,1024]{1,0:T(8,128)S(1)} %shard_map.62), channel_id=1, source_target_pairs={{4,8},{12,16},{20,24},{28,0},{8,4},{16,12},{24,20},{0,28},{5,9},{1... | collective-permute-start | bytes 786440 | tf_op jit(solution)/shard_map/ppermute | solution.py:523
  21.5 1.2 %collective-permute-start = (f32[20,128]{1,0:T(8,128)S(1)}, f32[20,128]{1,0:T(8,128)S(1)}, u32[]{:S(2)}, u32[]{:S(2)}) collective-permute-start(f32[20,128]{1,0:T(8,128)S(1)} %get-tuple-element.28.mine_ref), channel_id=1, source_target_pairs={{0,1},{1,0},{2,3},{3,2},{4,5},{5,4},{6,7},{7,6},{8,9},{9,8},{10,11... | collective-permute-start | bytes 30728 | tf_op jit(solution)/shard_map/cond/branch_1_fun/ppermute | solution.py:517
  22.7 4.9 %collective-permute-start.1 = (f32[32,128]{1,0:T(8,128)S(1)}, f32[32,128]{1,0:T(8,128)S(1)}, u32[]{:S(2)}, u32[]{:S(2)}) collective-permute-start(f32[32,128]{1,0:T(8,128)S(1)} %branch_1_fun.5.mine_ref), channel_id=1, source_target_pairs={{0,2},{1,3},{2,0},{3,1},{4,6},{5,7},{6,4},{7,5},{8,10},{9,11},{10,... | collective-permute-start | bytes 49160 | tf_op jit(solution)/shard_map/cond/branch_1_fun/ppermute | solution.py:517

commit v8 on v7

--- a/solution.py
+++ b/solution.py
@@ -375,6 +375,11 @@
                 )
 
 
+def finish_sums(span_cells, devices, span, mine_ref, theirs_ref, *refs):
+    wall_fluxes(span_cells, devices, span, mine_ref, theirs_ref, refs[-1])
+    finish_gas(span_cells, mine_ref, theirs_ref, *refs[:-1])
+
+
 def surface_flux(wall_ref, mask_ref, flux_ref):
     cells = mask_ref.shape[0]
     top = lax.axis_index("sa") == 0
@@ -622,17 +627,11 @@
             ),
         )(velocity, gas_cross, gas_mate, heat, halo, halo_mate, halo_cross)
         mine, theirs = exchange(message, "sa")
-        rates = call(
-            functools.partial(finish_gas, span_cells),
-            (vector, scalar, array(2, rows, span)),
+        return call(
+            functools.partial(finish_sums, span_cells, devices, span),
+            (vector, scalar, array(2, rows, span), array(2 * cells, width)),
             [VMEM] * 8,
         )(mine, theirs, base, eddy, strength, velocity, heat, halo)
-        wall = call(
-            functools.partial(wall_fluxes, span_cells, devices, span),
-            array(2 * cells, width),
-            [VMEM, VMEM],
-        )(mine, theirs)
-        return *rates, wall
 
     rate, heat_inside, share, wall = fenced(
         gas_part, velocity, gas_cross, gas_mate, heat, halo, halo_mate, halo_cross

time: 29.5 us -> 29.5 us (level)
  no operation moved by 1% of the time
where the time goes in v8:
time: 29.5 us; the launch traced here: 29.3 us
  starting transfers between devices  19.1 us (65%)
  Pallas kernels  5.61 us (19%)
  waiting for transfers between devices  3.82 us (13%)
  between operations  0.74 us (3%)
    ppermute x3, starting transfers between devices, swap_across(): return lax.ppermute(source, axis, pairs + [(j, i) for i, j in pairs])  7.59 us
    ppermute x5, starting transfers between devices, swap(): lax.ppermute(source, axis, [(i, i ^ mask) for i in range(lax.axis_size(ax...  7.3 us
    ppermute x2, starting transfers between devices, swap_aside(): return lax.ppermute(source, ('gx', 'sa'), pairs)  4.21 us
    ppermute x5, waiting for transfers between devices, swap(): lax.ppermute(source, axis, [(i, i ^ mask) for i in range(lax.axis_size(ax...  3.38 us
    pallas_call x1, Pallas kernels, gas_part(): call(germano, (vector, vector, scalar, array(message_rows, LANES)), [VMEM...  2.75 us
    pallas_call x1, Pallas kernels, on_device(): call(pack_sides, (side, side, array(3 * cells + 1, rows, span), array(cel...  1.17 us
    pallas_call x1, Pallas kernels, on_device(): call(finish, (array(4, cells, rows, span), whole), [VMEM] * 10, scratch=(...  0.92 us
  transfers between devices with their start and end apart: 10, of which 4 were waited for; matrix products, arithmetic and copies ran while one was open for 0% of the time, Pallas kernels for 16%

profile of v8, /device:TPU:0, one launch (start us, length us, event | category | flops | bytes accessed | tf_op | source)
XLA Modules:
  0.0 29.3 jit_solution(16457737245837739302)
XLA Ops:
  0.6 0.0 copy-start
  0.6 3.0 %collective-permute-start.5 = (f32[4,2,32,256]{3,2,1,0:T(8,128)}, f32[4,2,32,256]{3,2,1,0:T(8,128)S(1)}, u32[]{:S(2)}, u32[]{:S(2)}) collective-permute-start(f32[4,2,32,256]{3,2,1,0:T(8,128)} %gas_hbm.1), channel_id=1, source_target_pairs={{0,4},{4,0},{8,12},{12,8},{16,20},{20,16},{24,28},{28,24},{1,5},{5... | collective-permute-start | bytes 786440 | tf_op jit(solution)/shard_map/ppermute | solution.py:522
  3.7 1.2 %shard_map.59 = (f32[40,128]{1,0:T(8,128)S(1)}, f32[40,128]{1,0:T(8,128)S(1)}, f32[7,32,256]{2,1,0:T(8,128)S(1)}, f32[2,32,256]{2,1,0:T(8,128)S(1)}) custom-call(f32[4,2,32,256]{3,2,1,0:T(8,128)} %gas_hbm.1, f32[2,2,32,1024]{3,2,1,0:T(8,128)} %melt_ref.3), custom_call_target="tpu_custom_call" | custom-call | flops 1 | bytes 1 | tf_op jit(solution)/shard_map/pallas_call | solution.py:586
  4.9 0.7 %collective-permute-start.2 = (f32[40,128]{1,0:T(8,128)S(1)}, f32[40,128]{1,0:T(8,128)S(1)}, u32[]{:S(2)}, u32[]{:S(2)}) collective-permute-start(f32[40,128]{1,0:T(8,128)S(1)} %get-tuple-element.45), channel_id=1, source_target_pairs={{1,2},{3,0},{2,1},{0,3},{5,6},{7,4},{6,5},{4,7},{9,10},{11,8},{10,... | collective-permute-start | bytes 61448 | tf_op jit(solution)/shard_map/ppermute | solution.py:528
  5.6 1.0 %collective-permute-start.3 = (f32[40,128]{1,0:T(8,128)S(1)}, f32[40,128]{1,0:T(8,128)S(1)}, u32[]{:S(2)}, u32[]{:S(2)}) collective-permute-start(f32[40,128]{1,0:T(8,128)S(1)} %get-tuple-element.46), channel_id=1, source_target_pairs={{0,1},{1,0},{2,3},{3,2},{4,5},{5,4},{6,7},{7,6},{8,9},{9,8},{10,11... | collective-permute-start | bytes 61448 | tf_op jit(solution)/shard_map/ppermute | solution.py:522
  6.5 3.5 %collective-permute-start.4 = (f32[7,32,256]{2,1,0:T(8,128)S(1)}, f32[7,32,256]{2,1,0:T(8,128)S(1)}, u32[]{:S(2)}, u32[]{:S(2)}) collective-permute-start(f32[7,32,256]{2,1,0:T(8,128)S(1)} %get-tuple-element.47), channel_id=1, source_target_pairs={{4,8},{12,16},{20,24},{28,0},{8,4},{16,12},{24,20},{0,28},{5,9},{1... | collective-permute-start | bytes 688136 | tf_op jit(solution)/shard_map/ppermute | solution.py:528
  10.1 0.0 collective-permute-done.2.cross_ref
  10.1 0.0 collective-permute-done.3.mate_ref
  10.1 0.0 copy-start.2
  10.1 0.0 copy-start.1
  10.1 0.1 collective-permute-start.6
  10.2 4.1 %collective-permute-start.7 = (f32[8,128]{1,0:T(8,128)S(1)}, f32[8,128]{1,0:T(8,128)S(1)}, u32[]{:S(2)}, u32[]{:S(2)}) collective-permute-start(f32[8,128]{1,0:T(8,128)S(1)} %get-tuple-element.56), channel_id=1, source_target_pairs={{4,10},{8,6},{5,11},{9,7},{6,8},{10,4},{7,9},{11,5},{12,18},{16,14... | collective-permute-start | bytes 12296 | tf_op jit(solution)/shard_map/ppermute | solution.py:539
  14.4 0.4 %collective-permute-done.6.after_ref = f32[8,128]{1,0:T(8,128)S(1)} collective-permute-done((f32[8,128]{1,0:T(8,128)S(1)}, f32[8,128]{1,0:T(8,128)S(1)}, u32[]{:S(2)}, u32[]{:S(2)}) %collective-permute-start.6) | collective-permute-done | bytes 4128 | tf_op jit(solution)/shard_map/ppermute | solution.py:539
  14.8 0.0 copy-done
  14.8 0.0 copy-done.2
  14.8 0.0 copy-done.1
  14.8 0.5 %shard_map.61 = (f32[64,1024]{1,0:T(8,128)S(1)}, f32[2,2,32,1024]{3,2,1,0:T(8,128)S(1)}, s32[2,1024]{1,0:T(2,128)S(1)}) custom-call(f32[2,2,32,1024]{3,2,1,0:T(8,128)S(1)} %copy-done, f32[2,32,256]{2,1,0:T(8,128)S(1)} %get-tuple-element.48.heat_ref.refs_0_, f32[40,128]{1,0:T(8,128)S(1)} %collective-permute-done.3.mate_ref, ...), custom_call_target="tpu_custom_call" | custom-call | flops 1 | bytes 1 | tf_op jit(solution)/shard_map/pallas_call | solution.py:608
  15.3 0.1 collective-permute-start.8
  15.4 0.0 collective-permute-done.5.refs_1_.gas_mate_ref
  15.4 3.3 %collective-permute-start.9 = (f32[64,1024]{1,0:T(8,128)S(1)}, f32[64,1024]{1,0:T(8,128)S(1)}, u32[]{:S(2)}, u32[]{:S(2)}) collective-permute-start(f32[64,1024]{1,0:T(8,128)S(1)} %shard_map.62), channel_id=1, source_target_pairs={{4,8},{12,16},{20,24},{28,0},{8,4},{16,12},{24,20},{0,28},{5,9},{1... | collective-permute-start | bytes 786440 | tf_op jit(solution)/shard_map/ppermute | solution.py:528
  18.8 0.0 collective-permute-done.7
  18.8 0.0 collective-permute-done.4.gas_cross_ref
  18.8 9.1 %conditional.1 = ((f32[3,2,32,256]{3,2,1,0:T(8,128)S(1)}, f32[2,32,256]{2,1,0:T(8,128)S(1)}, f32[2,32,256]{2,1,0:T(8,128)S(1)}, f32[4,1024]{1,0:T(4,128)S(1)})) conditional(s32[]{:T(128)} %convert_element_type.3, () %tuple.14, (pred[8,128]{1,0:T(8,128)(4,1)S(1)}, f32[8,128]{1,0:T(8,128)S(1)}, f32[8,128]{1,0:T(8,128)S(1)}, ...), branch_computations={%region_0.1_spmd, %region_1.2_spmd} | conditional | flops 1027 | bytes 344120 | solution.py:559
  18.8 2.8 %branch_1_fun.3 = (f32[3,2,32,256]{3,2,1,0:T(8,128)S(1)}, f32[3,2,32,256]{3,2,1,0:T(8,128)S(1)}, f32[2,32,256]{2,1,0:T(8,128)S(1)}, f32[20,128]{1,0:T(8,128)S(1)}) custom-call(f32[7,32,256]{2,1,0:T(8,128)S(1)} %get-tuple-element.19.own_ref.refs_3_, f32[7,32,256]{2,1,0:T(8,128)S(1)} %get-tuple-element.20.cross_ref, ...), custom_call_target="tpu_custom_call" | custom-call | flops 1 | bytes 1 | tf_op jit(solution)/shard_map/cond/branch_1_fun/pallas_call | solution.py:620
  21.5 0.0 collective-permute-start
  21.6 1.2 %collective-permute-done.theirs_ref = f32[20,128]{1,0:T(8,128)S(1)} collective-permute-done((f32[20,128]{1,0:T(8,128)S(1)}, f32[20,128]{1,0:T(8,128)S(1)}, u32[]{:S(2)}, u32[]{:S(2)}) %collective-permute-start) | collective-permute-done | bytes 10272 | tf_op jit(solution)/shard_map/cond/branch_1_fun/ppermute | solution.py:522
  22.7 3.2 %collective-permute-start.1 = (f32[32,128]{1,0:T(8,128)S(1)}, f32[32,128]{1,0:T(8,128)S(1)}, u32[]{:S(2)}, u32[]{:S(2)}) collective-permute-start(f32[32,128]{1,0:T(8,128)S(1)} %branch_1_fun.4.mine_ref), channel_id=1, source_target_pairs={{0,2},{1,3},{2,0},{3,1},{4,6},{5,7},{6,4},{7,5},{8,10},{9,11},{10,... | collective-permute-start | bytes 49160 | tf_op jit(solution)/shard_map/cond/branch_1_fun/ppermute | solution.py:522
  26.0 1.7 %collective-permute-done.1.theirs_ref = f32[32,128]{1,0:T(8,128)S(1)} collective-permute-done((f32[32,128]{1,0:T(8,128)S(1)}, f32[32,128]{1,0:T(8,128)S(1)}, u32[]{:S(2)}, u32[]{:S(2)}) %collective-permute-start.1) | collective-permute-done | bytes 16416 | tf_op jit(solution)/shard_map/cond/branch_1_fun/ppermute | solution.py:522
  27.7 0.2 branch_1_fun.5
  27.9 0.5 %collective-permute-done.8.beside_mate_ref = f32[64,1024]{1,0:T(8,128)S(1)} collective-permute-done((f32[64,1024]{1,0:T(8,128)S(1)}, f32[64,1024]{1,0:T(8,128)S(1)}, u32[]{:S(2)}, u32[]{:S(2)}) %collective-permute-start.8) | collective-permute-done | bytes 262176 | tf_op jit(solution)/shard_map/ppermute | solution.py:522
  28.4 0.0 collective-permute-done.9.beside_cross_ref
  28.4 0.9 %shard_map.63 = (f32[4,2,32,256]{3,2,1,0:T(8,128)}, f32[2,2,32,1024]{3,2,1,0:T(8,128)}) custom-call(f32[4,1024]{1,0:T(4,128)S(1)} %shard_map.60.flux_ref, f32[2,2,32,1024]{3,2,1,0:T(8,128)S(1)} %get-tuple-element.50.inside_ref, f32[64,1024]{1,0:T(8,128)S(1)} %collective-permute-done.8.beside_mate_ref, ...), custom_call_target="tpu_custom_call" | custom-call | flops 1 | bytes 1 | tf_op jit(solution)/shard_map/pallas_call | solution.py:642
  (7 shorter events, 0.1 us)
Async XLA Ops:
  0.6 14.2 %copy-start = (f32[2,2,32,1024]{3,2,1,0:T(8,128)S(1)}, f32[2,2,32,1024]{3,2,1,0:T(8,128)}, u32[]{:S(2)}) copy-start(f32[2,2,32,1024]{3,2,1,0:T(8,128)} %melt_ref.3) | copy-start | bytes 1572868
  0.6 14.7 %collective-permute-start.5 = (f32[4,2,32,256]{3,2,1,0:T(8,128)}, f32[4,2,32,256]{3,2,1,0:T(8,128)S(1)}, u32[]{:S(2)}, u32[]{:S(2)}) collective-permute-start(f32[4,2,32,256]{3,2,1,0:T(8,128)} %gas_hbm.1), channel_id=1, source_target_pairs={{0,4},{4,0},{8,12},{12,8},{16,20},{20,16},{24,28},{28,24},{1,5},{5... | collective-permute-start | bytes 786440 | tf_op jit(solution)/shard_map/ppermute | solution.py:522
  4.9 5.2 %collective-permute-start.2 = (f32[40,128]{1,0:T(8,128)S(1)}, f32[40,128]{1,0:T(8,128)S(1)}, u32[]{:S(2)}, u32[]{:S(2)}) collective-permute-start(f32[40,128]{1,0:T(8,128)S(1)} %get-tuple-element.45), channel_id=1, source_target_pairs={{1,2},{3,0},{2,1},{0,3},{5,6},{7,4},{6,5},{4,7},{9,10},{11,8},{10,... | collective-permute-start | bytes 61448 | tf_op jit(solution)/shard_map/ppermute | solution.py:528
  5.6 4.5 %collective-permute-start.3 = (f32[40,128]{1,0:T(8,128)S(1)}, f32[40,128]{1,0:T(8,128)S(1)}, u32[]{:S(2)}, u32[]{:S(2)}) collective-permute-start(f32[40,128]{1,0:T(8,128)S(1)} %get-tuple-element.46), channel_id=1, source_target_pairs={{0,1},{1,0},{2,3},{3,2},{4,5},{5,4},{6,7},{7,6},{8,9},{9,8},{10,11... | collective-permute-start | bytes 61448 | tf_op jit(solution)/shard_map/ppermute | solution.py:522
  6.5 12.3 %collective-permute-start.4 = (f32[7,32,256]{2,1,0:T(8,128)S(1)}, f32[7,32,256]{2,1,0:T(8,128)S(1)}, u32[]{:S(2)}, u32[]{:S(2)}) collective-permute-start(f32[7,32,256]{2,1,0:T(8,128)S(1)} %get-tuple-element.47), channel_id=1, source_target_pairs={{4,8},{12,16},{20,24},{28,0},{8,4},{16,12},{24,20},{0,28},{5,9},{1... | collective-permute-start | bytes 688136 | tf_op jit(solution)/shard_map/ppermute | solution.py:528
  10.1 4.7 %copy-start.2 = (s32[2,1024]{1,0:T(2,128)S(1)}, s32[2,1024]{1,0:T(2,128)}, u32[]{:S(2)}) copy-start(s32[2,1024]{1,0:T(2,128)} %mask_ref.3) | copy-start | bytes 24580
  10.1 4.7 %copy-start.1 = (s32[2,1024]{1,0:T(2,128)S(1)}, s32[2,1024]{1,0:T(2,128)}, u32[]{:S(2)}) copy-start(s32[2,1024]{1,0:T(2,128)} %level_ref.1) | copy-start | bytes 24580
  10.1 4.7 %collective-permute-start.6 = (f32[8,128]{1,0:T(8,128)S(1)}, f32[8,128]{1,0:T(8,128)S(1)}, u32[]{:S(2)}, u32[]{:S(2)}) collective-permute-start(f32[8,128]{1,0:T(8,128)S(1)} %get-tuple-element.56), channel_id=1, source_target_pairs={{0,6},{4,2},{1,7},{5,3},{2,4},{6,0},{3,5},{7,1},{8,14},{12,10},{9,... | collective-permute-start | bytes 12296 | tf_op jit(solution)/shard_map/ppermute | solution.py:539
  10.2 8.6 %collective-permute-start.7 = (f32[8,128]{1,0:T(8,128)S(1)}, f32[8,128]{1,0:T(8,128)S(1)}, u32[]{:S(2)}, u32[]{:S(2)}) collective-permute-start(f32[8,128]{1,0:T(8,128)S(1)} %get-tuple-element.56), channel_id=1, source_target_pairs={{4,10},{8,6},{5,11},{9,7},{6,8},{10,4},{7,9},{11,5},{12,18},{16,14... | collective-permute-start | bytes 12296 | tf_op jit(solution)/shard_map/ppermute | solution.py:539
  15.3 13.1 %collective-permute-start.8 = (f32[64,1024]{1,0:T(8,128)S(1)}, f32[64,1024]{1,0:T(8,128)S(1)}, u32[]{:S(2)}, u32[]{:S(2)}) collective-permute-start(f32[64,1024]{1,0:T(8,128)S(1)} %get-tuple-element.51.refs_2_), channel_id=1, source_target_pairs={{0,4},{4,0},{8,12},{12,8},{16,20},{20,16},{24,28},{28,24},{1,5},{5... | collective-permute-start | bytes 786440 | tf_op jit(solution)/shard_map/ppermute | solution.py:522
  15.4 13.0 %collective-permute-start.9 = (f32[64,1024]{1,0:T(8,128)S(1)}, f32[64,1024]{1,0:T(8,128)S(1)}, u32[]{:S(2)}, u32[]{:S(2)}) collective-permute-start(f32[64,1024]{1,0:T(8,128)S(1)} %shard_map.62), channel_id=1, source_target_pairs={{4,8},{12,16},{20,24},{28,0},{8,4},{16,12},{24,20},{0,28},{5,9},{1... | collective-permute-start | bytes 786440 | tf_op jit(solution)/shard_map/ppermute | solution.py:528
  21.5 1.2 %collective-permute-start = (f32[20,128]{1,0:T(8,128)S(1)}, f32[20,128]{1,0:T(8,128)S(1)}, u32[]{:S(2)}, u32[]{:S(2)}) collective-permute-start(f32[20,128]{1,0:T(8,128)S(1)} %get-tuple-element.28.mine_ref), channel_id=1, source_target_pairs={{0,1},{1,0},{2,3},{3,2},{4,5},{5,4},{6,7},{7,6},{8,9},{9,8},{10,11... | collective-permute-start | bytes 30728 | tf_op jit(solution)/shard_map/cond/branch_1_fun/ppermute | solution.py:522
  22.7 4.9 %collective-permute-start.1 = (f32[32,128]{1,0:T(8,128)S(1)}, f32[32,128]{1,0:T(8,128)S(1)}, u32[]{:S(2)}, u32[]{:S(2)}) collective-permute-start(f32[32,128]{1,0:T(8,128)S(1)} %branch_1_fun.4.mine_ref), channel_id=1, source_target_pairs={{0,2},{1,3},{2,0},{3,1},{4,6},{5,7},{6,4},{7,5},{8,10},{9,11},{10,... | collective-permute-start | bytes 49160 | tf_op jit(solution)/shard_map/cond/branch_1_fun/ppermute | solution.py:522
